TPU v7x, 512 devices: a whole 4x4x16 slice. The times are simulated.
512 devices in a mesh: loop: 32 (over y, z_hi, x), dp: 16 (over z_lo, core).
Axes of the slice: x: 4, y: 4, z: 16 (z_hi: 2, z_lo: 8; z = z_hi * 8 + z_lo), core: 2. Of those that a mesh axis runs over, the one named last changes fastest.
Arguments:
- image_raw: bfloat16 [16, 4096, 1152], P('dp', 'loop'), may hold values from -0.19921875 to 0.19921875
- text_feat: bfloat16 [16, 4096, 1152], P('dp', 'loop'), may hold values from -6 to 6
- text_head: bfloat16 [1152, 1152], replicated, may hold values from -0.1875 to 0.1875
- image_of_pair: int32 [16, 4096], P('dp', 'loop'), may hold values from 0 to 1023, as said below
- logit_scale: float32 [], replicated, may hold values from 10 to 30
- logit_bias: float32 [], replicated, may hold values from -3 to -1
Outputs:
- d_text_feat: float32 [16, 4096, 1152], P('dp', 'loop')
- d_image: float32 [32, 1024, 1152], P('loop', 'dp')
Inputs may be any that keep to these rules, and one draw needn't show every extreme that they name: `image_of_pair`: pair row i of a replica belongs to column i // 128. Every image of a column is named by 1 to 5 pairs of that column over all replicas. Image m of a column is owned by the device of that column's loop index and dp index m // 64. The pairs of one device name images of one owner at most 20 times; in every draw some owner receives exactly 20 from every device of its column.
All inputs are finite; a program needn't handle non-finite values.
Results may differ from a plain program's by a relative error of at most 0.0057.
Values may be sent and summed in bfloat16 or wider, within the bound.
No kernel may reach another device: no remote copies, remote signals or barrier semaphores. Data moves between devices by JAX's collectives and lax.ppermute only.
A program may use at most 64 MiB of HBM per device.

v0:
```python
import jax
import jax.numpy as jnp
from jax import lax
from jax.sharding import PartitionSpec as P

LEVELS = 3


EPS = 1e-06


def from_partner(value, axis, apart):
    mask = 2**apart
    pairs = [(source, source ^ mask) for source in range(lax.axis_size(axis))]
    return lax.ppermute(value, axis, pairs)


def unit_rows(values):
    inv = lax.rsqrt(jnp.sum(values * values, axis=-1, keepdims=True) + EPS)
    return (values * inv, inv)


def pair_weights(left, right, same, scale, shift):
    logits = (
        scale
        * lax.dot_general(left, right, (((1,), (1,)), ((), ())), preferred_element_type=jnp.float32)
        + shift
    )
    sign = jnp.where(same, jnp.float32(1.0), jnp.float32(-1.0))
    return (-sign * jax.nn.sigmoid(-sign * logits)).astype(jnp.bfloat16)


def left_product(weight, block):
    return lax.dot_general(
        weight, block, (((0,), (0,)), ((), ())), preferred_element_type=jnp.float32
    )


def shards(image_raw, text_feat, text_head, image_of_pair, logit_scale, logit_bias):
    rows = image_raw.shape[1]
    width = image_raw.shape[2]
    unit_x, inv_x = unit_rows(image_raw[0].astype(jnp.float32))
    image_emb = unit_x.astype(jnp.bfloat16)
    text_pre = jnp.dot(text_feat[0], text_head, preferred_element_type=jnp.float32)
    unit_y, inv_y = unit_rows(text_pre)
    text_emb = unit_y.astype(jnp.bfloat16)
    labels = image_of_pair[0]
    group = 2**LEVELS
    position = lax.axis_index("loop") % group
    same_home = labels[:, None] == labels[None, :]
    w_home = pair_weights(image_emb, text_emb, same_home, logit_scale, logit_bias)
    img_grad = logit_scale * jnp.dot(w_home, text_emb, preferred_element_type=jnp.float32)
    txt_grad = logit_scale * left_product(w_home, image_emb)
    held = jnp.stack([image_emb, text_emb])
    for level in range(LEVELS):
        far = from_partner(held, "loop", level)
        far_x = far[0]
        far_y = far[1]
        apart = jnp.zeros((rows, far_y.shape[0]), jnp.bool_)
        w_image = pair_weights(image_emb, far_y, apart, logit_scale, logit_bias)
        img_grad = img_grad + logit_scale * jnp.dot(
            w_image, far_y, preferred_element_type=jnp.float32
        )
        w_text = pair_weights(far_x, text_emb, apart.T, logit_scale, logit_bias)
        txt_grad = txt_grad + logit_scale * left_product(w_text, far_x)
        if level + 1 < LEVELS:
            lower = position // 2**level % 2 == 0
            held = jnp.where(
                lower, jnp.concatenate([held, far], axis=1), jnp.concatenate([far, held], axis=1)
            )
    d_image_pair = (img_grad - unit_x * jnp.sum(unit_x * img_grad, axis=-1, keepdims=True)) * inv_x
    d_text_pre = (
        (txt_grad - unit_y * jnp.sum(unit_y * txt_grad, axis=-1, keepdims=True)) * inv_y
    ).astype(jnp.bfloat16)
    d_text_feat = lax.dot_general(
        d_text_pre, text_head, (((1,), (1,)), ((), ())), preferred_element_type=jnp.float32
    )
    owners = lax.axis_size("dp")
    images_dev = rows // 2
    table_ids = jnp.arange(images_dev * owners, dtype=jnp.int32)
    onehot = (table_ids[:, None] == labels[None, :]).astype(jnp.float32)
    table = jnp.dot(onehot, d_image_pair, precision=lax.Precision.HIGHEST).reshape(
        owners, images_dev, width
    )
    arrived = lax.all_to_all(table, "dp", split_axis=0, concat_axis=0, tiled=True)
    d_image = jnp.sum(arrived, axis=0)
    return (d_text_feat[None], d_image[None])


def solution(mesh):
    placed = (P("dp", "loop", None), P("dp", "loop", None), P(), P("dp", "loop"), P(), P())
    return jax.shard_map(
        shards,
        mesh=mesh,
        in_specs=placed,
        out_specs=(P("dp", "loop", None), P("loop", "dp", None)),
        check_vma=False,
    )
```

profile of v0, /device:TPU:127, one launch (start us, length us, event | category | flops | bytes accessed | tf_op | source)
XLA Modules:
  0.0 506.8 jit_solution(7064541191688605563)
XLA Ops:
  0.6 0.0 copy-start
  0.6 1.3 fusion.60
  1.9 1.1 fusion.61
  3.0 0.0 copy-start.4
  3.0 1.8 multiply_reduce_fusion.1
  4.8 0.1 fusion.120
  4.9 0.9 pad_maximum_fusion
  5.8 2.5 collective-permute-start
  8.3 13.9 %collective-permute-done = bf16[2,128,1152]{2,1,0:T(8,128)(2,1)} collective-permute-done((bf16[2,128,1152]{2,1,0:T(8,128)(2,1)}, bf16[2,128,1152]{2,1,0:T(8,128)(2,1)}, u32[]{:S(2)}, u32[]{:S(2)}) %collective-permute-start) | collective-permute-done | bytes 589856 | tf_op jit(solution)/shard_map/ppermute | solution.py:15
  22.2 2.8 maximum_select_fusion.1
  25.0 3.0 collective-permute-start.1
  28.1 26.5 %collective-permute-done.1 = bf16[2,256,1152]{2,1,0:T(8,128)(2,1)} collective-permute-done((bf16[2,256,1152]{2,1,0:T(8,128)(2,1)}, bf16[2,256,1152]{2,1,0:T(8,128)(2,1)}, u32[]{:S(2)}, u32[]{:S(2)}) %collective-permute-start.1) | collective-permute-done | bytes 1179680 | tf_op jit(solution)/shard_map/ppermute | solution.py:15
  54.6 3.9 maximum_select_fusion
  58.5 12.8 %collective-permute-start.2 = (bf16[2,512,1152]{2,1,0:T(8,128)(2,1)}, bf16[2,512,1152]{2,1,0:T(8,128)(2,1)}, u32[]{:S(2)}, u32[]{:S(2)}) collective-permute-start(bf16[2,512,1152]{2,1,0:T(8,128)(2,1)} %maximum_select_fusion), channel_id=1, source_target_pairs={{0,64},{16,80},{32,96},{48,112},{64,0},{80,16},{96,32},{112,48},{1... | collective-permute-start | bytes 7077896 | tf_op jit(solution)/shard_map/ppermute | solution.py:15
  72.6 0.1 multiply_convert_fusion.1
  72.7 0.3 fusion.47
  73.1 0.3 copy-done.2
  73.4 0.6 copy-done.5
  74.0 1.0 fusion.110
  75.1 2.7 convolution_add_fusion.1
  77.8 167.2 %collective-permute-done.2 = bf16[2,512,1152]{2,1,0:T(8,128)(2,1)} collective-permute-done((bf16[2,512,1152]{2,1,0:T(8,128)(2,1)}, bf16[2,512,1152]{2,1,0:T(8,128)(2,1)}, u32[]{:S(2)}, u32[]{:S(2)}) %collective-permute-start.2) | collective-permute-done | bytes 2359328 | tf_op jit(solution)/shard_map/ppermute | solution.py:15
  245.0 3.3 fusion.27
  248.3 3.1 fusion.55
  251.5 5.4 %fusion.58 = f32[1024,1152]{1,0:T(8,128)} fusion(f32[128,1152]{1,0:T(8,128)} %get-tuple-element.7, bf16[1,128,1152]{2,1,0:T(8,128)(2,1)S(1)} %copy-done.1, f32[128]{0:T(128)S(1)} %get-tuple-element.6, f32[128]{0:T(128)S(1)} %add_rsqrt_fusion.1, s32[128]{0:T(128)S(1)} %bitcast.91), kind=kOutput, calls=%fused_computation.76 | convolution fusion | flops 1812807680 | bytes 5604864 | tf_op jit(solution)/shard_map/dot_general | solution.py:82
  256.8 40.6 %all-to-all-start = ((f32[16,64,1152]{2,1,0:T(8,128)}), f32[16,64,1152]{2,1,0:T(8,128)}, u32[]{:S(2)}, u32[]{:S(2)}) async-start(f32[16,64,1152]{2,1,0:T(8,128)} %bitcast.88), calls=%async_computation | async-start | bytes 9437184 | tf_op jit(solution)/shard_map/all_to_all | solution.py:85
  297.5 1.9 fusion.81
  299.4 2.7 convolution_add_fusion.3
  302.1 3.6 fusion.26
  305.7 3.1 multiply_reduce_fusion
  308.9 2.8 convolution_bitcast_fusion
  311.7 191.8 %all-to-all-done = f32[16,64,1152]{2,1,0:T(8,128)} async-done(((f32[16,64,1152]{2,1,0:T(8,128)}), f32[16,64,1152]{2,1,0:T(8,128)}, u32[]{:S(2)}, u32[]{:S(2)}) %all-to-all-start) | async-done | bytes 4718624 | tf_op jit(solution)/shard_map/all_to_all | solution.py:85
  503.5 3.3 reduce_sum.49
  (12 shorter events, 0.0 us)
Async XLA Ops:
  0.6 2.4 copy-start
  3.0 2.8 copy-start.4
  5.8 16.4 %collective-permute-start = (bf16[2,128,1152]{2,1,0:T(8,128)(2,1)}, bf16[2,128,1152]{2,1,0:T(8,128)(2,1)}, u32[]{:S(2)}, u32[]{:S(2)}) collective-permute-start(bf16[2,128,1152]{2,1,0:T(8,128)(2,1)} %pad_maximum_fusion), channel_id=1, source_target_pairs={{0,16},{16,0},{32,48},{48,32},{64,80},{80,64},{96,112},{112,96},{1... | collective-permute-start | bytes 1769480 | tf_op jit(solution)/shard_map/ppermute | solution.py:15
  25.0 29.6 %collective-permute-start.1 = (bf16[2,256,1152]{2,1,0:T(8,128)(2,1)}, bf16[2,256,1152]{2,1,0:T(8,128)(2,1)}, u32[]{:S(2)}, u32[]{:S(2)}) collective-permute-start(bf16[2,256,1152]{2,1,0:T(8,128)(2,1)} %maximum_select_fusion.1), channel_id=1, source_target_pairs={{0,32},{16,48},{32,0},{48,16},{64,96},{80,112},{96,64},{112,80},{1... | collective-permute-start | bytes 3538952 | tf_op jit(solution)/shard_map/ppermute | solution.py:15
  28.1 44.7 %copy-start.1 = (bf16[1,128,1152]{2,1,0:T(8,128)(2,1)S(1)}, bf16[1,128,1152]{2,1,0:T(8,128)(2,1)}, u32[]{:S(2)}) copy-start(bf16[1,128,1152]{2,1,0:T(8,128)(2,1)} %param.6) | copy-start | bytes 884740
  28.1 44.7 %copy-start.6 = (s32[1,128]{1,0:T(1,128)S(1)}, s32[1,128]{1,0:T(1,128)}, u32[]{:S(2)}) copy-start(s32[1,128]{1,0:T(1,128)} %param.9) | copy-start | bytes 1540
  58.5 186.5 %collective-permute-start.2 = (bf16[2,512,1152]{2,1,0:T(8,128)(2,1)}, bf16[2,512,1152]{2,1,0:T(8,128)(2,1)}, u32[]{:S(2)}, u32[]{:S(2)}) collective-permute-start(bf16[2,512,1152]{2,1,0:T(8,128)(2,1)} %maximum_select_fusion), channel_id=1, source_target_pairs={{0,64},{16,80},{32,96},{48,112},{64,0},{80,16},{96,32},{112,48},{1... | collective-permute-start | bytes 7077896 | tf_op jit(solution)/shard_map/ppermute | solution.py:15
  72.7 0.7 copy-start.2
  73.4 0.6 copy-start.5
  256.8 246.7 %all-to-all-start = ((f32[16,64,1152]{2,1,0:T(8,128)}), f32[16,64,1152]{2,1,0:T(8,128)}, u32[]{:S(2)}, u32[]{:S(2)}) async-start(f32[16,64,1152]{2,1,0:T(8,128)} %bitcast.88), calls=%async_computation | async-start | bytes 9437184 | tf_op jit(solution)/shard_map/all_to_all | solution.py:85
  302.1 3.6 copy-start.3
where the time goes:
time: 508 us; the launch traced here: 507 us
  waiting for transfers between devices  399 us (79%)
  starting transfers between devices  58.9 us (12%)
  matrix products  31.9 us (6%)
  other arithmetic  13.5 us (3%)
    ppermute x3, waiting for transfers between devices, from_partner(): return lax.ppermute(value, axis, pairs)  208 us
    all_to_all x1, waiting for transfers between devices, shards(): lax.all_to_all(table, 'dp', split_axis=0, concat_axis=0, tiled=True)  192 us
    all_to_all x1, starting transfers between devices, shards(): lax.all_to_all(table, 'dp', split_axis=0, concat_axis=0, tiled=True)  40.6 us
    ppermute x3, starting transfers between devices, from_partner(): return lax.ppermute(value, axis, pairs)  18.3 us
    dot_general x4, matrix products, left_product(): lax.dot_general(weight, block, (((0,), (0,)), ((), ())), preferred_elemen...  11.4 us
  transfers between devices with their start and end apart: 4, of which 4 were waited for; matrix products, arithmetic and copies ran while one was open for 4% of the time, Pallas kernels for 0%

commit v1 on v0

v1 whole, which is shorter than its diff:
```python
import functools

import jax
import jax.numpy as jnp
from jax import lax
from jax.experimental import pallas as pl
from jax.experimental.pallas import tpu as pltpu
from jax.sharding import PartitionSpec as P

EPS = 1e-06
IMG_DEV = 64
SLOTS = 20
MSG = 24
RING = 4
F32 = jnp.float32
BF16 = jnp.bfloat16


def call(kernel, outs, flops=0, bytes_accessed=0):
    return pl.pallas_call(
        kernel,
        out_shape=outs,
        compiler_params=pltpu.CompilerParams(vmem_limit_bytes=48 * 2**20),
        cost_estimate=pl.CostEstimate(flops=flops, bytes_accessed=bytes_accessed, transcendentals=0),
    )


def inv_norm(values):
    return lax.rsqrt(jnp.sum(values * values, axis=-1, keepdims=True) + EPS)


def dot(a, b, dims):
    return lax.dot_general(a, b, ((dims[0], dims[1]), ((), ())), preferred_element_type=F32)


NT = ((1,), (1,))
NN = ((1,), (0,))
TN = ((0,), (0,))


def embed_kernel(img_ref, feat_ref, head_ref, held_ref, unit_ref, inv_ref):
    x = img_ref[...].astype(F32)
    held_ref[0] = (x * inv_norm(x)).astype(BF16)
    pre = dot(feat_ref[...], head_ref[...], NN)
    inv = inv_norm(pre)
    unit = pre * inv
    held_ref[1] = unit.astype(BF16)
    unit_ref[...] = unit
    inv_ref[...] = inv


def text_kernel(feat_ref, head_ref, emb_ref):
    pre = dot(feat_ref[...], head_ref[...], NN)
    emb_ref[...] = (pre * inv_norm(pre)).astype(BF16)


def apart_weights(own, others, scale, shift):
    logits = scale * dot(own, others, NT) + shift
    return (1.0 / (1.0 + jnp.exp(-logits))).astype(BF16)


def near_kernel(
    scale_ref, shift_ref, lab_ref, labt_ref, held_ref, a_ref, b_ref, c_ref, img_ref, txt_ref
):
    scale, shift = scale_ref[0], shift_ref[0]
    x, y = held_ref[0], held_ref[1]
    same = labt_ref[...] == lab_ref[...]
    sign = jnp.where(same, F32(1.0), F32(-1.0))
    logits = scale * dot(x, y, NT) + shift
    home = (-sign / (1.0 + jnp.exp(sign * logits))).astype(BF16)
    others_y = jnp.concatenate([a_ref[1], b_ref[1], c_ref[1]], axis=0)
    img_ref[...] = dot(home, y, NN) + dot(apart_weights(x, others_y, scale, shift), others_y, NN)
    others_x = jnp.concatenate([a_ref[0], b_ref[0], c_ref[0]], axis=0)
    txt_ref[...] = dot(home, x, TN) + dot(apart_weights(y, others_x, scale, shift), others_x, NN)


def far_image_kernel(
    scale_ref, shift_ref, raw_ref, held_ref, part_ref, a_ref, b_ref, c_ref, d_ref, pick_ref, tag_ref, out_ref
):
    scale, shift = scale_ref[0], shift_ref[0]
    others = jnp.concatenate([a_ref[...], b_ref[...], c_ref[...], d_ref[...]], axis=0)
    weight = apart_weights(held_ref[0], others, scale, shift)
    grad = scale * (part_ref[...] + dot(weight, others, NN))
    x = raw_ref[...].astype(F32)
    inv = inv_norm(x)
    unit = x * inv
    pair = (grad - unit * jnp.sum(unit * grad, axis=-1, keepdims=True)) * inv
    rows = jnp.concatenate([pair.astype(BF16), tag_ref[...]], axis=0)
    sent = dot(pick_ref[...], rows, NN)
    for owner in range(out_ref.shape[0]):
        out_ref[owner] = sent[owner * MSG : (owner + 1) * MSG].astype(BF16)


def far_text_kernel(
    scale_ref, shift_ref, unit_ref, inv_ref, held_ref, part_ref, a_ref, b_ref, c_ref, d_ref, head_ref, out_ref
):
    scale, shift = scale_ref[0], shift_ref[0]
    others = jnp.concatenate([a_ref[...], b_ref[...], c_ref[...], d_ref[...]], axis=0)
    weight = apart_weights(held_ref[1], others, scale, shift)
    grad = scale * (part_ref[...] + dot(weight, others, NN))
    unit = unit_ref[...]
    pre = (grad - unit * jnp.sum(unit * grad, axis=-1, keepdims=True)) * inv_ref[...]
    out_ref[...] = dot(pre.astype(BF16), head_ref[...], NT)


def sum_kernel(arrived_ref, out_ref):
    image = lax.broadcasted_iota(jnp.int32, (IMG_DEV, MSG), 0).astype(F32) + 1.0
    total = jnp.zeros(out_ref.shape, F32)
    for sender in range(arrived_ref.shape[0]):
        rows = arrived_ref[sender]
        tags = rows.astype(F32)[SLOTS : SLOTS + 1, :MSG]
        total = total + dot((image == tags).astype(BF16), rows, NN)
    out_ref[...] = total


def routing(labels, owners, width):
    count = labels.shape[0]
    owner = labels // IMG_DEV
    index = jnp.arange(count)
    rank = jnp.sum(
        ((owner[:, None] == owner[None, :]) & (index[None, :] < index[:, None])).astype(jnp.int32), axis=1
    )
    slot = owner * MSG + rank
    row = jnp.arange(owners * MSG)
    pick = row[:, None] == slot[None, :]
    mark = row[:, None] == (index * MSG + SLOTS)[None, :]
    picks = jnp.concatenate([pick, mark], axis=1).astype(BF16)
    mine = (index[:, None] == owner[None, :]).astype(BF16)
    values = jnp.where(
        rank[:, None] == jnp.arange(width)[None, :], (labels % IMG_DEV + 1)[:, None], 0
    ).astype(BF16)
    tags = jnp.dot(mine, values, preferred_element_type=F32).astype(BF16)
    return picks, tags


def shards(image_raw, text_feat, text_head, image_of_pair, logit_scale, logit_bias):
    rows, width = image_raw.shape[1:]
    owners = lax.axis_size("dp")
    loops = lax.axis_size("loop")
    image, feat, labels = image_raw[0], text_feat[0], image_of_pair[0]
    scale, shift = logit_scale[None], logit_bias[None]
    across = [(i, i ^ RING) for i in range(loops)]
    turns = [
        [(i, i & ~(RING - 1) | (i + 1) % RING) for i in range(loops)],
        [(i, i & ~(RING - 1) | (i - 1) % RING) for i in range(loops)],
        [(i, i ^ 2) for i in range(loops)],
    ]

    def ring(value):
        return [lax.ppermute(value, "loop", turn) for turn in turns]

    block = jax.ShapeDtypeStruct((rows, width), BF16)
    wide = jax.ShapeDtypeStruct((rows, width), F32)
    smem = pl.BlockSpec(memory_space=pltpu.SMEM)

    far_feat = lax.ppermute(feat, "loop", across)
    held, unit_y, inv_y = call(
        embed_kernel,
        (
            jax.ShapeDtypeStruct((2, rows, width), BF16),
            wide,
            jax.ShapeDtypeStruct((rows, 1), F32),
        ),
    )(image, feat, text_head)
    near = ring(held)
    image_emb = held[0]
    image_emb, far_feat = lax.optimization_barrier((image_emb, far_feat))
    far_x = lax.ppermute(image_emb, "loop", across)
    far_y = call(text_kernel, block)(far_feat, text_head)
    far_ys = [far_y, *ring(far_y)]
    scalars = functools.partial(with_scalars, scale, shift)
    part_img, part_txt = scalars(near_kernel, (wide, wide), labels[None, :], labels[:, None], held, *near)
    picks, tags = routing(labels, owners, width)
    sent = scalars(
        far_image_kernel,
        jax.ShapeDtypeStruct((owners, MSG, width), BF16),
        image, held, part_img, *far_ys, picks, tags,
    )
    arrived = lax.all_to_all(sent, "dp", split_axis=0, concat_axis=0, tiled=True)
    far_xs = [far_x, *ring(far_x)]
    d_text_feat = scalars(far_text_kernel, wide, unit_y, inv_y, held, part_txt, *far_xs, text_head)
    d_image = call(sum_kernel, jax.ShapeDtypeStruct((IMG_DEV, width), F32))(arrived)
    return (d_text_feat[None], d_image[None])


def with_scalars(scale, shift, kernel, outs, *operands):
    smem = pl.BlockSpec(memory_space=pltpu.SMEM)
    vmem = pl.BlockSpec(memory_space=pltpu.VMEM)
    return pl.pallas_call(
        kernel,
        out_shape=outs,
        in_specs=[smem, smem] + [vmem] * len(operands),
        compiler_params=pltpu.CompilerParams(vmem_limit_bytes=48 * 2**20),
    )(scale, shift, *operands)


def solution(mesh):
    placed = (P("dp", "loop", None), P("dp", "loop", None), P(), P("dp", "loop"), P(), P())
    return jax.shard_map(
        shards,
        mesh=mesh,
        in_specs=placed,
        out_specs=(P("dp", "loop", None), P("loop", "dp", None)),
        check_vma=False,
    )
```

time: 508 us -> 186 us (0.37)
  the two profiles are of different devices: /device:TPU:127 before, /device:TPU:138 now
where the time goes in v1:
time: 186 us; the launch traced here: 185 us
  waiting for transfers between devices  95.7 us (51%)
  starting transfers between devices  63.5 us (34%)
  Pallas kernels  12.2 us (7%)
  local copies, waits for them, and re-layouts  10 us (5%)
  between operations  2.2 us (1%)
    ppermute x1, waiting for transfers between devices, shards(): far_x = lax.ppermute(image_emb, 'loop', across)  60.2 us
    ppermute x9, starting transfers between devices, ring(): return [lax.ppermute(value, 'loop', turn) for turn in turns]  29.8 us
    ppermute x1, waiting for transfers between devices, shards(): far_feat = lax.ppermute(feat, 'loop', across)  18.9 us
    ppermute x9, waiting for transfers between devices, ring(): return [lax.ppermute(value, 'loop', turn) for turn in turns]  16.7 us
    all_to_all x1, starting transfers between devices, shards(): lax.all_to_all(sent, 'dp', split_axis=0, concat_axis=0, tiled=True)  13.8 us
    ppermute x1, starting transfers between devices, shards(): far_feat = lax.ppermute(feat, 'loop', across)  10.9 us
    ppermute x1, starting transfers between devices, shards(): far_x = lax.ppermute(image_emb, 'loop', across)  9.02 us
    unnamed x32, local copies, waits for them, and re-layouts  8.54 us
  transfers between devices with their start and end apart: 12, of which 6 were waited for; matrix products, arithmetic and copies ran while one was open for 1% of the time, Pallas kernels for 3%

profile of v1, /device:TPU:138, one launch (start us, length us, event | category | flops | bytes accessed | tf_op | source)
XLA Modules:
  0.0 184.9 jit_solution(14944415849182143396)
XLA Ops:
  0.6 1.7 copy-done
  2.4 1.0 copy-done.3
  3.4 1.8 shard_map.77
  5.2 0.8 copy-done.5
  6.6 3.4 %collective-permute-start = (bf16[2,128,1152]{2,1,0:T(8,128)(2,1)S(1)}, bf16[2,128,1152]{2,1,0:T(8,128)(2,1)}, u32[]{:S(2)}, u32[]{:S(2)}) collective-permute-start(bf16[2,128,1152]{2,1,0:T(8,128)(2,1)S(1)} %get-tuple-element.11.held_ref), channel_id=1, source_target_pairs={{0,16},{16,32},{32,48},{48,0},{64,80},{80,96},{96,112},{112,64},{1... | collective-permute-start | bytes 1769480 | tf_op jit(solution)/shard_map/ppermute | solution.py:150
  10.0 2.4 %collective-permute-start.1 = (bf16[2,128,1152]{2,1,0:T(8,128)(2,1)S(1)}, bf16[2,128,1152]{2,1,0:T(8,128)(2,1)}, u32[]{:S(2)}, u32[]{:S(2)}) collective-permute-start(bf16[2,128,1152]{2,1,0:T(8,128)(2,1)S(1)} %get-tuple-element.11.held_ref), channel_id=1, source_target_pairs={{0,48},{16,0},{32,16},{48,32},{64,112},{80,64},{96,80},{112,96},{1... | collective-permute-start | bytes 1769480 | tf_op jit(solution)/shard_map/ppermute | solution.py:150
  12.5 4.0 %collective-permute-start.2 = (bf16[2,128,1152]{2,1,0:T(8,128)(2,1)S(1)}, bf16[2,128,1152]{2,1,0:T(8,128)(2,1)}, u32[]{:S(2)}, u32[]{:S(2)}) collective-permute-start(bf16[2,128,1152]{2,1,0:T(8,128)(2,1)S(1)} %get-tuple-element.11.held_ref), channel_id=1, source_target_pairs={{0,32},{16,48},{32,0},{48,16},{64,96},{80,112},{96,64},{112,80},{1... | collective-permute-start | bytes 1769480 | tf_op jit(solution)/shard_map/ppermute | solution.py:150
  16.5 10.9 %collective-permute-start.3 = (bf16[128,1152]{1,0:T(8,128)(2,1)}, bf16[128,1152]{1,0:T(8,128)(2,1)S(1)}, u32[]{:S(2)}, u32[]{:S(2)}) collective-permute-start(bf16[128,1152]{1,0:T(8,128)(2,1)} %bitcast.3.feat_ref), channel_id=1, source_target_pairs={{0,64},{16,80},{32,96},{48,112},{64,0},{80,16},{96,32},{112,48},{1... | collective-permute-start | bytes 884744 | tf_op jit(solution)/shard_map/ppermute | solution.py:156
  27.5 0.7 slice_bitcast_fusion
  30.8 0.7 copy.9.labt_ref
  31.6 18.9 %collective-permute-done.3.feat_ref = bf16[128,1152]{1,0:T(8,128)(2,1)S(1)} collective-permute-done((bf16[128,1152]{1,0:T(8,128)(2,1)}, bf16[128,1152]{1,0:T(8,128)(2,1)S(1)}, u32[]{:S(2)}, u32[]{:S(2)}) %collective-permute-start.3) | collective-permute-done | bytes 294944 | tf_op jit(solution)/shard_map/ppermute | solution.py:156
  50.5 0.7 shard_map.80.a_ref
  51.2 3.0 %collective-permute-start.8 = (bf16[128,1152]{1,0:T(8,128)(2,1)S(1)}, bf16[128,1152]{1,0:T(8,128)(2,1)S(1)}, u32[]{:S(2)}, u32[]{:S(2)}) collective-permute-start(bf16[128,1152]{1,0:T(8,128)(2,1)S(1)} %shard_map.80.a_ref), channel_id=1, source_target_pairs={{0,16},{16,32},{32,48},{48,0},{64,80},{80,96},{96,112},{112,64},{1... | collective-permute-start | bytes 884744 | tf_op jit(solution)/shard_map/ppermute | solution.py:150
  54.2 2.9 %collective-permute-start.9 = (bf16[128,1152]{1,0:T(8,128)(2,1)S(1)}, bf16[128,1152]{1,0:T(8,128)(2,1)S(1)}, u32[]{:S(2)}, u32[]{:S(2)}) collective-permute-start(bf16[128,1152]{1,0:T(8,128)(2,1)S(1)} %shard_map.80.a_ref), channel_id=1, source_target_pairs={{0,48},{16,0},{32,16},{48,32},{64,112},{80,64},{96,80},{112,96},{1... | collective-permute-start | bytes 884744 | tf_op jit(solution)/shard_map/ppermute | solution.py:150
  57.1 3.4 %collective-permute-start.10 = (bf16[128,1152]{1,0:T(8,128)(2,1)S(1)}, bf16[128,1152]{1,0:T(8,128)(2,1)S(1)}, u32[]{:S(2)}, u32[]{:S(2)}) collective-permute-start(bf16[128,1152]{1,0:T(8,128)(2,1)S(1)} %shard_map.80.a_ref), channel_id=1, source_target_pairs={{0,32},{16,48},{32,0},{48,16},{64,96},{80,112},{96,64},{112,80},{1... | collective-permute-start | bytes 884744 | tf_op jit(solution)/shard_map/ppermute | solution.py:150
  60.9 3.0 %shard_map.78 = (f32[128,1152]{1,0:T(8,128)S(1)}, f32[128,1152]{1,0:T(8,128)S(1)}) custom-call(f32[1]{0:T(128)} %bitcast.32.scale_ref, f32[1]{0:T(128)} %bitcast.35.shift_ref, s32[1,128]{1,0:T(1,128)S(1)} %copy-done.12, s32[128,1]{1,0:T(8,128)S(1)} %copy-done.9, bf16[2,128,1152]{2,1,0:T(8,128)(2,1)S(1)} %get-tuple-element.11.held_ref, ...), custom_call_target="tpu_custom_call" | custom-call | tf_op jit(solution)/shard_map/pallas_call | solution.py:189
  63.9 0.8 copy-done.7
  65.1 5.6 %collective-permute-done.10.d_ref = bf16[128,1152]{1,0:T(8,128)(2,1)S(1)} collective-permute-done((bf16[128,1152]{1,0:T(8,128)(2,1)S(1)}, bf16[128,1152]{1,0:T(8,128)(2,1)S(1)}, u32[]{:S(2)}, u32[]{:S(2)}) %collective-permute-start.10) | collective-permute-done | bytes 294944 | tf_op jit(solution)/shard_map/ppermute | solution.py:150
  70.7 1.4 shard_map.81
  72.1 0.9 copy-done.2
  73.0 13.8 %all-to-all-start = ((bf16[16,24,1152]{2,1,0:T(8,128)(2,1)}), bf16[16,24,1152]{2,1,0:T(8,128)(2,1)}, u32[]{:S(2)}, u32[]{:S(2)}) async-start(bf16[16,24,1152]{2,1,0:T(8,128)(2,1)} %copy-done.2), calls=%async_computation | async-start | bytes 1769472 | tf_op jit(solution)/shard_map/all_to_all | solution.py:179
  86.8 9.0 %collective-permute-start.4 = (bf16[128,1152]{1,0:T(8,128)(2,1)}, bf16[128,1152]{1,0:T(8,128)(2,1)S(1)}, u32[]{:S(2)}, u32[]{:S(2)}) collective-permute-start(bf16[128,1152]{1,0:T(8,128)(2,1)} %slice_bitcast_fusion), channel_id=1, source_target_pairs={{0,64},{16,80},{32,96},{48,112},{64,0},{80,16},{96,32},{112,48},{1... | collective-permute-start | bytes 884744 | tf_op jit(solution)/shard_map/ppermute | solution.py:168
  95.9 60.2 %collective-permute-done.4.a_ref = bf16[128,1152]{1,0:T(8,128)(2,1)S(1)} collective-permute-done((bf16[128,1152]{1,0:T(8,128)(2,1)}, bf16[128,1152]{1,0:T(8,128)(2,1)S(1)}, u32[]{:S(2)}, u32[]{:S(2)}) %collective-permute-start.4) | collective-permute-done | bytes 294944 | tf_op jit(solution)/shard_map/ppermute | solution.py:168
  156.0 1.9 %collective-permute-start.5 = (bf16[128,1152]{1,0:T(8,128)(2,1)S(1)}, bf16[128,1152]{1,0:T(8,128)(2,1)S(1)}, u32[]{:S(2)}, u32[]{:S(2)}) collective-permute-start(bf16[128,1152]{1,0:T(8,128)(2,1)S(1)} %collective-permute-done.4.a_ref), channel_id=1, source_target_pairs={{0,16},{16,32},{32,48},{48,0},{64,80},{80,96},{96,112},{112,64},{1... | collective-permute-start | bytes 884744 | tf_op jit(solution)/shard_map/ppermute | solution.py:150
  157.9 3.9 %collective-permute-start.6 = (bf16[128,1152]{1,0:T(8,128)(2,1)S(1)}, bf16[128,1152]{1,0:T(8,128)(2,1)S(1)}, u32[]{:S(2)}, u32[]{:S(2)}) collective-permute-start(bf16[128,1152]{1,0:T(8,128)(2,1)S(1)} %collective-permute-done.4.a_ref), channel_id=1, source_target_pairs={{0,48},{16,0},{32,16},{48,32},{64,112},{80,64},{96,80},{112,96},{1... | collective-permute-start | bytes 884744 | tf_op jit(solution)/shard_map/ppermute | solution.py:150
  161.9 4.9 %collective-permute-start.7 = (bf16[128,1152]{1,0:T(8,128)(2,1)S(1)}, bf16[128,1152]{1,0:T(8,128)(2,1)S(1)}, u32[]{:S(2)}, u32[]{:S(2)}) collective-permute-start(bf16[128,1152]{1,0:T(8,128)(2,1)S(1)} %collective-permute-done.4.a_ref), channel_id=1, source_target_pairs={{0,32},{16,48},{32,0},{48,16},{64,96},{80,112},{96,64},{112,80},{1... | collective-permute-start | bytes 884744 | tf_op jit(solution)/shard_map/ppermute | solution.py:150
  166.8 3.6 %collective-permute-done.6.c_ref = bf16[128,1152]{1,0:T(8,128)(2,1)S(1)} collective-permute-done((bf16[128,1152]{1,0:T(8,128)(2,1)S(1)}, bf16[128,1152]{1,0:T(8,128)(2,1)S(1)}, u32[]{:S(2)}, u32[]{:S(2)}) %collective-permute-start.6) | collective-permute-done | bytes 294944 | tf_op jit(solution)/shard_map/ppermute | solution.py:150
  170.4 7.0 %collective-permute-done.7.d_ref = bf16[128,1152]{1,0:T(8,128)(2,1)S(1)} collective-permute-done((bf16[128,1152]{1,0:T(8,128)(2,1)S(1)}, bf16[128,1152]{1,0:T(8,128)(2,1)S(1)}, u32[]{:S(2)}, u32[]{:S(2)}) %collective-permute-start.7) | collective-permute-done | bytes 294944 | tf_op jit(solution)/shard_map/ppermute | solution.py:150
  177.4 1.1 copy-done.6
  178.5 1.1 copy-done.8
  179.6 2.7 %shard_map.79 = f32[128,1152]{1,0:T(8,128)} custom-call(f32[1]{0:T(128)} %bitcast.33.scale_ref, f32[1]{0:T(128)} %bitcast.36.shift_ref, f32[128,1152]{1,0:T(8,128)S(1)} %copy-done.6, f32[128,1]{1,0:T(8,128)S(1)} %copy-done.11, bf16[2,128,1152]{2,1,0:T(8,128)(2,1)S(1)} %get-tuple-element.11.held_ref, f32[128,1152]{1,0:T(8,128)S(1)} %copy-done.8, ...), custom_call_target="tpu_custom_call" | custom-call | tf_op jit(solution)/shard_map/pallas_call | solution.py:189
  182.2 2.6 %shard_map.82 = f32[64,1152]{1,0:T(8,128)} custom-call(bf16[16,24,1152]{2,1,0:T(8,128)(2,1)} %all-to-all-done.arrived_ref), custom_call_target="tpu_custom_call" | custom-call | tf_op jit(solution)/shard_map/pallas_call | solution.py:182
  (40 shorter events, 2.7 us)
Async XLA Ops:
  0.6 27.6 %copy-start.12 = (s32[1,128]{1,0:T(1,128)S(1)}, s32[1,128]{1,0:T(1,128)}, u32[]{:S(2)}) copy-start(s32[1,128]{1,0:T(1,128)} %lab_ref.1) | copy-start | bytes 1540
  0.6 1.8 copy-start
  2.4 1.0 copy-start.3
  3.4 47.1 %copy-start.1 = (bf16[1152,1152]{1,0:T(8,128)(2,1)S(1)}, bf16[1152,1152]{1,0:T(8,128)(2,1)}, u32[]{:S(2)}) copy-start(bf16[1152,1152]{1,0:T(8,128)(2,1)} %head_ref.5) | copy-start | bytes 7962628
  5.2 0.8 copy-start.5
  6.0 0.6 copy-start.10
  6.6 50.4 %collective-permute-start = (bf16[2,128,1152]{2,1,0:T(8,128)(2,1)S(1)}, bf16[2,128,1152]{2,1,0:T(8,128)(2,1)}, u32[]{:S(2)}, u32[]{:S(2)}) collective-permute-start(bf16[2,128,1152]{2,1,0:T(8,128)(2,1)S(1)} %get-tuple-element.11.held_ref), channel_id=1, source_target_pairs={{0,16},{16,32},{32,48},{48,0},{64,80},{80,96},{96,112},{112,64},{1... | collective-permute-start | bytes 1769480 | tf_op jit(solution)/shard_map/ppermute | solution.py:150
  10.0 50.8 %collective-permute-start.1 = (bf16[2,128,1152]{2,1,0:T(8,128)(2,1)S(1)}, bf16[2,128,1152]{2,1,0:T(8,128)(2,1)}, u32[]{:S(2)}, u32[]{:S(2)}) collective-permute-start(bf16[2,128,1152]{2,1,0:T(8,128)(2,1)S(1)} %get-tuple-element.11.held_ref), channel_id=1, source_target_pairs={{0,48},{16,0},{32,16},{48,32},{64,112},{80,64},{96,80},{112,96},{1... | collective-permute-start | bytes 1769480 | tf_op jit(solution)/shard_map/ppermute | solution.py:150
  12.5 48.4 %collective-permute-start.2 = (bf16[2,128,1152]{2,1,0:T(8,128)(2,1)S(1)}, bf16[2,128,1152]{2,1,0:T(8,128)(2,1)}, u32[]{:S(2)}, u32[]{:S(2)}) collective-permute-start(bf16[2,128,1152]{2,1,0:T(8,128)(2,1)S(1)} %get-tuple-element.11.held_ref), channel_id=1, source_target_pairs={{0,32},{16,48},{32,0},{48,16},{64,96},{80,112},{96,64},{112,80},{1... | collective-permute-start | bytes 1769480 | tf_op jit(solution)/shard_map/ppermute | solution.py:150
  16.5 33.9 %collective-permute-start.3 = (bf16[128,1152]{1,0:T(8,128)(2,1)}, bf16[128,1152]{1,0:T(8,128)(2,1)S(1)}, u32[]{:S(2)}, u32[]{:S(2)}) collective-permute-start(bf16[128,1152]{1,0:T(8,128)(2,1)} %bitcast.3.feat_ref), channel_id=1, source_target_pairs={{0,64},{16,80},{32,96},{48,112},{64,0},{80,16},{96,32},{112,48},{1... | collective-permute-start | bytes 884744 | tf_op jit(solution)/shard_map/ppermute | solution.py:156
  28.9 0.5 copy-start.14
  31.5 29.0 %copy-start.13 = (s32[128]{0:T(128)S(1)}, s32[128]{0:T(128)}, u32[]{:S(2)}) copy-start(s32[128]{0:T(128)} %get-tuple-element.16) | copy-start | bytes 1540
  31.5 29.0 %copy-start.15 = (s32[128]{0:T(128)S(1)}, s32[128]{0:T(128)}, u32[]{:S(2)}) copy-start(s32[128]{0:T(128)} %copy-done.14) | copy-start | bytes 1540
  31.5 29.3 %copy-start.9 = (s32[128,1]{1,0:T(8,128)S(1)}, s32[128,1]{1,0:T(8,128)}, u32[]{:S(2)}) copy-start(s32[128,1]{1,0:T(8,128)} %copy.9.labt_ref) | copy-start | bytes 1540
  31.6 39.1 %copy-start.4 = (bf16[1,128,1152]{2,1,0:T(8,128)(2,1)S(1)}, bf16[1,128,1152]{2,1,0:T(8,128)(2,1)}, u32[]{:S(2)}) copy-start(bf16[1,128,1152]{2,1,0:T(8,128)(2,1)} %param.6) | copy-start | bytes 884740
  51.2 13.5 %collective-permute-start.8 = (bf16[128,1152]{1,0:T(8,128)(2,1)S(1)}, bf16[128,1152]{1,0:T(8,128)(2,1)S(1)}, u32[]{:S(2)}, u32[]{:S(2)}) collective-permute-start(bf16[128,1152]{1,0:T(8,128)(2,1)S(1)} %shard_map.80.a_ref), channel_id=1, source_target_pairs={{0,16},{16,32},{32,48},{48,0},{64,80},{80,96},{96,112},{112,64},{1... | collective-permute-start | bytes 884744 | tf_op jit(solution)/shard_map/ppermute | solution.py:150
  54.2 10.9 %collective-permute-start.9 = (bf16[128,1152]{1,0:T(8,128)(2,1)S(1)}, bf16[128,1152]{1,0:T(8,128)(2,1)S(1)}, u32[]{:S(2)}, u32[]{:S(2)}) collective-permute-start(bf16[128,1152]{1,0:T(8,128)(2,1)S(1)} %shard_map.80.a_ref), channel_id=1, source_target_pairs={{0,48},{16,0},{32,16},{48,32},{64,112},{80,64},{96,80},{112,96},{1... | collective-permute-start | bytes 884744 | tf_op jit(solution)/shard_map/ppermute | solution.py:150
  57.1 13.6 %collective-permute-start.10 = (bf16[128,1152]{1,0:T(8,128)(2,1)S(1)}, bf16[128,1152]{1,0:T(8,128)(2,1)S(1)}, u32[]{:S(2)}, u32[]{:S(2)}) collective-permute-start(bf16[128,1152]{1,0:T(8,128)(2,1)S(1)} %shard_map.80.a_ref), channel_id=1, source_target_pairs={{0,32},{16,48},{32,0},{48,16},{64,96},{80,112},{96,64},{112,80},{1... | collective-permute-start | bytes 884744 | tf_op jit(solution)/shard_map/ppermute | solution.py:150
  63.9 0.8 copy-start.7
  70.7 106.7 %copy-start.11 = (f32[128,1]{1,0:T(8,128)S(1)}, f32[128,1]{1,0:T(8,128)}, u32[]{:S(2)}) copy-start(f32[128,1]{1,0:T(8,128)} %copy-done.10) | copy-start | bytes 1540
  72.1 0.9 copy-start.2
  73.0 109.2 %all-to-all-start = ((bf16[16,24,1152]{2,1,0:T(8,128)(2,1)}), bf16[16,24,1152]{2,1,0:T(8,128)(2,1)}, u32[]{:S(2)}, u32[]{:S(2)}) async-start(bf16[16,24,1152]{2,1,0:T(8,128)(2,1)} %copy-done.2), calls=%async_computation | async-start | bytes 1769472 | tf_op jit(solution)/shard_map/all_to_all | solution.py:179
  86.8 69.2 %collective-permute-start.4 = (bf16[128,1152]{1,0:T(8,128)(2,1)}, bf16[128,1152]{1,0:T(8,128)(2,1)S(1)}, u32[]{:S(2)}, u32[]{:S(2)}) collective-permute-start(bf16[128,1152]{1,0:T(8,128)(2,1)} %slice_bitcast_fusion), channel_id=1, source_target_pairs={{0,64},{16,80},{32,96},{48,112},{64,0},{80,16},{96,32},{112,48},{1... | collective-permute-start | bytes 884744 | tf_op jit(solution)/shard_map/ppermute | solution.py:168
  156.0 10.7 %collective-permute-start.5 = (bf16[128,1152]{1,0:T(8,128)(2,1)S(1)}, bf16[128,1152]{1,0:T(8,128)(2,1)S(1)}, u32[]{:S(2)}, u32[]{:S(2)}) collective-permute-start(bf16[128,1152]{1,0:T(8,128)(2,1)S(1)} %collective-permute-done.4.a_ref), channel_id=1, source_target_pairs={{0,16},{16,32},{32,48},{48,0},{64,80},{80,96},{96,112},{112,64},{1... | collective-permute-start | bytes 884744 | tf_op jit(solution)/shard_map/ppermute | solution.py:150
  157.9 12.4 %collective-permute-start.6 = (bf16[128,1152]{1,0:T(8,128)(2,1)S(1)}, bf16[128,1152]{1,0:T(8,128)(2,1)S(1)}, u32[]{:S(2)}, u32[]{:S(2)}) collective-permute-start(bf16[128,1152]{1,0:T(8,128)(2,1)S(1)} %collective-permute-done.4.a_ref), channel_id=1, source_target_pairs={{0,48},{16,0},{32,16},{48,32},{64,112},{80,64},{96,80},{112,96},{1... | collective-permute-start | bytes 884744 | tf_op jit(solution)/shard_map/ppermute | solution.py:150
  161.9 15.5 %collective-permute-start.7 = (bf16[128,1152]{1,0:T(8,128)(2,1)S(1)}, bf16[128,1152]{1,0:T(8,128)(2,1)S(1)}, u32[]{:S(2)}, u32[]{:S(2)}) collective-permute-start(bf16[128,1152]{1,0:T(8,128)(2,1)S(1)} %collective-permute-done.4.a_ref), channel_id=1, source_target_pairs={{0,32},{16,48},{32,0},{48,16},{64,96},{80,112},{96,64},{112,80},{1... | collective-permute-start | bytes 884744 | tf_op jit(solution)/shard_map/ppermute | solution.py:150
  177.4 1.1 copy-start.6
  178.5 1.1 copy-start.8

commit v2 on v1

v2 whole, which is shorter than its diff:
```python
import jax
import jax.numpy as jnp
from jax import lax
from jax.experimental import pallas as pl
from jax.experimental.pallas import tpu as pltpu
from jax.sharding import PartitionSpec as P

EPS = 1e-06
IMG_DEV = 64
RING = 4
LANES = 128
MAIN = 16
EXTRA = 4
F32 = jnp.float32
BF16 = jnp.bfloat16

NT = ((1,), (1,))
NN = ((1,), (0,))
TN = ((0,), (0,))


def call(kernel, outs, *operands, scalars=0, scratch=()):
    smem = pl.BlockSpec(memory_space=pltpu.SMEM)
    vmem = pl.BlockSpec(memory_space=pltpu.VMEM)
    return pl.pallas_call(
        kernel,
        out_shape=outs,
        in_specs=[smem] * scalars + [vmem] * (len(operands) - scalars),
        scratch_shapes=scratch,
        compiler_params=pltpu.CompilerParams(vmem_limit_bytes=48 * 2**20),
    )(*operands)


def inv_norm(values):
    return lax.rsqrt(jnp.sum(values * values, axis=-1, keepdims=True) + EPS)


def dot(a, b, dims):
    return lax.dot_general(a, b, (dims, ((), ())), preferred_element_type=F32)


def embed_kernel(img_ref, feat_ref, head_ref, x_ref, y_ref, unit_ref, inv_ref):
    x = img_ref[...].astype(F32)
    x_ref[...] = (x * inv_norm(x)).astype(BF16)
    pre = dot(feat_ref[...], head_ref[...], NN)
    inv = inv_norm(pre)
    unit = pre * inv
    y_ref[...] = unit.astype(BF16)
    unit_ref[...] = unit
    inv_ref[...] = inv


def text_kernel(feat_ref, head_ref, emb_ref):
    pre = dot(feat_ref[...], head_ref[...], NN)
    emb_ref[...] = (pre * inv_norm(pre)).astype(BF16)


def apart_weights(own, others, scale, shift):
    logits = scale * dot(own, others, NT) + shift
    return (1.0 / (1.0 + jnp.exp(-logits))).astype(BF16)


def column(row):
    size = row.shape[1]
    at = [lax.broadcasted_iota(jnp.int32, (size, size), axis) for axis in range(2)]
    return jnp.sum(jnp.where(at[0] == at[1], row, 0), axis=1, keepdims=True)


def home_weights(x, y, lab_ref, scale, shift):
    lab = lab_ref[...]
    sign = jnp.where(column(lab) == lab, F32(1.0), F32(-1.0))
    logits = scale * dot(x, y, NT) + shift
    return (-sign / (1.0 + jnp.exp(sign * logits))).astype(BF16)


def near_image_kernel(scale_ref, shift_ref, lab_ref, x_ref, y_ref, a_ref, b_ref, c_ref, out_ref):
    scale, shift = scale_ref[0], shift_ref[0]
    x, y = x_ref[...], y_ref[...]
    home = home_weights(x, y, lab_ref, scale, shift)
    others = jnp.concatenate([a_ref[...], b_ref[...], c_ref[...]], axis=0)
    out_ref[...] = dot(home, y, NN) + dot(apart_weights(x, others, scale, shift), others, NN)


def far_image_kernel(
    scale_ref, shift_ref, raw_ref, x_ref, part_ref, a_ref, b_ref, c_ref, d_ref, pick_ref, tag_ref, out_ref
):
    scale, shift = scale_ref[0], shift_ref[0]
    others = jnp.concatenate([a_ref[...], b_ref[...], c_ref[...], d_ref[...]], axis=0)
    weight = apart_weights(x_ref[...], others, scale, shift)
    grad = scale * (part_ref[...] + dot(weight, others, NN))
    x = raw_ref[...].astype(F32)
    inv = inv_norm(x)
    unit = x * inv
    pair = (grad - unit * jnp.sum(unit * grad, axis=-1, keepdims=True)) * inv
    sent = dot(pick_ref[...], pair.astype(BF16), NN)
    low = lax.broadcasted_iota(jnp.int32, (2 * EXTRA, LANES), 0) < EXTRA
    step = MAIN + 2 * EXTRA
    for owner in range(out_ref.shape[0]):
        rows = sent[owner * step : (owner + 1) * step]
        cols = [rows[:, at : at + LANES] for at in range(0, rows.shape[1], LANES)]
        ends = [col[MAIN:] for col in cols] + [tag_ref[owner]]
        pairs = [jnp.where(low, ends[at], ends[at + 1]) for at in range(0, len(ends), 2)]
        out_ref[owner] = jnp.concatenate([col[:MAIN] for col in cols] + pairs, axis=0).astype(BF16)


def text_grad_kernel(scale_ref, shift_ref, lab_ref, unit_ref, inv_ref, x_ref, y_ref, *refs):
    *other_refs, head_ref, out_ref = refs
    scale, shift = scale_ref[0], shift_ref[0]
    x, y = x_ref[...], y_ref[...]
    home = home_weights(x, y, lab_ref, scale, shift)
    others = jnp.concatenate([ref[...] for ref in other_refs], axis=0)
    weight = apart_weights(y, others, scale, shift)
    grad = scale * (dot(home, x, TN) + dot(weight, others, NN))
    unit = unit_ref[...]
    pre = (grad - unit * jnp.sum(unit * grad, axis=-1, keepdims=True)) * inv_ref[...]
    out_ref[...] = dot(pre.astype(BF16), head_ref[...], NT)


def sum_kernel(arrived_ref, out_ref, main_ref):
    senders = arrived_ref.shape[0]
    chunks = out_ref.shape[1] // LANES
    ends = []
    for sender in range(senders):
        block = arrived_ref[sender]
        for c in range(chunks):
            main_ref[sender * MAIN : (sender + 1) * MAIN, c * LANES : (c + 1) * LANES] = block[
                c * MAIN : (c + 1) * MAIN
            ]
        tail = block.astype(F32)[chunks * MAIN :]
        ends.append([tail[at : at + 2 * EXTRA] for at in range(0, tail.shape[0], 2 * EXTRA)])
    image = lax.broadcasted_iota(jnp.int32, (IMG_DEV, LANES), 0).astype(F32) + 1.0
    half = senders // 2
    first = sum(end[-1] for end in ends[:half])
    second = sum(end[-1] for end in ends[half:])
    both = first + second
    match = jnp.concatenate(
        [image == first[EXTRA : EXTRA + 1], image == second[EXTRA : EXTRA + 1]], axis=1
    ).astype(BF16)
    low = lax.broadcasted_iota(jnp.int32, (IMG_DEV, LANES), 1) % (2 * EXTRA) < EXTRA
    extra = image == both[EXTRA + 1 : EXTRA + 2]
    extras = ((extra & low).astype(BF16), (extra & ~low).astype(BF16))
    total = dot(match, main_ref[...], NN)
    for c in range(chunks):
        tail = jnp.concatenate([end[c // 2] for end in ends], axis=0).astype(BF16)
        out_ref[:, c * LANES : (c + 1) * LANES] = total[:, c * LANES : (c + 1) * LANES] + dot(
            extras[c % 2], tail, NN
        )


def routing_kernel(me_ref, lab_ref, pick_ref, tag_ref):
    me = me_ref[0]
    row = lab_ref[...]
    count = row.shape[1]
    owners = tag_ref.shape[0]
    col = column(row)
    owner_row, owner_col = row // IMG_DEV, col // IMG_DEV
    at = [lax.broadcasted_iota(jnp.int32, (count, count), axis) for axis in range(2)]
    same = owner_col == owner_row
    rank_row = jnp.sum(jnp.where(same & (at[0] < at[1]), 1, 0), axis=0, keepdims=True)
    rank_col = jnp.sum(jnp.where(same & (at[1] < at[0]), 1, 0), axis=1, keepdims=True)
    step = MAIN + 2 * EXTRA
    slot = lax.broadcasted_iota(jnp.int32, (step, count), 0)
    want = jnp.where(slot < MAIN, slot, MAIN + slot % EXTRA)
    hit = want == rank_row
    picks = [jnp.where(hit & (owner_row == owner), F32(1.0), F32(0.0)) for owner in range(owners)]
    pick_ref[...] = jnp.concatenate(picks, axis=0).astype(BF16)
    lane = at[1]
    value = (col % IMG_DEV + 1).astype(F32)
    main_at = (rank_col < MAIN) & (lane - me % (owners // 2) * MAIN == rank_col)
    extra_at = (lane // (2 * EXTRA) == me) & (MAIN + lane % EXTRA == rank_col)
    marks = jnp.concatenate([jnp.where(main_at, value, 0.0), jnp.where(extra_at, value, 0.0)], axis=1)
    mine = lax.broadcasted_iota(jnp.int32, (owners, count), 0) == owner_row
    tags = dot(jnp.where(mine, F32(1.0), F32(0.0)).astype(BF16), marks.astype(BF16), NN)
    sub = lax.broadcasted_iota(jnp.int32, (2 * EXTRA, LANES), 0)
    for owner in range(owners):
        main, extra = tags[owner : owner + 1, :LANES], tags[owner : owner + 1, LANES:]
        tag_ref[owner] = jnp.where(sub == EXTRA, main, jnp.where(sub == EXTRA + 1, extra, 0.0))


def shards(image_raw, text_feat, text_head, image_of_pair, logit_scale, logit_bias):
    rows, width = image_raw.shape[1:]
    owners = lax.axis_size("dp")
    loops = lax.axis_size("loop")
    image, feat, labels = image_raw[0], text_feat[0], image_of_pair[0]
    scalars = (logit_scale[None], logit_bias[None])
    lab = labels[None, :]
    across = [(i, i ^ RING) for i in range(loops)]
    turns = [
        [(i, i & ~(RING - 1) | (i + 1) % RING) for i in range(loops)],
        [(i, i & ~(RING - 1) | (i - 1) % RING) for i in range(loops)],
        [(i, i ^ 2) for i in range(loops)],
    ]

    def ring(value):
        return [lax.ppermute(value, "loop", turn) for turn in turns]

    block = jax.ShapeDtypeStruct((rows, width), BF16)
    wide = jax.ShapeDtypeStruct((rows, width), F32)

    step = MAIN + 2 * EXTRA
    halves = [list(range(at, at + RING)) for at in range(0, loops, RING)]
    picks, tags = call(
        routing_kernel,
        (
            jax.ShapeDtypeStruct((owners * step, rows), BF16),
            jax.ShapeDtypeStruct((owners, 2 * EXTRA, LANES), F32),
        ),
        lax.axis_index("dp")[None], lab, scalars=1,
    )
    far_feat = lax.ppermute(feat, "loop", across)
    x, y, unit_y, inv_y = call(
        embed_kernel, (block, block, wide, jax.ShapeDtypeStruct((rows, 1), F32)), image, feat, text_head
    )
    part = call(near_image_kernel, wide, *scalars, lab, x, y, *ring(y), scalars=2)
    x_out, far_feat = lax.optimization_barrier((x, far_feat))
    far_x = lax.ppermute(x_out, "loop", across)
    far_y = call(text_kernel, block, far_feat, text_head)
    far_ys = ring(far_y)
    part, far_x = lax.optimization_barrier((part, far_x))
    sent = call(
        far_image_kernel,
        jax.ShapeDtypeStruct((owners, (MAIN + EXTRA) * width // LANES + EXTRA, LANES), BF16),
        *scalars, image, x, part, far_y, *far_ys, picks, tags, scalars=2,
    )
    sent, x_near = lax.optimization_barrier((sent, x))
    arrived = lax.all_to_all(sent, "dp", split_axis=0, concat_axis=0, tiled=True)
    xs = [*ring(x_near), far_x, *ring(far_x)]
    d_text_feat = call(
        text_grad_kernel, wide, *scalars, lab, unit_y, inv_y, x, y, *xs, text_head, scalars=2
    )
    d_image = call(
        sum_kernel,
        jax.ShapeDtypeStruct((IMG_DEV, width), F32),
        arrived,
        scratch=[pltpu.VMEM((owners * MAIN, width), BF16)],
    )
    return (d_text_feat[None], d_image[None])


def solution(mesh):
    placed = (P("dp", "loop", None), P("dp", "loop", None), P(), P("dp", "loop"), P(), P())
    return jax.shard_map(
        shards,
        mesh=mesh,
        in_specs=placed,
        out_specs=(P("dp", "loop", None), P("loop", "dp", None)),
        check_vma=False,
    )
```

time: 186 us -> 128 us (0.69)
  the two profiles are of different devices: /device:TPU:138 before, /device:TPU:1 now
where the time goes in v2:
time: 128 us; the launch traced here: 127 us
  starting transfers between devices  84.7 us (66%)
  waiting for transfers between devices  17 us (13%)
  Pallas kernels  13.1 us (10%)
  local copies, waits for them, and re-layouts  9.89 us (8%)
  between operations  2.2 us (2%)
    ppermute x12, starting transfers between devices, ring(): return [lax.ppermute(value, 'loop', turn) for turn in turns]  37.2 us
    all_to_all x1, starting transfers between devices, shards(): lax.all_to_all(sent, 'dp', split_axis=0, concat_axis=0, tiled=True)  27.6 us
    ppermute x1, starting transfers between devices, shards(): far_feat = lax.ppermute(feat, 'loop', across)  16.3 us
    ppermute x12, waiting for transfers between devices, ring(): return [lax.ppermute(value, 'loop', turn) for turn in turns]  14.4 us
    pallas_call x7, Pallas kernels, call(): pl.pallas_call(kernel, out_shape=outs, in_specs=[smem] * scalars + [vmem]...  13.1 us
    unnamed x32, local copies, waits for them, and re-layouts  9.89 us
    ppermute x1, starting transfers between devices, shards(): far_x = lax.ppermute(x_out, 'loop', across)  3.65 us
    ppermute x1, waiting for transfers between devices, shards(): far_x = lax.ppermute(x_out, 'loop', across)  2.6 us
  transfers between devices with their start and end apart: 15, of which 6 were waited for; matrix products, arithmetic and copies ran while one was open for 0% of the time, Pallas kernels for 7%

profile of v2, /device:TPU:1, one launch (start us, length us, event | category | flops | bytes accessed | tf_op | source)
XLA Modules:
  0.0 126.9 jit_solution(10433429553082653125)
XLA Ops:
  0.6 16.3 %collective-permute-start.3 = (bf16[128,1152]{1,0:T(8,128)(2,1)}, bf16[128,1152]{1,0:T(8,128)(2,1)S(1)}, u32[]{:S(2)}, u32[]{:S(2)}) collective-permute-start(bf16[128,1152]{1,0:T(8,128)(2,1)} %bitcast.15), channel_id=1, source_target_pairs={{0,64},{16,80},{32,96},{48,112},{64,0},{80,16},{96,32},{112,48},{1... | collective-permute-start | bytes 884744 | tf_op jit(solution)/shard_map/ppermute | solution.py:210
  16.9 1.7 %copy-done = bf16[1152,1152]{1,0:T(8,128)(2,1)S(1)} copy-done((bf16[1152,1152]{1,0:T(8,128)(2,1)S(1)}, bf16[1152,1152]{1,0:T(8,128)(2,1)}, u32[]{:S(2)}) %copy-start) | copy-done | bytes 2654232
  18.7 1.0 copy-done.4
  19.6 1.0 copy-done.8
  20.6 1.4 %shard_map.77 = (bf16[128,1152]{1,0:T(8,128)(2,1)S(1)}, bf16[128,1152]{1,0:T(8,128)(2,1)}, f32[128,1152]{1,0:T(8,128)S(1)}, f32[128,1]{1,0:T(8,128)S(1)}) custom-call(bf16[128,1152]{1,0:T(8,128)(2,1)S(1)} %bitcast.13, bf16[128,1152]{1,0:T(8,128)(2,1)S(1)} %bitcast.16, bf16[1152,1152]{1,0:T(8,128)(2,1)S(1)} %copy-done), custom_call_target="tpu_custom_call" | custom-call | tf_op jit(solution)/shard_map/pallas_call | solution.py:25
  22.0 4.6 %collective-permute-start.2 = (bf16[128,1152]{1,0:T(8,128)(2,1)}, bf16[128,1152]{1,0:T(8,128)(2,1)S(1)}, u32[]{:S(2)}, u32[]{:S(2)}) collective-permute-start(bf16[128,1152]{1,0:T(8,128)(2,1)} %get-tuple-element.17.y_ref), channel_id=1, source_target_pairs={{0,32},{16,48},{32,0},{48,16},{64,96},{80,112},{96,64},{112,80},{1... | collective-permute-start | bytes 884744 | tf_op jit(solution)/shard_map/ppermute | solution.py:195
  26.7 2.8 %collective-permute-start.1 = (bf16[128,1152]{1,0:T(8,128)(2,1)}, bf16[128,1152]{1,0:T(8,128)(2,1)S(1)}, u32[]{:S(2)}, u32[]{:S(2)}) collective-permute-start(bf16[128,1152]{1,0:T(8,128)(2,1)} %get-tuple-element.17.y_ref), channel_id=1, source_target_pairs={{0,48},{16,0},{32,16},{48,32},{64,112},{80,64},{96,80},{112,96},{1... | collective-permute-start | bytes 884744 | tf_op jit(solution)/shard_map/ppermute | solution.py:195
  29.5 2.5 %collective-permute-start = (bf16[128,1152]{1,0:T(8,128)(2,1)}, bf16[128,1152]{1,0:T(8,128)(2,1)}, u32[]{:S(2)}, u32[]{:S(2)}) collective-permute-start(bf16[128,1152]{1,0:T(8,128)(2,1)} %get-tuple-element.17.y_ref), channel_id=1, source_target_pairs={{0,16},{16,32},{32,48},{48,0},{64,80},{80,96},{96,112},{112,64},{1... | collective-permute-start | bytes 884744 | tf_op jit(solution)/shard_map/ppermute | solution.py:195
  32.7 3.7 %collective-permute-start.4 = (bf16[128,1152]{1,0:T(8,128)(2,1)S(1)}, bf16[128,1152]{1,0:T(8,128)(2,1)}, u32[]{:S(2)}, u32[]{:S(2)}) collective-permute-start(bf16[128,1152]{1,0:T(8,128)(2,1)S(1)} %get-tuple-element.23.x_ref), channel_id=1, source_target_pairs={{0,64},{16,80},{32,96},{48,112},{64,0},{80,16},{96,32},{112,48},{1... | collective-permute-start | bytes 884744 | tf_op jit(solution)/shard_map/ppermute | solution.py:216
  36.4 4.7 %collective-permute-start.7 = (bf16[128,1152]{1,0:T(8,128)(2,1)S(1)}, bf16[128,1152]{1,0:T(8,128)(2,1)}, u32[]{:S(2)}, u32[]{:S(2)}) collective-permute-start(bf16[128,1152]{1,0:T(8,128)(2,1)S(1)} %shard_map.79.a_ref), channel_id=1, source_target_pairs={{0,32},{16,48},{32,0},{48,16},{64,96},{80,112},{96,64},{112,80},{1... | collective-permute-start | bytes 884744 | tf_op jit(solution)/shard_map/ppermute | solution.py:195
  41.8 2.8 %collective-permute-start.6 = (bf16[128,1152]{1,0:T(8,128)(2,1)S(1)}, bf16[128,1152]{1,0:T(8,128)(2,1)}, u32[]{:S(2)}, u32[]{:S(2)}) collective-permute-start(bf16[128,1152]{1,0:T(8,128)(2,1)S(1)} %shard_map.79.a_ref), channel_id=1, source_target_pairs={{0,48},{16,0},{32,16},{48,32},{64,112},{80,64},{96,80},{112,96},{1... | collective-permute-start | bytes 884744 | tf_op jit(solution)/shard_map/ppermute | solution.py:195
  45.3 2.5 %collective-permute-start.5 = (bf16[128,1152]{1,0:T(8,128)(2,1)S(1)}, bf16[128,1152]{1,0:T(8,128)(2,1)}, u32[]{:S(2)}, u32[]{:S(2)}) collective-permute-start(bf16[128,1152]{1,0:T(8,128)(2,1)S(1)} %shard_map.79.a_ref), channel_id=1, source_target_pairs={{0,16},{16,32},{32,48},{48,0},{64,80},{80,96},{96,112},{112,64},{1... | collective-permute-start | bytes 884744 | tf_op jit(solution)/shard_map/ppermute | solution.py:195
  49.5 1.0 copy-done.10
  50.5 1.0 copy-done.12
  51.4 1.9 %shard_map.78.part_ref = f32[128,1152]{1,0:T(8,128)S(1)} custom-call(f32[1]{0:T(128)} %bitcast.7.scale_ref, f32[1]{0:T(128)} %bitcast.10.shift_ref, s32[1,128]{1,0:T(1,128)S(1)} %copy-done.15, bf16[128,1152]{1,0:T(8,128)(2,1)S(1)} %get-tuple-element.23.x_ref, bf16[128,1152]{1,0:T(8,128)(2,1)} %get-tuple-element.17.y_ref, ...), custom_call_target="tpu_custom_call" | custom-call | tf_op jit(solution)/shard_map/pallas_call | solution.py:25
  53.4 2.6 %collective-permute-done.4.refs_3_ = bf16[128,1152]{1,0:T(8,128)(2,1)} collective-permute-done((bf16[128,1152]{1,0:T(8,128)(2,1)S(1)}, bf16[128,1152]{1,0:T(8,128)(2,1)}, u32[]{:S(2)}, u32[]{:S(2)}) %collective-permute-start.4) | collective-permute-done | bytes 294944 | tf_op jit(solution)/shard_map/ppermute | solution.py:216
  56.3 3.4 %shard_map.81 = bf16[16,184,128]{2,1,0:T(8,128)(2,1)} custom-call(f32[1]{0:T(128)} %bitcast.8.scale_ref, f32[1]{0:T(128)} %bitcast.11.shift_ref, bf16[128,1152]{1,0:T(8,128)(2,1)S(1)} %bitcast.14, bf16[128,1152]{1,0:T(8,128)(2,1)S(1)} %get-tuple-element.23.x_ref, f32[128,1152]{1,0:T(8,128)S(1)} %shard_map.78.part_ref, ...), custom_call_target="tpu_custom_call" | custom-call | tf_op jit(solution)/shard_map/pallas_call | solution.py:25
  59.6 27.6 %all-to-all-start = ((bf16[16,184,128]{2,1,0:T(8,128)(2,1)}), bf16[16,184,128]{2,1,0:T(8,128)(2,1)S(1)}, u32[]{:S(2)}, u32[]{:S(2)}) async-start(bf16[16,184,128]{2,1,0:T(8,128)(2,1)} %shard_map.81), calls=%async_computation | async-start | bytes 1507328 | tf_op jit(solution)/shard_map/all_to_all | solution.py:226
  87.2 2.2 %collective-permute-start.10 = (bf16[128,1152]{1,0:T(8,128)(2,1)}, bf16[128,1152]{1,0:T(8,128)(2,1)S(1)}, u32[]{:S(2)}, u32[]{:S(2)}) collective-permute-start(bf16[128,1152]{1,0:T(8,128)(2,1)} %copy-done.2), channel_id=1, source_target_pairs={{0,32},{16,48},{32,0},{48,16},{64,96},{80,112},{96,64},{112,80},{1... | collective-permute-start | bytes 884744 | tf_op jit(solution)/shard_map/ppermute | solution.py:195
  89.5 3.4 %collective-permute-start.9 = (bf16[128,1152]{1,0:T(8,128)(2,1)}, bf16[128,1152]{1,0:T(8,128)(2,1)S(1)}, u32[]{:S(2)}, u32[]{:S(2)}) collective-permute-start(bf16[128,1152]{1,0:T(8,128)(2,1)} %copy-done.2), channel_id=1, source_target_pairs={{0,48},{16,0},{32,16},{48,32},{64,112},{80,64},{96,80},{112,96},{1... | collective-permute-start | bytes 884744 | tf_op jit(solution)/shard_map/ppermute | solution.py:195
  92.9 1.9 %collective-permute-start.8 = (bf16[128,1152]{1,0:T(8,128)(2,1)}, bf16[128,1152]{1,0:T(8,128)(2,1)S(1)}, u32[]{:S(2)}, u32[]{:S(2)}) collective-permute-start(bf16[128,1152]{1,0:T(8,128)(2,1)} %copy-done.2), channel_id=1, source_target_pairs={{0,16},{16,32},{32,48},{48,0},{64,80},{80,96},{96,112},{112,64},{1... | collective-permute-start | bytes 884744 | tf_op jit(solution)/shard_map/ppermute | solution.py:195
  94.8 4.6 %collective-permute-start.13 = (bf16[128,1152]{1,0:T(8,128)(2,1)}, bf16[128,1152]{1,0:T(8,128)(2,1)S(1)}, u32[]{:S(2)}, u32[]{:S(2)}) collective-permute-start(bf16[128,1152]{1,0:T(8,128)(2,1)} %collective-permute-done.4.refs_3_), channel_id=1, source_target_pairs={{0,32},{16,48},{32,0},{48,16},{64,96},{80,112},{96,64},{112,80},{1... | collective-permute-start | bytes 884744 | tf_op jit(solution)/shard_map/ppermute | solution.py:195
  99.4 2.5 %collective-permute-start.12 = (bf16[128,1152]{1,0:T(8,128)(2,1)}, bf16[128,1152]{1,0:T(8,128)(2,1)S(1)}, u32[]{:S(2)}, u32[]{:S(2)}) collective-permute-start(bf16[128,1152]{1,0:T(8,128)(2,1)} %collective-permute-done.4.refs_3_), channel_id=1, source_target_pairs={{0,48},{16,0},{32,16},{48,32},{64,112},{80,64},{96,80},{112,96},{1... | collective-permute-start | bytes 884744 | tf_op jit(solution)/shard_map/ppermute | solution.py:195
  101.9 2.8 %collective-permute-start.11 = (bf16[128,1152]{1,0:T(8,128)(2,1)}, bf16[128,1152]{1,0:T(8,128)(2,1)S(1)}, u32[]{:S(2)}, u32[]{:S(2)}) collective-permute-start(bf16[128,1152]{1,0:T(8,128)(2,1)} %collective-permute-done.4.refs_3_), channel_id=1, source_target_pairs={{0,16},{16,32},{32,48},{48,0},{64,80},{80,96},{96,112},{112,64},{1... | collective-permute-start | bytes 884744 | tf_op jit(solution)/shard_map/ppermute | solution.py:195
  104.7 1.4 %collective-permute-done.8.refs_0_ = bf16[128,1152]{1,0:T(8,128)(2,1)S(1)} collective-permute-done((bf16[128,1152]{1,0:T(8,128)(2,1)}, bf16[128,1152]{1,0:T(8,128)(2,1)S(1)}, u32[]{:S(2)}, u32[]{:S(2)}) %collective-permute-start.8) | collective-permute-done | bytes 294944 | tf_op jit(solution)/shard_map/ppermute | solution.py:195
  106.1 6.0 %collective-permute-done.13.refs_6_ = bf16[128,1152]{1,0:T(8,128)(2,1)S(1)} collective-permute-done((bf16[128,1152]{1,0:T(8,128)(2,1)}, bf16[128,1152]{1,0:T(8,128)(2,1)S(1)}, u32[]{:S(2)}, u32[]{:S(2)}) %collective-permute-start.13) | collective-permute-done | bytes 294944 | tf_op jit(solution)/shard_map/ppermute | solution.py:195
  112.1 4.5 %collective-permute-done.12.refs_5_ = bf16[128,1152]{1,0:T(8,128)(2,1)S(1)} collective-permute-done((bf16[128,1152]{1,0:T(8,128)(2,1)}, bf16[128,1152]{1,0:T(8,128)(2,1)S(1)}, u32[]{:S(2)}, u32[]{:S(2)}) %collective-permute-start.12) | collective-permute-done | bytes 294944 | tf_op jit(solution)/shard_map/ppermute | solution.py:195
  116.6 2.1 %collective-permute-done.11.refs_4_ = bf16[128,1152]{1,0:T(8,128)(2,1)S(1)} collective-permute-done((bf16[128,1152]{1,0:T(8,128)(2,1)}, bf16[128,1152]{1,0:T(8,128)(2,1)S(1)}, u32[]{:S(2)}, u32[]{:S(2)}) %collective-permute-start.11) | collective-permute-done | bytes 294944 | tf_op jit(solution)/shard_map/ppermute | solution.py:195
  118.8 1.0 copy-done.3
  119.7 1.1 copy-done.7
  121.6 4.2 %shard_map.82 = f32[128,1152]{1,0:T(8,128)} custom-call(f32[1]{0:T(128)} %bitcast.9.scale_ref, f32[1]{0:T(128)} %bitcast.12.shift_ref, s32[1,128]{1,0:T(1,128)S(1)} %copy-done.15, f32[128,1152]{1,0:T(8,128)S(1)} %copy-done.7, f32[128,1]{1,0:T(8,128)S(1)} %copy-done.14, bf16[128,1152]{1,0:T(8,128)(2,1)S(1)} %copy-done.3, ...), custom_call_target="tpu_custom_call" | custom-call | tf_op jit(solution)/shard_map/pallas_call | solution.py:25
  125.8 1.1 shard_map.83
  (37 shorter events, 3.7 us)
Async XLA Ops:
  0.6 31.4 %collective-permute-start.3 = (bf16[128,1152]{1,0:T(8,128)(2,1)}, bf16[128,1152]{1,0:T(8,128)(2,1)S(1)}, u32[]{:S(2)}, u32[]{:S(2)}) collective-permute-start(bf16[128,1152]{1,0:T(8,128)(2,1)} %bitcast.15), channel_id=1, source_target_pairs={{0,64},{16,80},{32,96},{48,112},{64,0},{80,16},{96,32},{112,48},{1... | collective-permute-start | bytes 884744 | tf_op jit(solution)/shard_map/ppermute | solution.py:210
  16.9 1.8 %copy-start = (bf16[1152,1152]{1,0:T(8,128)(2,1)S(1)}, bf16[1152,1152]{1,0:T(8,128)(2,1)}, u32[]{:S(2)}) copy-start(bf16[1152,1152]{1,0:T(8,128)(2,1)} %refs_7_.1) | copy-start | bytes 7962628
  18.7 1.0 copy-start.4
  19.6 1.0 copy-start.8
  20.6 11.4 %copy-start.1 = (bf16[1152,1152]{1,0:T(8,128)(2,1)S(1)}, bf16[1152,1152]{1,0:T(8,128)(2,1)}, u32[]{:S(2)}) copy-start(bf16[1152,1152]{1,0:T(8,128)(2,1)} %refs_7_.1) | copy-start | bytes 7962628
  20.6 28.5 %copy-start.15 = (s32[1,128]{1,0:T(1,128)S(1)}, s32[1,128]{1,0:T(1,128)}, u32[]{:S(2)}) copy-start(s32[1,128]{1,0:T(1,128)} %lab_ref.5) | copy-start | bytes 1540
  22.0 22.5 %copy-start.6 = (f32[128,1152]{1,0:T(8,128)}, f32[128,1152]{1,0:T(8,128)S(1)}, u32[]{:S(2)}) copy-start(f32[128,1152]{1,0:T(8,128)S(1)} %get-tuple-element.14.unit_ref) | copy-start | bytes 1769476
  22.0 22.5 %copy-start.13 = (f32[128,1]{1,0:T(8,128)}, f32[128,1]{1,0:T(8,128)S(1)}, u32[]{:S(2)}) copy-start(f32[128,1]{1,0:T(8,128)S(1)} %get-tuple-element.15.inv_ref) | copy-start | bytes 1540
  22.0 34.2 %copy-start.2 = (bf16[128,1152]{1,0:T(8,128)(2,1)}, bf16[128,1152]{1,0:T(8,128)(2,1)S(1)}, u32[]{:S(2)}) copy-start(bf16[128,1152]{1,0:T(8,128)(2,1)S(1)} %get-tuple-element.23.x_ref) | copy-start | bytes 884740
  22.0 19.0 %collective-permute-start.2 = (bf16[128,1152]{1,0:T(8,128)(2,1)}, bf16[128,1152]{1,0:T(8,128)(2,1)S(1)}, u32[]{:S(2)}, u32[]{:S(2)}) collective-permute-start(bf16[128,1152]{1,0:T(8,128)(2,1)} %get-tuple-element.17.y_ref), channel_id=1, source_target_pairs={{0,32},{16,48},{32,0},{48,16},{64,96},{80,112},{96,64},{112,80},{1... | collective-permute-start | bytes 884744 | tf_op jit(solution)/shard_map/ppermute | solution.py:195
  26.7 17.9 %collective-permute-start.1 = (bf16[128,1152]{1,0:T(8,128)(2,1)}, bf16[128,1152]{1,0:T(8,128)(2,1)S(1)}, u32[]{:S(2)}, u32[]{:S(2)}) collective-permute-start(bf16[128,1152]{1,0:T(8,128)(2,1)} %get-tuple-element.17.y_ref), channel_id=1, source_target_pairs={{0,48},{16,0},{32,16},{48,32},{64,112},{80,64},{96,80},{112,96},{1... | collective-permute-start | bytes 884744 | tf_op jit(solution)/shard_map/ppermute | solution.py:195
  29.5 20.0 %collective-permute-start = (bf16[128,1152]{1,0:T(8,128)(2,1)}, bf16[128,1152]{1,0:T(8,128)(2,1)}, u32[]{:S(2)}, u32[]{:S(2)}) collective-permute-start(bf16[128,1152]{1,0:T(8,128)(2,1)} %get-tuple-element.17.y_ref), channel_id=1, source_target_pairs={{0,16},{16,32},{32,48},{48,0},{64,80},{80,96},{96,112},{112,64},{1... | collective-permute-start | bytes 884744 | tf_op jit(solution)/shard_map/ppermute | solution.py:195
  32.0 24.3 %copy-start.5 = (bf16[1,128,1152]{2,1,0:T(8,128)(2,1)S(1)}, bf16[1,128,1152]{2,1,0:T(8,128)(2,1)}, u32[]{:S(2)}) copy-start(bf16[1,128,1152]{2,1,0:T(8,128)(2,1)} %param.6) | copy-start | bytes 884740
  32.7 23.2 %collective-permute-start.4 = (bf16[128,1152]{1,0:T(8,128)(2,1)S(1)}, bf16[128,1152]{1,0:T(8,128)(2,1)}, u32[]{:S(2)}, u32[]{:S(2)}) collective-permute-start(bf16[128,1152]{1,0:T(8,128)(2,1)S(1)} %get-tuple-element.23.x_ref), channel_id=1, source_target_pairs={{0,64},{16,80},{32,96},{48,112},{64,0},{80,16},{96,32},{112,48},{1... | collective-permute-start | bytes 884744 | tf_op jit(solution)/shard_map/ppermute | solution.py:216
  36.4 19.6 %collective-permute-start.7 = (bf16[128,1152]{1,0:T(8,128)(2,1)S(1)}, bf16[128,1152]{1,0:T(8,128)(2,1)}, u32[]{:S(2)}, u32[]{:S(2)}) collective-permute-start(bf16[128,1152]{1,0:T(8,128)(2,1)S(1)} %shard_map.79.a_ref), channel_id=1, source_target_pairs={{0,32},{16,48},{32,0},{48,16},{64,96},{80,112},{96,64},{112,80},{1... | collective-permute-start | bytes 884744 | tf_op jit(solution)/shard_map/ppermute | solution.py:195
  41.1 0.7 copy-start.9
  41.8 14.2 %collective-permute-start.6 = (bf16[128,1152]{1,0:T(8,128)(2,1)S(1)}, bf16[128,1152]{1,0:T(8,128)(2,1)}, u32[]{:S(2)}, u32[]{:S(2)}) collective-permute-start(bf16[128,1152]{1,0:T(8,128)(2,1)S(1)} %shard_map.79.a_ref), channel_id=1, source_target_pairs={{0,48},{16,0},{32,16},{48,32},{64,112},{80,64},{96,80},{112,96},{1... | collective-permute-start | bytes 884744 | tf_op jit(solution)/shard_map/ppermute | solution.py:195
  44.6 0.7 copy-start.11
  45.3 11.0 %collective-permute-start.5 = (bf16[128,1152]{1,0:T(8,128)(2,1)S(1)}, bf16[128,1152]{1,0:T(8,128)(2,1)}, u32[]{:S(2)}, u32[]{:S(2)}) collective-permute-start(bf16[128,1152]{1,0:T(8,128)(2,1)S(1)} %shard_map.79.a_ref), channel_id=1, source_target_pairs={{0,16},{16,32},{32,48},{48,0},{64,80},{80,96},{96,112},{112,64},{1... | collective-permute-start | bytes 884744 | tf_op jit(solution)/shard_map/ppermute | solution.py:195
  49.5 1.0 copy-start.10
  50.5 1.0 copy-start.12
  59.6 66.2 %all-to-all-start = ((bf16[16,184,128]{2,1,0:T(8,128)(2,1)}), bf16[16,184,128]{2,1,0:T(8,128)(2,1)S(1)}, u32[]{:S(2)}, u32[]{:S(2)}) async-start(bf16[16,184,128]{2,1,0:T(8,128)(2,1)} %shard_map.81), calls=%async_computation | async-start | bytes 1507328 | tf_op jit(solution)/shard_map/all_to_all | solution.py:226
  87.2 14.7 %collective-permute-start.10 = (bf16[128,1152]{1,0:T(8,128)(2,1)}, bf16[128,1152]{1,0:T(8,128)(2,1)S(1)}, u32[]{:S(2)}, u32[]{:S(2)}) collective-permute-start(bf16[128,1152]{1,0:T(8,128)(2,1)} %copy-done.2), channel_id=1, source_target_pairs={{0,32},{16,48},{32,0},{48,16},{64,96},{80,112},{96,64},{112,80},{1... | collective-permute-start | bytes 884744 | tf_op jit(solution)/shard_map/ppermute | solution.py:195
  89.5 15.2 %collective-permute-start.9 = (bf16[128,1152]{1,0:T(8,128)(2,1)}, bf16[128,1152]{1,0:T(8,128)(2,1)S(1)}, u32[]{:S(2)}, u32[]{:S(2)}) collective-permute-start(bf16[128,1152]{1,0:T(8,128)(2,1)} %copy-done.2), channel_id=1, source_target_pairs={{0,48},{16,0},{32,16},{48,32},{64,112},{80,64},{96,80},{112,96},{1... | collective-permute-start | bytes 884744 | tf_op jit(solution)/shard_map/ppermute | solution.py:195
  92.9 13.2 %collective-permute-start.8 = (bf16[128,1152]{1,0:T(8,128)(2,1)}, bf16[128,1152]{1,0:T(8,128)(2,1)S(1)}, u32[]{:S(2)}, u32[]{:S(2)}) collective-permute-start(bf16[128,1152]{1,0:T(8,128)(2,1)} %copy-done.2), channel_id=1, source_target_pairs={{0,16},{16,32},{32,48},{48,0},{64,80},{80,96},{96,112},{112,64},{1... | collective-permute-start | bytes 884744 | tf_op jit(solution)/shard_map/ppermute | solution.py:195
  94.8 17.3 %collective-permute-start.13 = (bf16[128,1152]{1,0:T(8,128)(2,1)}, bf16[128,1152]{1,0:T(8,128)(2,1)S(1)}, u32[]{:S(2)}, u32[]{:S(2)}) collective-permute-start(bf16[128,1152]{1,0:T(8,128)(2,1)} %collective-permute-done.4.refs_3_), channel_id=1, source_target_pairs={{0,32},{16,48},{32,0},{48,16},{64,96},{80,112},{96,64},{112,80},{1... | collective-permute-start | bytes 884744 | tf_op jit(solution)/shard_map/ppermute | solution.py:195
  99.4 17.3 %collective-permute-start.12 = (bf16[128,1152]{1,0:T(8,128)(2,1)}, bf16[128,1152]{1,0:T(8,128)(2,1)S(1)}, u32[]{:S(2)}, u32[]{:S(2)}) collective-permute-start(bf16[128,1152]{1,0:T(8,128)(2,1)} %collective-permute-done.4.refs_3_), channel_id=1, source_target_pairs={{0,48},{16,0},{32,16},{48,32},{64,112},{80,64},{96,80},{112,96},{1... | collective-permute-start | bytes 884744 | tf_op jit(solution)/shard_map/ppermute | solution.py:195
  101.9 16.9 %collective-permute-start.11 = (bf16[128,1152]{1,0:T(8,128)(2,1)}, bf16[128,1152]{1,0:T(8,128)(2,1)S(1)}, u32[]{:S(2)}, u32[]{:S(2)}) collective-permute-start(bf16[128,1152]{1,0:T(8,128)(2,1)} %collective-permute-done.4.refs_3_), channel_id=1, source_target_pairs={{0,16},{16,32},{32,48},{48,0},{64,80},{80,96},{96,112},{112,64},{1... | collective-permute-start | bytes 884744 | tf_op jit(solution)/shard_map/ppermute | solution.py:195
  118.8 1.0 copy-start.3
  119.7 1.1 copy-start.7
  120.8 0.8 copy-start.14

commit v3 on v2

--- a/solution.py
+++ b/solution.py
@@ -212,8 +212,7 @@
         embed_kernel, (block, block, wide, jax.ShapeDtypeStruct((rows, 1), F32)), image, feat, text_head
     )
     part = call(near_image_kernel, wide, *scalars, lab, x, y, *ring(y), scalars=2)
-    x_out, far_feat = lax.optimization_barrier((x, far_feat))
-    far_x = lax.ppermute(x_out, "loop", across)
+    far_x = lax.ppermute(x, "loop", across)
     far_y = call(text_kernel, block, far_feat, text_head)
     far_ys = ring(far_y)
     part, far_x = lax.optimization_barrier((part, far_x))

time: 128 us -> 123 us (0.961)
  starting transfers between devices: 84.7 us -> 66.4 us
  waiting for transfers between devices: 17 us -> 30.8 us
    all_to_all x1, starting transfers between devices: 27.6 us -> 10.4 us  [shards(): lax.all_to_all(sent, 'dp', split_axis=0, concat_axis=0, tiled=True)]
    ppermute x1, waiting for transfers between devices: 2.6 us -> 17.5 us  [shards(): far_x = lax.ppermute(x, 'loop', across)]
    ppermute x1, starting transfers between devices: 3.65 us -> 2.05 us  [shards(): far_x = lax.ppermute(x, 'loop', across)]
where the time goes in v3:
time: 123 us; the launch traced here: 122 us
  starting transfers between devices  66.4 us (54%)
  waiting for transfers between devices  30.8 us (25%)
  Pallas kernels  13.1 us (11%)
  local copies, waits for them, and re-layouts  9.89 us (8%)
  between operations  2.21 us (2%)
    ppermute x12, starting transfers between devices, ring(): return [lax.ppermute(value, 'loop', turn) for turn in turns]  37.7 us
    ppermute x1, waiting for transfers between devices, shards(): far_x = lax.ppermute(x, 'loop', across)  17.5 us
    ppermute x1, starting transfers between devices, shards(): far_feat = lax.ppermute(feat, 'loop', across)  16.3 us
    ppermute x12, waiting for transfers between devices, ring(): return [lax.ppermute(value, 'loop', turn) for turn in turns]  13.3 us
    pallas_call x7, Pallas kernels, call(): pl.pallas_call(kernel, out_shape=outs, in_specs=[smem] * scalars + [vmem]...  13.1 us
    all_to_all x1, starting transfers between devices, shards(): lax.all_to_all(sent, 'dp', split_axis=0, concat_axis=0, tiled=True)  10.4 us
    unnamed x32, local copies, waits for them, and re-layouts  9.89 us
  transfers between devices with their start and end apart: 15, of which 6 were waited for; matrix products, arithmetic and copies ran while one was open for 0% of the time, Pallas kernels for 7%

profile of v3, /device:TPU:1, one launch (start us, length us, event | category | flops | bytes accessed | tf_op | source)
XLA Modules:
  0.0 122.4 jit_solution(12370965527474016814)
XLA Ops:
  0.6 16.3 %collective-permute-start.4 = (bf16[128,1152]{1,0:T(8,128)(2,1)}, bf16[128,1152]{1,0:T(8,128)(2,1)S(1)}, u32[]{:S(2)}, u32[]{:S(2)}) collective-permute-start(bf16[128,1152]{1,0:T(8,128)(2,1)} %bitcast.15), channel_id=1, source_target_pairs={{0,64},{16,80},{32,96},{48,112},{64,0},{80,16},{96,32},{112,48},{1... | collective-permute-start | bytes 884744 | tf_op jit(solution)/shard_map/ppermute | solution.py:210
  16.9 1.7 %copy-done = bf16[1152,1152]{1,0:T(8,128)(2,1)S(1)} copy-done((bf16[1152,1152]{1,0:T(8,128)(2,1)S(1)}, bf16[1152,1152]{1,0:T(8,128)(2,1)}, u32[]{:S(2)}) %copy-start) | copy-done | bytes 2654232
  18.7 1.0 copy-done.4
  19.6 1.0 copy-done.8
  20.6 1.4 %shard_map.77 = (bf16[128,1152]{1,0:T(8,128)(2,1)S(1)}, bf16[128,1152]{1,0:T(8,128)(2,1)}, f32[128,1152]{1,0:T(8,128)S(1)}, f32[128,1]{1,0:T(8,128)S(1)}) custom-call(bf16[128,1152]{1,0:T(8,128)(2,1)S(1)} %bitcast.13, bf16[128,1152]{1,0:T(8,128)(2,1)S(1)} %bitcast.16, bf16[1152,1152]{1,0:T(8,128)(2,1)S(1)} %copy-done), custom_call_target="tpu_custom_call" | custom-call | tf_op jit(solution)/shard_map/pallas_call | solution.py:25
  22.0 4.6 %collective-permute-start.2 = (bf16[128,1152]{1,0:T(8,128)(2,1)}, bf16[128,1152]{1,0:T(8,128)(2,1)S(1)}, u32[]{:S(2)}, u32[]{:S(2)}) collective-permute-start(bf16[128,1152]{1,0:T(8,128)(2,1)} %get-tuple-element.15.y_ref), channel_id=1, source_target_pairs={{0,32},{16,48},{32,0},{48,16},{64,96},{80,112},{96,64},{112,80},{1... | collective-permute-start | bytes 884744 | tf_op jit(solution)/shard_map/ppermute | solution.py:195
  26.7 2.8 %collective-permute-start.1 = (bf16[128,1152]{1,0:T(8,128)(2,1)}, bf16[128,1152]{1,0:T(8,128)(2,1)S(1)}, u32[]{:S(2)}, u32[]{:S(2)}) collective-permute-start(bf16[128,1152]{1,0:T(8,128)(2,1)} %get-tuple-element.15.y_ref), channel_id=1, source_target_pairs={{0,48},{16,0},{32,16},{48,32},{64,112},{80,64},{96,80},{112,96},{1... | collective-permute-start | bytes 884744 | tf_op jit(solution)/shard_map/ppermute | solution.py:195
  29.5 2.5 %collective-permute-start = (bf16[128,1152]{1,0:T(8,128)(2,1)}, bf16[128,1152]{1,0:T(8,128)(2,1)}, u32[]{:S(2)}, u32[]{:S(2)}) collective-permute-start(bf16[128,1152]{1,0:T(8,128)(2,1)} %get-tuple-element.15.y_ref), channel_id=1, source_target_pairs={{0,16},{16,32},{32,48},{48,0},{64,80},{80,96},{96,112},{112,64},{1... | collective-permute-start | bytes 884744 | tf_op jit(solution)/shard_map/ppermute | solution.py:195
  32.0 2.1 %collective-permute-start.3 = (bf16[128,1152]{1,0:T(8,128)(2,1)S(1)}, bf16[128,1152]{1,0:T(8,128)(2,1)}, u32[]{:S(2)}, u32[]{:S(2)}) collective-permute-start(bf16[128,1152]{1,0:T(8,128)(2,1)S(1)} %get-tuple-element.19.x_ref), channel_id=1, source_target_pairs={{0,64},{16,80},{32,96},{48,112},{64,0},{80,16},{96,32},{112,48},{1... | collective-permute-start | bytes 884744 | tf_op jit(solution)/shard_map/ppermute | solution.py:215
  34.8 2.6 %collective-permute-start.7 = (bf16[128,1152]{1,0:T(8,128)(2,1)S(1)}, bf16[128,1152]{1,0:T(8,128)(2,1)}, u32[]{:S(2)}, u32[]{:S(2)}) collective-permute-start(bf16[128,1152]{1,0:T(8,128)(2,1)S(1)} %shard_map.79.a_ref), channel_id=1, source_target_pairs={{0,32},{16,48},{32,0},{48,16},{64,96},{80,112},{96,64},{112,80},{1... | collective-permute-start | bytes 884744 | tf_op jit(solution)/shard_map/ppermute | solution.py:195
  38.1 4.0 %collective-permute-start.6 = (bf16[128,1152]{1,0:T(8,128)(2,1)S(1)}, bf16[128,1152]{1,0:T(8,128)(2,1)}, u32[]{:S(2)}, u32[]{:S(2)}) collective-permute-start(bf16[128,1152]{1,0:T(8,128)(2,1)S(1)} %shard_map.79.a_ref), channel_id=1, source_target_pairs={{0,48},{16,0},{32,16},{48,32},{64,112},{80,64},{96,80},{112,96},{1... | collective-permute-start | bytes 884744 | tf_op jit(solution)/shard_map/ppermute | solution.py:195
  42.1 0.7 copy-done.11
  42.8 2.8 %collective-permute-start.5 = (bf16[128,1152]{1,0:T(8,128)(2,1)S(1)}, bf16[128,1152]{1,0:T(8,128)(2,1)}, u32[]{:S(2)}, u32[]{:S(2)}) collective-permute-start(bf16[128,1152]{1,0:T(8,128)(2,1)S(1)} %shard_map.79.a_ref), channel_id=1, source_target_pairs={{0,16},{16,32},{32,48},{48,0},{64,80},{80,96},{96,112},{112,64},{1... | collective-permute-start | bytes 884744 | tf_op jit(solution)/shard_map/ppermute | solution.py:195
  47.3 1.0 copy-done.10
  48.3 1.0 copy-done.12
  49.3 1.9 %shard_map.78.part_ref = f32[128,1152]{1,0:T(8,128)S(1)} custom-call(f32[1]{0:T(128)} %bitcast.7.scale_ref, f32[1]{0:T(128)} %bitcast.10.shift_ref, s32[1,128]{1,0:T(1,128)S(1)} %copy-done.15, bf16[128,1152]{1,0:T(8,128)(2,1)S(1)} %get-tuple-element.19.x_ref, bf16[128,1152]{1,0:T(8,128)(2,1)} %get-tuple-element.15.y_ref, ...), custom_call_target="tpu_custom_call" | custom-call | tf_op jit(solution)/shard_map/pallas_call | solution.py:25
  51.2 17.5 %collective-permute-done.3.refs_3_ = bf16[128,1152]{1,0:T(8,128)(2,1)} collective-permute-done((bf16[128,1152]{1,0:T(8,128)(2,1)S(1)}, bf16[128,1152]{1,0:T(8,128)(2,1)}, u32[]{:S(2)}, u32[]{:S(2)}) %collective-permute-start.3) | collective-permute-done | bytes 294944 | tf_op jit(solution)/shard_map/ppermute | solution.py:215
  68.7 3.4 %shard_map.81 = bf16[16,184,128]{2,1,0:T(8,128)(2,1)} custom-call(f32[1]{0:T(128)} %bitcast.8.scale_ref, f32[1]{0:T(128)} %bitcast.11.shift_ref, bf16[128,1152]{1,0:T(8,128)(2,1)S(1)} %bitcast.14, bf16[128,1152]{1,0:T(8,128)(2,1)S(1)} %get-tuple-element.19.x_ref, f32[128,1152]{1,0:T(8,128)S(1)} %shard_map.78.part_ref, ...), custom_call_target="tpu_custom_call" | custom-call | tf_op jit(solution)/shard_map/pallas_call | solution.py:25
  72.1 10.4 %all-to-all-start = ((bf16[16,184,128]{2,1,0:T(8,128)(2,1)}), bf16[16,184,128]{2,1,0:T(8,128)(2,1)S(1)}, u32[]{:S(2)}, u32[]{:S(2)}) async-start(bf16[16,184,128]{2,1,0:T(8,128)(2,1)} %shard_map.81), calls=%async_computation | async-start | bytes 1507328 | tf_op jit(solution)/shard_map/all_to_all | solution.py:225
  82.5 3.6 %collective-permute-start.13 = (bf16[128,1152]{1,0:T(8,128)(2,1)}, bf16[128,1152]{1,0:T(8,128)(2,1)S(1)}, u32[]{:S(2)}, u32[]{:S(2)}) collective-permute-start(bf16[128,1152]{1,0:T(8,128)(2,1)} %collective-permute-done.3.refs_3_), channel_id=1, source_target_pairs={{0,32},{16,48},{32,0},{48,16},{64,96},{80,112},{96,64},{112,80},{1... | collective-permute-start | bytes 884744 | tf_op jit(solution)/shard_map/ppermute | solution.py:195
  86.1 3.9 %collective-permute-start.12 = (bf16[128,1152]{1,0:T(8,128)(2,1)}, bf16[128,1152]{1,0:T(8,128)(2,1)S(1)}, u32[]{:S(2)}, u32[]{:S(2)}) collective-permute-start(bf16[128,1152]{1,0:T(8,128)(2,1)} %collective-permute-done.3.refs_3_), channel_id=1, source_target_pairs={{0,48},{16,0},{32,16},{48,32},{64,112},{80,64},{96,80},{112,96},{1... | collective-permute-start | bytes 884744 | tf_op jit(solution)/shard_map/ppermute | solution.py:195
  89.9 1.9 %collective-permute-start.11 = (bf16[128,1152]{1,0:T(8,128)(2,1)}, bf16[128,1152]{1,0:T(8,128)(2,1)S(1)}, u32[]{:S(2)}, u32[]{:S(2)}) collective-permute-start(bf16[128,1152]{1,0:T(8,128)(2,1)} %collective-permute-done.3.refs_3_), channel_id=1, source_target_pairs={{0,16},{16,32},{32,48},{48,0},{64,80},{80,96},{96,112},{112,64},{1... | collective-permute-start | bytes 884744 | tf_op jit(solution)/shard_map/ppermute | solution.py:195
  91.9 3.1 %collective-permute-start.10 = (bf16[128,1152]{1,0:T(8,128)(2,1)}, bf16[128,1152]{1,0:T(8,128)(2,1)S(1)}, u32[]{:S(2)}, u32[]{:S(2)}) collective-permute-start(bf16[128,1152]{1,0:T(8,128)(2,1)} %copy-done.2), channel_id=1, source_target_pairs={{0,32},{16,48},{32,0},{48,16},{64,96},{80,112},{96,64},{112,80},{1... | collective-permute-start | bytes 884744 | tf_op jit(solution)/shard_map/ppermute | solution.py:195
  95.0 4.0 %collective-permute-start.9 = (bf16[128,1152]{1,0:T(8,128)(2,1)}, bf16[128,1152]{1,0:T(8,128)(2,1)S(1)}, u32[]{:S(2)}, u32[]{:S(2)}) collective-permute-start(bf16[128,1152]{1,0:T(8,128)(2,1)} %copy-done.2), channel_id=1, source_target_pairs={{0,48},{16,0},{32,16},{48,32},{64,112},{80,64},{96,80},{112,96},{1... | collective-permute-start | bytes 884744 | tf_op jit(solution)/shard_map/ppermute | solution.py:195
  99.0 1.9 %collective-permute-start.8 = (bf16[128,1152]{1,0:T(8,128)(2,1)}, bf16[128,1152]{1,0:T(8,128)(2,1)S(1)}, u32[]{:S(2)}, u32[]{:S(2)}) collective-permute-start(bf16[128,1152]{1,0:T(8,128)(2,1)} %copy-done.2), channel_id=1, source_target_pairs={{0,16},{16,32},{32,48},{48,0},{64,80},{80,96},{96,112},{112,64},{1... | collective-permute-start | bytes 884744 | tf_op jit(solution)/shard_map/ppermute | solution.py:195
  101.3 6.0 %collective-permute-done.10.refs_2_ = bf16[128,1152]{1,0:T(8,128)(2,1)S(1)} collective-permute-done((bf16[128,1152]{1,0:T(8,128)(2,1)}, bf16[128,1152]{1,0:T(8,128)(2,1)S(1)}, u32[]{:S(2)}, u32[]{:S(2)}) %collective-permute-start.10) | collective-permute-done | bytes 294944 | tf_op jit(solution)/shard_map/ppermute | solution.py:195
  107.3 6.4 %collective-permute-done.9.refs_1_ = bf16[128,1152]{1,0:T(8,128)(2,1)S(1)} collective-permute-done((bf16[128,1152]{1,0:T(8,128)(2,1)}, bf16[128,1152]{1,0:T(8,128)(2,1)S(1)}, u32[]{:S(2)}, u32[]{:S(2)}) %collective-permute-start.9) | collective-permute-done | bytes 294944 | tf_op jit(solution)/shard_map/ppermute | solution.py:195
  114.3 1.0 copy-done.3
  115.2 1.1 copy-done.7
  116.3 0.8 copy-done.14
  117.1 4.2 %shard_map.82 = f32[128,1152]{1,0:T(8,128)} custom-call(f32[1]{0:T(128)} %bitcast.9.scale_ref, f32[1]{0:T(128)} %bitcast.12.shift_ref, s32[1,128]{1,0:T(1,128)S(1)} %copy-done.15, f32[128,1152]{1,0:T(8,128)S(1)} %copy-done.7, f32[128,1]{1,0:T(8,128)S(1)} %copy-done.14, bf16[128,1152]{1,0:T(8,128)(2,1)S(1)} %copy-done.3, ...), custom_call_target="tpu_custom_call" | custom-call | tf_op jit(solution)/shard_map/pallas_call | solution.py:25
  121.3 1.1 shard_map.83
  (37 shorter events, 2.7 us)
Async XLA Ops:
  0.6 33.4 %collective-permute-start.4 = (bf16[128,1152]{1,0:T(8,128)(2,1)}, bf16[128,1152]{1,0:T(8,128)(2,1)S(1)}, u32[]{:S(2)}, u32[]{:S(2)}) collective-permute-start(bf16[128,1152]{1,0:T(8,128)(2,1)} %bitcast.15), channel_id=1, source_target_pairs={{0,64},{16,80},{32,96},{48,112},{64,0},{80,16},{96,32},{112,48},{1... | collective-permute-start | bytes 884744 | tf_op jit(solution)/shard_map/ppermute | solution.py:210
  16.9 1.8 %copy-start = (bf16[1152,1152]{1,0:T(8,128)(2,1)S(1)}, bf16[1152,1152]{1,0:T(8,128)(2,1)}, u32[]{:S(2)}) copy-start(bf16[1152,1152]{1,0:T(8,128)(2,1)} %refs_7_.1) | copy-start | bytes 7962628
  18.7 1.0 copy-start.4
  19.6 1.0 copy-start.8
  20.6 13.5 %copy-start.1 = (bf16[1152,1152]{1,0:T(8,128)(2,1)S(1)}, bf16[1152,1152]{1,0:T(8,128)(2,1)}, u32[]{:S(2)}) copy-start(bf16[1152,1152]{1,0:T(8,128)(2,1)} %refs_7_.1) | copy-start | bytes 7962628
  20.6 26.4 %copy-start.15 = (s32[1,128]{1,0:T(1,128)S(1)}, s32[1,128]{1,0:T(1,128)}, u32[]{:S(2)}) copy-start(s32[1,128]{1,0:T(1,128)} %lab_ref.5) | copy-start | bytes 1540
  22.0 20.0 %copy-start.6 = (f32[128,1152]{1,0:T(8,128)}, f32[128,1152]{1,0:T(8,128)S(1)}, u32[]{:S(2)}) copy-start(f32[128,1152]{1,0:T(8,128)S(1)} %get-tuple-element.12.unit_ref) | copy-start | bytes 1769476
  22.0 20.0 %copy-start.13 = (f32[128,1]{1,0:T(8,128)}, f32[128,1]{1,0:T(8,128)S(1)}, u32[]{:S(2)}) copy-start(f32[128,1]{1,0:T(8,128)S(1)} %get-tuple-element.13.inv_ref) | copy-start | bytes 1540
  22.0 46.6 %copy-start.2 = (bf16[128,1152]{1,0:T(8,128)(2,1)}, bf16[128,1152]{1,0:T(8,128)(2,1)S(1)}, u32[]{:S(2)}) copy-start(bf16[128,1152]{1,0:T(8,128)(2,1)S(1)} %get-tuple-element.19.x_ref) | copy-start | bytes 884740
  22.0 15.3 %collective-permute-start.2 = (bf16[128,1152]{1,0:T(8,128)(2,1)}, bf16[128,1152]{1,0:T(8,128)(2,1)S(1)}, u32[]{:S(2)}, u32[]{:S(2)}) collective-permute-start(bf16[128,1152]{1,0:T(8,128)(2,1)} %get-tuple-element.15.y_ref), channel_id=1, source_target_pairs={{0,32},{16,48},{32,0},{48,16},{64,96},{80,112},{96,64},{112,80},{1... | collective-permute-start | bytes 884744 | tf_op jit(solution)/shard_map/ppermute | solution.py:195
  26.7 15.4 %collective-permute-start.1 = (bf16[128,1152]{1,0:T(8,128)(2,1)}, bf16[128,1152]{1,0:T(8,128)(2,1)S(1)}, u32[]{:S(2)}, u32[]{:S(2)}) collective-permute-start(bf16[128,1152]{1,0:T(8,128)(2,1)} %get-tuple-element.15.y_ref), channel_id=1, source_target_pairs={{0,48},{16,0},{32,16},{48,32},{64,112},{80,64},{96,80},{112,96},{1... | collective-permute-start | bytes 884744 | tf_op jit(solution)/shard_map/ppermute | solution.py:195
  29.5 17.9 %collective-permute-start = (bf16[128,1152]{1,0:T(8,128)(2,1)}, bf16[128,1152]{1,0:T(8,128)(2,1)}, u32[]{:S(2)}, u32[]{:S(2)}) collective-permute-start(bf16[128,1152]{1,0:T(8,128)(2,1)} %get-tuple-element.15.y_ref), channel_id=1, source_target_pairs={{0,16},{16,32},{32,48},{48,0},{64,80},{80,96},{96,112},{112,64},{1... | collective-permute-start | bytes 884744 | tf_op jit(solution)/shard_map/ppermute | solution.py:195
  32.0 36.7 %copy-start.5 = (bf16[1,128,1152]{2,1,0:T(8,128)(2,1)S(1)}, bf16[1,128,1152]{2,1,0:T(8,128)(2,1)}, u32[]{:S(2)}) copy-start(bf16[1,128,1152]{2,1,0:T(8,128)(2,1)} %param.6) | copy-start | bytes 884740
  32.0 36.7 %collective-permute-start.3 = (bf16[128,1152]{1,0:T(8,128)(2,1)S(1)}, bf16[128,1152]{1,0:T(8,128)(2,1)}, u32[]{:S(2)}, u32[]{:S(2)}) collective-permute-start(bf16[128,1152]{1,0:T(8,128)(2,1)S(1)} %get-tuple-element.19.x_ref), channel_id=1, source_target_pairs={{0,64},{16,80},{32,96},{48,112},{64,0},{80,16},{96,32},{112,48},{1... | collective-permute-start | bytes 884744 | tf_op jit(solution)/shard_map/ppermute | solution.py:215
  34.8 33.9 %collective-permute-start.7 = (bf16[128,1152]{1,0:T(8,128)(2,1)S(1)}, bf16[128,1152]{1,0:T(8,128)(2,1)}, u32[]{:S(2)}, u32[]{:S(2)}) collective-permute-start(bf16[128,1152]{1,0:T(8,128)(2,1)S(1)} %shard_map.79.a_ref), channel_id=1, source_target_pairs={{0,32},{16,48},{32,0},{48,16},{64,96},{80,112},{96,64},{112,80},{1... | collective-permute-start | bytes 884744 | tf_op jit(solution)/shard_map/ppermute | solution.py:195
  37.4 0.7 copy-start.9
  38.1 30.6 %collective-permute-start.6 = (bf16[128,1152]{1,0:T(8,128)(2,1)S(1)}, bf16[128,1152]{1,0:T(8,128)(2,1)}, u32[]{:S(2)}, u32[]{:S(2)}) collective-permute-start(bf16[128,1152]{1,0:T(8,128)(2,1)S(1)} %shard_map.79.a_ref), channel_id=1, source_target_pairs={{0,48},{16,0},{32,16},{48,32},{64,112},{80,64},{96,80},{112,96},{1... | collective-permute-start | bytes 884744 | tf_op jit(solution)/shard_map/ppermute | solution.py:195
  42.1 0.7 copy-start.11
  42.8 25.9 %collective-permute-start.5 = (bf16[128,1152]{1,0:T(8,128)(2,1)S(1)}, bf16[128,1152]{1,0:T(8,128)(2,1)}, u32[]{:S(2)}, u32[]{:S(2)}) collective-permute-start(bf16[128,1152]{1,0:T(8,128)(2,1)S(1)} %shard_map.79.a_ref), channel_id=1, source_target_pairs={{0,16},{16,32},{32,48},{48,0},{64,80},{80,96},{96,112},{112,64},{1... | collective-permute-start | bytes 884744 | tf_op jit(solution)/shard_map/ppermute | solution.py:195
  47.3 1.0 copy-start.10
  48.3 1.0 copy-start.12
  72.1 49.2 %all-to-all-start = ((bf16[16,184,128]{2,1,0:T(8,128)(2,1)}), bf16[16,184,128]{2,1,0:T(8,128)(2,1)S(1)}, u32[]{:S(2)}, u32[]{:S(2)}) async-start(bf16[16,184,128]{2,1,0:T(8,128)(2,1)} %shard_map.81), calls=%async_computation | async-start | bytes 1507328 | tf_op jit(solution)/shard_map/all_to_all | solution.py:225
  82.5 16.5 %collective-permute-start.13 = (bf16[128,1152]{1,0:T(8,128)(2,1)}, bf16[128,1152]{1,0:T(8,128)(2,1)S(1)}, u32[]{:S(2)}, u32[]{:S(2)}) collective-permute-start(bf16[128,1152]{1,0:T(8,128)(2,1)} %collective-permute-done.3.refs_3_), channel_id=1, source_target_pairs={{0,32},{16,48},{32,0},{48,16},{64,96},{80,112},{96,64},{112,80},{1... | collective-permute-start | bytes 884744 | tf_op jit(solution)/shard_map/ppermute | solution.py:195
  86.1 15.0 %collective-permute-start.12 = (bf16[128,1152]{1,0:T(8,128)(2,1)}, bf16[128,1152]{1,0:T(8,128)(2,1)S(1)}, u32[]{:S(2)}, u32[]{:S(2)}) collective-permute-start(bf16[128,1152]{1,0:T(8,128)(2,1)} %collective-permute-done.3.refs_3_), channel_id=1, source_target_pairs={{0,48},{16,0},{32,16},{48,32},{64,112},{80,64},{96,80},{112,96},{1... | collective-permute-start | bytes 884744 | tf_op jit(solution)/shard_map/ppermute | solution.py:195
  89.9 11.4 %collective-permute-start.11 = (bf16[128,1152]{1,0:T(8,128)(2,1)}, bf16[128,1152]{1,0:T(8,128)(2,1)S(1)}, u32[]{:S(2)}, u32[]{:S(2)}) collective-permute-start(bf16[128,1152]{1,0:T(8,128)(2,1)} %collective-permute-done.3.refs_3_), channel_id=1, source_target_pairs={{0,16},{16,32},{32,48},{48,0},{64,80},{80,96},{96,112},{112,64},{1... | collective-permute-start | bytes 884744 | tf_op jit(solution)/shard_map/ppermute | solution.py:195
  91.9 15.5 %collective-permute-start.10 = (bf16[128,1152]{1,0:T(8,128)(2,1)}, bf16[128,1152]{1,0:T(8,128)(2,1)S(1)}, u32[]{:S(2)}, u32[]{:S(2)}) collective-permute-start(bf16[128,1152]{1,0:T(8,128)(2,1)} %copy-done.2), channel_id=1, source_target_pairs={{0,32},{16,48},{32,0},{48,16},{64,96},{80,112},{96,64},{112,80},{1... | collective-permute-start | bytes 884744 | tf_op jit(solution)/shard_map/ppermute | solution.py:195
  95.0 18.8 %collective-permute-start.9 = (bf16[128,1152]{1,0:T(8,128)(2,1)}, bf16[128,1152]{1,0:T(8,128)(2,1)S(1)}, u32[]{:S(2)}, u32[]{:S(2)}) collective-permute-start(bf16[128,1152]{1,0:T(8,128)(2,1)} %copy-done.2), channel_id=1, source_target_pairs={{0,48},{16,0},{32,16},{48,32},{64,112},{80,64},{96,80},{112,96},{1... | collective-permute-start | bytes 884744 | tf_op jit(solution)/shard_map/ppermute | solution.py:195
  99.0 15.3 %collective-permute-start.8 = (bf16[128,1152]{1,0:T(8,128)(2,1)}, bf16[128,1152]{1,0:T(8,128)(2,1)S(1)}, u32[]{:S(2)}, u32[]{:S(2)}) collective-permute-start(bf16[128,1152]{1,0:T(8,128)(2,1)} %copy-done.2), channel_id=1, source_target_pairs={{0,16},{16,32},{32,48},{48,0},{64,80},{80,96},{96,112},{112,64},{1... | collective-permute-start | bytes 884744 | tf_op jit(solution)/shard_map/ppermute | solution.py:195
  114.3 1.0 copy-start.3
  115.2 1.1 copy-start.7
  116.3 0.8 copy-start.14

commit v4 on v3

--- a/solution.py
+++ b/solution.py
@@ -19,13 +19,15 @@
 TN = ((0,), (0,))
 
 
-def call(kernel, outs, *operands, scalars=0, scratch=()):
+def call(kernel, outs, *operands, scalars=0, away=0, scratch=()):
     smem = pl.BlockSpec(memory_space=pltpu.SMEM)
     vmem = pl.BlockSpec(memory_space=pltpu.VMEM)
     return pl.pallas_call(
         kernel,
         out_shape=outs,
-        in_specs=[smem] * scalars + [vmem] * (len(operands) - scalars),
+        in_specs=[smem] * scalars
+        + [vmem] * (len(operands) - scalars - away)
+        + [pl.BlockSpec(memory_space=pl.ANY)] * away,
         scratch_shapes=scratch,
         compiler_params=pltpu.CompilerParams(vmem_limit_bytes=48 * 2**20),
     )(*operands)
@@ -103,16 +105,31 @@
         out_ref[owner] = jnp.concatenate([col[:MAIN] for col in cols] + pairs, axis=0).astype(BF16)
 
 
-def text_grad_kernel(scale_ref, shift_ref, lab_ref, unit_ref, inv_ref, x_ref, y_ref, *refs):
-    *other_refs, head_ref, out_ref = refs
+def near_text_kernel(scale_ref, shift_ref, lab_ref, x_ref, y_ref, a_ref, b_ref, c_ref, d_ref, out_ref):
     scale, shift = scale_ref[0], shift_ref[0]
     x, y = x_ref[...], y_ref[...]
     home = home_weights(x, y, lab_ref, scale, shift)
-    others = jnp.concatenate([ref[...] for ref in other_refs], axis=0)
-    weight = apart_weights(y, others, scale, shift)
-    grad = scale * (dot(home, x, TN) + dot(weight, others, NN))
+    others = jnp.concatenate([a_ref[...], b_ref[...], c_ref[...], d_ref[...]], axis=0)
+    out_ref[...] = dot(home, x, TN) + dot(apart_weights(y, others, scale, shift), others, NN)
+
+
+def text_grad_kernel(
+    scale_ref, shift_ref, y_ref, part_ref, a_ref, b_ref, c_ref, inv_hbm, unit_hbm, head_hbm, out_ref,
+    inv_ref, unit_ref, head_ref, sems,
+):
+    scale, shift = scale_ref[0], shift_ref[0]
+    pairs = ((inv_hbm, inv_ref), (unit_hbm, unit_ref), (head_hbm, head_ref))
+    copies = [pltpu.make_async_copy(src, dst, sems.at[at]) for at, (src, dst) in enumerate(pairs)]
+    for copy in copies:
+        copy.start()
+    others = jnp.concatenate([a_ref[...], b_ref[...], c_ref[...]], axis=0)
+    weight = apart_weights(y_ref[...], others, scale, shift)
+    grad = scale * (part_ref[...] + dot(weight, others, NN))
+    copies[0].wait()
+    copies[1].wait()
     unit = unit_ref[...]
     pre = (grad - unit * jnp.sum(unit * grad, axis=-1, keepdims=True)) * inv_ref[...]
+    copies[2].wait()
     out_ref[...] = dot(pre.astype(BF16), head_ref[...], NT)
 
 
@@ -223,9 +240,17 @@
     )
     sent, x_near = lax.optimization_barrier((sent, x))
     arrived = lax.all_to_all(sent, "dp", split_axis=0, concat_axis=0, tiled=True)
-    xs = [*ring(x_near), far_x, *ring(far_x)]
+    part_txt = call(near_text_kernel, wide, *scalars, lab, x, y, *ring(x_near), far_x, scalars=2)
     d_text_feat = call(
-        text_grad_kernel, wide, *scalars, lab, unit_y, inv_y, x, y, *xs, text_head, scalars=2
+        text_grad_kernel, wide, *scalars, y, part_txt, *ring(far_x), inv_y, unit_y, text_head,
+        scalars=2,
+        away=3,
+        scratch=[
+            pltpu.VMEM((rows, 1), F32),
+            pltpu.VMEM((rows, width), F32),
+            pltpu.VMEM(text_head.shape, BF16),
+            pltpu.SemaphoreType.DMA((3,)),
+        ],
     )
     d_image = call(
         sum_kernel,

time: 123 us -> 122 us (level)
  the two profiles are of different devices: /device:TPU:1 before, /device:TPU:35 now
where the time goes in v4:
time: 122 us; the launch traced here: 121 us
  starting transfers between devices  70.9 us (58%)
  waiting for transfers between devices  24.6 us (20%)
  Pallas kernels  14.2 us (12%)
  local copies, waits for them, and re-layouts  8.97 us (7%)
  between operations  2.26 us (2%)
    ppermute x12, starting transfers between devices, ring(): return [lax.ppermute(value, 'loop', turn) for turn in turns]  35.5 us
    all_to_all x1, starting transfers between devices, shards(): lax.all_to_all(sent, 'dp', split_axis=0, concat_axis=0, tiled=True)  18.8 us
    ppermute x1, starting transfers between devices, shards(): far_feat = lax.ppermute(feat, 'loop', across)  14.5 us
    pallas_call x8, Pallas kernels, call(): pl.pallas_call(kernel, out_shape=outs, in_specs=[smem] * scalars + [vmem]...  14.2 us
    ppermute x12, waiting for transfers between devices, ring(): return [lax.ppermute(value, 'loop', turn) for turn in turns]  12.9 us
    ppermute x1, waiting for transfers between devices, shards(): far_feat = lax.ppermute(feat, 'loop', across)  9.65 us
    unnamed x36, local copies, waits for them, and re-layouts  8.97 us
  transfers between devices with their start and end apart: 15, of which 6 were waited for; matrix products, arithmetic and copies ran while one was open for 0% of the time, Pallas kernels for 8%

profile of v4, /device:TPU:35, one launch (start us, length us, event | category | flops | bytes accessed | tf_op | source)
XLA Modules:
  0.0 121.0 jit_solution(6293358537931630581)
XLA Ops:
  0.6 14.5 %collective-permute-start.4 = (bf16[128,1152]{1,0:T(8,128)(2,1)}, bf16[128,1152]{1,0:T(8,128)(2,1)S(1)}, u32[]{:S(2)}, u32[]{:S(2)}) collective-permute-start(bf16[128,1152]{1,0:T(8,128)(2,1)} %bitcast.17), channel_id=1, source_target_pairs={{0,64},{16,80},{32,96},{48,112},{64,0},{80,16},{96,32},{112,48},{1... | collective-permute-start | bytes 884744 | tf_op jit(solution)/shard_map/ppermute | solution.py:227
  15.2 1.7 %copy-done = bf16[1152,1152]{1,0:T(8,128)(2,1)S(1)} copy-done((bf16[1152,1152]{1,0:T(8,128)(2,1)S(1)}, bf16[1152,1152]{1,0:T(8,128)(2,1)}, u32[]{:S(2)}) %copy-start) | copy-done | bytes 2654232
  16.9 1.0 copy-done.6
  17.9 1.0 copy-done.10
  19.6 3.2 %collective-permute-start = (bf16[128,1152]{1,0:T(8,128)(2,1)S(1)}, bf16[128,1152]{1,0:T(8,128)(2,1)S(1)}, u32[]{:S(2)}, u32[]{:S(2)}) collective-permute-start(bf16[128,1152]{1,0:T(8,128)(2,1)S(1)} %get-tuple-element.12.y_ref), channel_id=1, source_target_pairs={{0,16},{16,32},{32,48},{48,0},{64,80},{80,96},{96,112},{112,64},{1... | collective-permute-start | bytes 884744 | tf_op jit(solution)/shard_map/ppermute | solution.py:212
  22.9 2.2 %collective-permute-start.1 = (bf16[128,1152]{1,0:T(8,128)(2,1)S(1)}, bf16[128,1152]{1,0:T(8,128)(2,1)S(1)}, u32[]{:S(2)}, u32[]{:S(2)}) collective-permute-start(bf16[128,1152]{1,0:T(8,128)(2,1)S(1)} %get-tuple-element.12.y_ref), channel_id=1, source_target_pairs={{0,48},{16,0},{32,16},{48,32},{64,112},{80,64},{96,80},{112,96},{1... | collective-permute-start | bytes 884744 | tf_op jit(solution)/shard_map/ppermute | solution.py:212
  25.1 3.8 %collective-permute-start.2 = (bf16[128,1152]{1,0:T(8,128)(2,1)S(1)}, bf16[128,1152]{1,0:T(8,128)(2,1)}, u32[]{:S(2)}, u32[]{:S(2)}) collective-permute-start(bf16[128,1152]{1,0:T(8,128)(2,1)S(1)} %get-tuple-element.12.y_ref), channel_id=1, source_target_pairs={{0,32},{16,48},{32,0},{48,16},{64,96},{80,112},{96,64},{112,80},{1... | collective-permute-start | bytes 884744 | tf_op jit(solution)/shard_map/ppermute | solution.py:212
  28.8 2.1 %collective-permute-start.3 = (bf16[128,1152]{1,0:T(8,128)(2,1)S(1)}, bf16[128,1152]{1,0:T(8,128)(2,1)}, u32[]{:S(2)}, u32[]{:S(2)}) collective-permute-start(bf16[128,1152]{1,0:T(8,128)(2,1)S(1)} %get-tuple-element.17.x_ref), channel_id=1, source_target_pairs={{0,64},{16,80},{32,96},{48,112},{64,0},{80,16},{96,32},{112,48},{1... | collective-permute-start | bytes 884744 | tf_op jit(solution)/shard_map/ppermute | solution.py:232
  30.9 9.6 %collective-permute-done.4.feat_ref = bf16[128,1152]{1,0:T(8,128)(2,1)S(1)} collective-permute-done((bf16[128,1152]{1,0:T(8,128)(2,1)}, bf16[128,1152]{1,0:T(8,128)(2,1)S(1)}, u32[]{:S(2)}, u32[]{:S(2)}) %collective-permute-start.4) | collective-permute-done | bytes 294944 | tf_op jit(solution)/shard_map/ppermute | solution.py:227
  40.6 1.4 %shard_map.79.a_ref = bf16[128,1152]{1,0:T(8,128)(2,1)} custom-call(bf16[128,1152]{1,0:T(8,128)(2,1)S(1)} %collective-permute-done.4.feat_ref, bf16[1152,1152]{1,0:T(8,128)(2,1)S(1)} %copy-done.1), custom_call_target="tpu_custom_call" | custom-call | tf_op jit(solution)/shard_map/pallas_call | solution.py:25
  42.0 3.1 %collective-permute-start.5 = (bf16[128,1152]{1,0:T(8,128)(2,1)}, bf16[128,1152]{1,0:T(8,128)(2,1)}, u32[]{:S(2)}, u32[]{:S(2)}) collective-permute-start(bf16[128,1152]{1,0:T(8,128)(2,1)} %shard_map.79.a_ref), channel_id=1, source_target_pairs={{0,16},{16,32},{32,48},{48,0},{64,80},{80,96},{96,112},{112,64},{1... | collective-permute-start | bytes 884744 | tf_op jit(solution)/shard_map/ppermute | solution.py:212
  45.8 2.2 %collective-permute-start.6 = (bf16[128,1152]{1,0:T(8,128)(2,1)}, bf16[128,1152]{1,0:T(8,128)(2,1)}, u32[]{:S(2)}, u32[]{:S(2)}) collective-permute-start(bf16[128,1152]{1,0:T(8,128)(2,1)} %shard_map.79.a_ref), channel_id=1, source_target_pairs={{0,48},{16,0},{32,16},{48,32},{64,112},{80,64},{96,80},{112,96},{1... | collective-permute-start | bytes 884744 | tf_op jit(solution)/shard_map/ppermute | solution.py:212
  48.7 3.7 %collective-permute-start.7 = (bf16[128,1152]{1,0:T(8,128)(2,1)}, bf16[128,1152]{1,0:T(8,128)(2,1)}, u32[]{:S(2)}, u32[]{:S(2)}) collective-permute-start(bf16[128,1152]{1,0:T(8,128)(2,1)} %shard_map.79.a_ref), channel_id=1, source_target_pairs={{0,32},{16,48},{32,0},{48,16},{64,96},{80,112},{96,64},{112,80},{1... | collective-permute-start | bytes 884744 | tf_op jit(solution)/shard_map/ppermute | solution.py:212
  55.1 1.0 copy-done.14
  56.1 1.8 %shard_map.78.part_ref = f32[128,1152]{1,0:T(8,128)S(1)} custom-call(f32[1]{0:T(128)} %bitcast.7.scale_ref, f32[1]{0:T(128)} %bitcast.11.shift_ref, s32[1,128]{1,0:T(1,128)S(1)} %copy-done.17, bf16[128,1152]{1,0:T(8,128)(2,1)S(1)} %get-tuple-element.17.x_ref, bf16[128,1152]{1,0:T(8,128)(2,1)S(1)} %get-tuple-element.12.y_ref, ...), custom_call_target="tpu_custom_call" | custom-call | tf_op jit(solution)/shard_map/pallas_call | solution.py:25
  58.0 3.4 %collective-permute-done.7.d_ref = bf16[128,1152]{1,0:T(8,128)(2,1)} collective-permute-done((bf16[128,1152]{1,0:T(8,128)(2,1)}, bf16[128,1152]{1,0:T(8,128)(2,1)}, u32[]{:S(2)}, u32[]{:S(2)}) %collective-permute-start.7) | collective-permute-done | bytes 294944 | tf_op jit(solution)/shard_map/ppermute | solution.py:212
  61.4 3.5 %shard_map.81 = bf16[16,184,128]{2,1,0:T(8,128)(2,1)} custom-call(f32[1]{0:T(128)} %bitcast.8.scale_ref, f32[1]{0:T(128)} %bitcast.12.shift_ref, bf16[128,1152]{1,0:T(8,128)(2,1)S(1)} %bitcast.16, bf16[128,1152]{1,0:T(8,128)(2,1)S(1)} %get-tuple-element.17.x_ref, f32[128,1152]{1,0:T(8,128)S(1)} %shard_map.78.part_ref, bf16[128,1152]{1,0:T(8,128)(2,1)} %shard_map.79.a_ref, ...), custom_call_target="tpu_custom_call" | custom-call | tf_op jit(solution)/shard_map/pallas_call | solution.py:25
  64.9 18.8 %all-to-all-start = ((bf16[16,184,128]{2,1,0:T(8,128)(2,1)}), bf16[16,184,128]{2,1,0:T(8,128)(2,1)S(1)}, u32[]{:S(2)}, u32[]{:S(2)}) async-start(bf16[16,184,128]{2,1,0:T(8,128)(2,1)} %shard_map.81), calls=%async_computation | async-start | bytes 1507328 | tf_op jit(solution)/shard_map/all_to_all | solution.py:242
  83.7 3.1 %collective-permute-start.10 = (bf16[128,1152]{1,0:T(8,128)(2,1)}, bf16[128,1152]{1,0:T(8,128)(2,1)S(1)}, u32[]{:S(2)}, u32[]{:S(2)}) collective-permute-start(bf16[128,1152]{1,0:T(8,128)(2,1)} %copy-done.4), channel_id=1, source_target_pairs={{0,32},{16,48},{32,0},{48,16},{64,96},{80,112},{96,64},{112,80},{1... | collective-permute-start | bytes 884744 | tf_op jit(solution)/shard_map/ppermute | solution.py:212
  86.8 1.9 %collective-permute-start.8 = (bf16[128,1152]{1,0:T(8,128)(2,1)}, bf16[128,1152]{1,0:T(8,128)(2,1)S(1)}, u32[]{:S(2)}, u32[]{:S(2)}) collective-permute-start(bf16[128,1152]{1,0:T(8,128)(2,1)} %copy-done.4), channel_id=1, source_target_pairs={{0,16},{16,32},{32,48},{48,0},{64,80},{80,96},{96,112},{112,64},{1... | collective-permute-start | bytes 884744 | tf_op jit(solution)/shard_map/ppermute | solution.py:212
  88.8 3.4 %collective-permute-start.9 = (bf16[128,1152]{1,0:T(8,128)(2,1)}, bf16[128,1152]{1,0:T(8,128)(2,1)S(1)}, u32[]{:S(2)}, u32[]{:S(2)}) collective-permute-start(bf16[128,1152]{1,0:T(8,128)(2,1)} %copy-done.4), channel_id=1, source_target_pairs={{0,48},{16,0},{32,16},{48,32},{64,112},{80,64},{96,80},{112,96},{1... | collective-permute-start | bytes 884744 | tf_op jit(solution)/shard_map/ppermute | solution.py:212
  92.1 2.5 %collective-permute-start.11 = (bf16[128,1152]{1,0:T(8,128)(2,1)}, bf16[128,1152]{1,0:T(8,128)(2,1)S(1)}, u32[]{:S(2)}, u32[]{:S(2)}) collective-permute-start(bf16[128,1152]{1,0:T(8,128)(2,1)} %collective-permute-done.3.d_ref), channel_id=1, source_target_pairs={{0,16},{16,32},{32,48},{48,0},{64,80},{80,96},{96,112},{112,64},{1... | collective-permute-start | bytes 884744 | tf_op jit(solution)/shard_map/ppermute | solution.py:212
  94.6 2.8 %collective-permute-start.12 = (bf16[128,1152]{1,0:T(8,128)(2,1)}, bf16[128,1152]{1,0:T(8,128)(2,1)S(1)}, u32[]{:S(2)}, u32[]{:S(2)}) collective-permute-start(bf16[128,1152]{1,0:T(8,128)(2,1)} %collective-permute-done.3.d_ref), channel_id=1, source_target_pairs={{0,48},{16,0},{32,16},{48,32},{64,112},{80,64},{96,80},{112,96},{1... | collective-permute-start | bytes 884744 | tf_op jit(solution)/shard_map/ppermute | solution.py:212
  97.5 3.6 %collective-permute-start.13 = (bf16[128,1152]{1,0:T(8,128)(2,1)}, bf16[128,1152]{1,0:T(8,128)(2,1)S(1)}, u32[]{:S(2)}, u32[]{:S(2)}) collective-permute-start(bf16[128,1152]{1,0:T(8,128)(2,1)} %collective-permute-done.3.d_ref), channel_id=1, source_target_pairs={{0,32},{16,48},{32,0},{48,16},{64,96},{80,112},{96,64},{112,80},{1... | collective-permute-start | bytes 884744 | tf_op jit(solution)/shard_map/ppermute | solution.py:212
  101.1 1.4 %collective-permute-done.9.b_ref = bf16[128,1152]{1,0:T(8,128)(2,1)S(1)} collective-permute-done((bf16[128,1152]{1,0:T(8,128)(2,1)}, bf16[128,1152]{1,0:T(8,128)(2,1)S(1)}, u32[]{:S(2)}, u32[]{:S(2)}) %collective-permute-start.9) | collective-permute-done | bytes 294944 | tf_op jit(solution)/shard_map/ppermute | solution.py:212
  102.6 1.0 copy-done.3
  104.5 2.0 %shard_map.82.part_ref = f32[128,1152]{1,0:T(8,128)S(1)} custom-call(f32[1]{0:T(128)} %bitcast.9.scale_ref, f32[1]{0:T(128)} %bitcast.13.shift_ref, s32[1,128]{1,0:T(1,128)S(1)} %copy-done.17, bf16[128,1152]{1,0:T(8,128)(2,1)S(1)} %copy-done.5, bf16[128,1152]{1,0:T(8,128)(2,1)S(1)} %copy-done.3, bf16[128,1152]{1,0:T(8,128)(2,1)S(1)} %collective-permute-done.8.a_ref, ...), custom_call_target="tpu_custom_call" | custom-call | tf_op jit(solution)/shard_map/pallas_call | solution.py:25
  106.5 3.1 %collective-permute-done.12.b_ref = bf16[128,1152]{1,0:T(8,128)(2,1)S(1)} collective-permute-done((bf16[128,1152]{1,0:T(8,128)(2,1)}, bf16[128,1152]{1,0:T(8,128)(2,1)S(1)}, u32[]{:S(2)}, u32[]{:S(2)}) %collective-permute-start.12) | collective-permute-done | bytes 294944 | tf_op jit(solution)/shard_map/ppermute | solution.py:212
  109.6 4.9 %collective-permute-done.13.c_ref = bf16[128,1152]{1,0:T(8,128)(2,1)S(1)} collective-permute-done((bf16[128,1152]{1,0:T(8,128)(2,1)}, bf16[128,1152]{1,0:T(8,128)(2,1)S(1)}, u32[]{:S(2)}, u32[]{:S(2)}) %collective-permute-start.13) | collective-permute-done | bytes 294944 | tf_op jit(solution)/shard_map/ppermute | solution.py:212
  114.5 3.3 %shard_map.83 = f32[128,1152]{1,0:T(8,128)} custom-call(f32[1]{0:T(128)} %bitcast.10.scale_ref, f32[1]{0:T(128)} %bitcast.14.shift_ref, bf16[128,1152]{1,0:T(8,128)(2,1)S(1)} %copy-done.3, f32[128,1152]{1,0:T(8,128)S(1)} %shard_map.82.part_ref, bf16[128,1152]{1,0:T(8,128)(2,1)S(1)} %collective-permute-done.11.a_ref, ...), custom_call_target="tpu_custom_call" | custom-call | tf_op jit(solution)/shard_map/pallas_call | solution.py:25
  117.8 2.1 %all-to-all-done.arrived_ref = bf16[16,184,128]{2,1,0:T(8,128)(2,1)S(1)} async-done(((bf16[16,184,128]{2,1,0:T(8,128)(2,1)}), bf16[16,184,128]{2,1,0:T(8,128)(2,1)S(1)}, u32[]{:S(2)}, u32[]{:S(2)}) %all-to-all-start) | async-done | bytes 753696 | tf_op jit(solution)/shard_map/all_to_all | solution.py:242
  119.9 1.1 shard_map.84
  (42 shorter events, 4.5 us)
Async XLA Ops:
  0.6 39.9 %collective-permute-start.4 = (bf16[128,1152]{1,0:T(8,128)(2,1)}, bf16[128,1152]{1,0:T(8,128)(2,1)S(1)}, u32[]{:S(2)}, u32[]{:S(2)}) collective-permute-start(bf16[128,1152]{1,0:T(8,128)(2,1)} %bitcast.17), channel_id=1, source_target_pairs={{0,64},{16,80},{32,96},{48,112},{64,0},{80,16},{96,32},{112,48},{1... | collective-permute-start | bytes 884744 | tf_op jit(solution)/shard_map/ppermute | solution.py:227
  15.2 1.8 %copy-start = (bf16[1152,1152]{1,0:T(8,128)(2,1)S(1)}, bf16[1152,1152]{1,0:T(8,128)(2,1)}, u32[]{:S(2)}) copy-start(bf16[1152,1152]{1,0:T(8,128)(2,1)} %head_hbm.1) | copy-start | bytes 7962628
  16.9 1.0 copy-start.6
  17.9 1.0 copy-start.10
  18.9 21.7 %copy-start.1 = (bf16[1152,1152]{1,0:T(8,128)(2,1)S(1)}, bf16[1152,1152]{1,0:T(8,128)(2,1)}, u32[]{:S(2)}) copy-start(bf16[1152,1152]{1,0:T(8,128)(2,1)} %head_hbm.1) | copy-start | bytes 7962628
  18.9 34.9 %copy-start.17 = (s32[1,128]{1,0:T(1,128)S(1)}, s32[1,128]{1,0:T(1,128)}, u32[]{:S(2)}) copy-start(s32[1,128]{1,0:T(1,128)} %lab_ref.5) | copy-start | bytes 1540
  19.6 28.4 %copy-start.8 = (f32[128,1152]{1,0:T(8,128)}, f32[128,1152]{1,0:T(8,128)S(1)}, u32[]{:S(2)}) copy-start(f32[128,1152]{1,0:T(8,128)S(1)} %get-tuple-element.20.unit_hbm) | copy-start | bytes 1769476
  19.6 32.9 %copy-start.15 = (f32[128,1]{1,0:T(8,128)}, f32[128,1]{1,0:T(8,128)S(1)}, u32[]{:S(2)}) copy-start(f32[128,1]{1,0:T(8,128)S(1)} %get-tuple-element.19.inv_hbm) | copy-start | bytes 1540
  19.6 38.3 %copy-start.2 = (bf16[128,1152]{1,0:T(8,128)(2,1)}, bf16[128,1152]{1,0:T(8,128)(2,1)S(1)}, u32[]{:S(2)}) copy-start(bf16[128,1152]{1,0:T(8,128)(2,1)S(1)} %get-tuple-element.12.y_ref) | copy-start | bytes 884740
  19.6 41.8 %copy-start.4 = (bf16[128,1152]{1,0:T(8,128)(2,1)}, bf16[128,1152]{1,0:T(8,128)(2,1)S(1)}, u32[]{:S(2)}) copy-start(bf16[128,1152]{1,0:T(8,128)(2,1)S(1)} %get-tuple-element.17.x_ref) | copy-start | bytes 884740
  19.6 25.5 %collective-permute-start = (bf16[128,1152]{1,0:T(8,128)(2,1)S(1)}, bf16[128,1152]{1,0:T(8,128)(2,1)S(1)}, u32[]{:S(2)}, u32[]{:S(2)}) collective-permute-start(bf16[128,1152]{1,0:T(8,128)(2,1)S(1)} %get-tuple-element.12.y_ref), channel_id=1, source_target_pairs={{0,16},{16,32},{32,48},{48,0},{64,80},{80,96},{96,112},{112,64},{1... | collective-permute-start | bytes 884744 | tf_op jit(solution)/shard_map/ppermute | solution.py:212
  22.9 25.1 %collective-permute-start.1 = (bf16[128,1152]{1,0:T(8,128)(2,1)S(1)}, bf16[128,1152]{1,0:T(8,128)(2,1)S(1)}, u32[]{:S(2)}, u32[]{:S(2)}) collective-permute-start(bf16[128,1152]{1,0:T(8,128)(2,1)S(1)} %get-tuple-element.12.y_ref), channel_id=1, source_target_pairs={{0,48},{16,0},{32,16},{48,32},{64,112},{80,64},{96,80},{112,96},{1... | collective-permute-start | bytes 884744 | tf_op jit(solution)/shard_map/ppermute | solution.py:212
  25.1 29.1 %collective-permute-start.2 = (bf16[128,1152]{1,0:T(8,128)(2,1)S(1)}, bf16[128,1152]{1,0:T(8,128)(2,1)}, u32[]{:S(2)}, u32[]{:S(2)}) collective-permute-start(bf16[128,1152]{1,0:T(8,128)(2,1)S(1)} %get-tuple-element.12.y_ref), channel_id=1, source_target_pairs={{0,32},{16,48},{32,0},{48,16},{64,96},{80,112},{96,64},{112,80},{1... | collective-permute-start | bytes 884744 | tf_op jit(solution)/shard_map/ppermute | solution.py:212
  28.8 32.6 %copy-start.7 = (bf16[1,128,1152]{2,1,0:T(8,128)(2,1)S(1)}, bf16[1,128,1152]{2,1,0:T(8,128)(2,1)}, u32[]{:S(2)}) copy-start(bf16[1,128,1152]{2,1,0:T(8,128)(2,1)} %param.6) | copy-start | bytes 884740
  28.8 29.1 %collective-permute-start.3 = (bf16[128,1152]{1,0:T(8,128)(2,1)S(1)}, bf16[128,1152]{1,0:T(8,128)(2,1)}, u32[]{:S(2)}, u32[]{:S(2)}) collective-permute-start(bf16[128,1152]{1,0:T(8,128)(2,1)S(1)} %get-tuple-element.17.x_ref), channel_id=1, source_target_pairs={{0,64},{16,80},{32,96},{48,112},{64,0},{80,16},{96,32},{112,48},{1... | collective-permute-start | bytes 884744 | tf_op jit(solution)/shard_map/ppermute | solution.py:232
  42.0 16.0 %collective-permute-start.5 = (bf16[128,1152]{1,0:T(8,128)(2,1)}, bf16[128,1152]{1,0:T(8,128)(2,1)}, u32[]{:S(2)}, u32[]{:S(2)}) collective-permute-start(bf16[128,1152]{1,0:T(8,128)(2,1)} %shard_map.79.a_ref), channel_id=1, source_target_pairs={{0,16},{16,32},{32,48},{48,0},{64,80},{80,96},{96,112},{112,64},{1... | collective-permute-start | bytes 884744 | tf_op jit(solution)/shard_map/ppermute | solution.py:212
  45.8 12.2 %collective-permute-start.6 = (bf16[128,1152]{1,0:T(8,128)(2,1)}, bf16[128,1152]{1,0:T(8,128)(2,1)}, u32[]{:S(2)}, u32[]{:S(2)}) collective-permute-start(bf16[128,1152]{1,0:T(8,128)(2,1)} %shard_map.79.a_ref), channel_id=1, source_target_pairs={{0,48},{16,0},{32,16},{48,32},{64,112},{80,64},{96,80},{112,96},{1... | collective-permute-start | bytes 884744 | tf_op jit(solution)/shard_map/ppermute | solution.py:212
  48.0 0.7 copy-start.13
  48.7 12.7 %collective-permute-start.7 = (bf16[128,1152]{1,0:T(8,128)(2,1)}, bf16[128,1152]{1,0:T(8,128)(2,1)}, u32[]{:S(2)}, u32[]{:S(2)}) collective-permute-start(bf16[128,1152]{1,0:T(8,128)(2,1)} %shard_map.79.a_ref), channel_id=1, source_target_pairs={{0,32},{16,48},{32,0},{48,16},{64,96},{80,112},{96,64},{112,80},{1... | collective-permute-start | bytes 884744 | tf_op jit(solution)/shard_map/ppermute | solution.py:212
  54.2 1.0 copy-start.12
  55.1 1.0 copy-start.14
  64.9 49.6 %copy-start.16 = (f32[128,1]{1,0:T(8,128)S(1)}, f32[128,1]{1,0:T(8,128)}, u32[]{:S(2)}) copy-start(f32[128,1]{1,0:T(8,128)} %copy-done.15) | copy-start | bytes 1540
  64.9 54.9 %all-to-all-start = ((bf16[16,184,128]{2,1,0:T(8,128)(2,1)}), bf16[16,184,128]{2,1,0:T(8,128)(2,1)S(1)}, u32[]{:S(2)}, u32[]{:S(2)}) async-start(bf16[16,184,128]{2,1,0:T(8,128)(2,1)} %shard_map.81), calls=%async_computation | async-start | bytes 1507328 | tf_op jit(solution)/shard_map/all_to_all | solution.py:242
  83.7 13.7 %collective-permute-start.10 = (bf16[128,1152]{1,0:T(8,128)(2,1)}, bf16[128,1152]{1,0:T(8,128)(2,1)S(1)}, u32[]{:S(2)}, u32[]{:S(2)}) collective-permute-start(bf16[128,1152]{1,0:T(8,128)(2,1)} %copy-done.4), channel_id=1, source_target_pairs={{0,32},{16,48},{32,0},{48,16},{64,96},{80,112},{96,64},{112,80},{1... | collective-permute-start | bytes 884744 | tf_op jit(solution)/shard_map/ppermute | solution.py:212
  86.8 14.3 %collective-permute-start.8 = (bf16[128,1152]{1,0:T(8,128)(2,1)}, bf16[128,1152]{1,0:T(8,128)(2,1)S(1)}, u32[]{:S(2)}, u32[]{:S(2)}) collective-permute-start(bf16[128,1152]{1,0:T(8,128)(2,1)} %copy-done.4), channel_id=1, source_target_pairs={{0,16},{16,32},{32,48},{48,0},{64,80},{80,96},{96,112},{112,64},{1... | collective-permute-start | bytes 884744 | tf_op jit(solution)/shard_map/ppermute | solution.py:212
  88.8 13.8 %collective-permute-start.9 = (bf16[128,1152]{1,0:T(8,128)(2,1)}, bf16[128,1152]{1,0:T(8,128)(2,1)S(1)}, u32[]{:S(2)}, u32[]{:S(2)}) collective-permute-start(bf16[128,1152]{1,0:T(8,128)(2,1)} %copy-done.4), channel_id=1, source_target_pairs={{0,48},{16,0},{32,16},{48,32},{64,112},{80,64},{96,80},{112,96},{1... | collective-permute-start | bytes 884744 | tf_op jit(solution)/shard_map/ppermute | solution.py:212
  92.1 14.4 %collective-permute-start.11 = (bf16[128,1152]{1,0:T(8,128)(2,1)}, bf16[128,1152]{1,0:T(8,128)(2,1)S(1)}, u32[]{:S(2)}, u32[]{:S(2)}) collective-permute-start(bf16[128,1152]{1,0:T(8,128)(2,1)} %collective-permute-done.3.d_ref), channel_id=1, source_target_pairs={{0,16},{16,32},{32,48},{48,0},{64,80},{80,96},{96,112},{112,64},{1... | collective-permute-start | bytes 884744 | tf_op jit(solution)/shard_map/ppermute | solution.py:212
  94.6 14.9 %collective-permute-start.12 = (bf16[128,1152]{1,0:T(8,128)(2,1)}, bf16[128,1152]{1,0:T(8,128)(2,1)S(1)}, u32[]{:S(2)}, u32[]{:S(2)}) collective-permute-start(bf16[128,1152]{1,0:T(8,128)(2,1)} %collective-permute-done.3.d_ref), channel_id=1, source_target_pairs={{0,48},{16,0},{32,16},{48,32},{64,112},{80,64},{96,80},{112,96},{1... | collective-permute-start | bytes 884744 | tf_op jit(solution)/shard_map/ppermute | solution.py:212
  97.5 17.0 %collective-permute-start.13 = (bf16[128,1152]{1,0:T(8,128)(2,1)}, bf16[128,1152]{1,0:T(8,128)(2,1)S(1)}, u32[]{:S(2)}, u32[]{:S(2)}) collective-permute-start(bf16[128,1152]{1,0:T(8,128)(2,1)} %collective-permute-done.3.d_ref), channel_id=1, source_target_pairs={{0,32},{16,48},{32,0},{48,16},{64,96},{80,112},{96,64},{112,80},{1... | collective-permute-start | bytes 884744 | tf_op jit(solution)/shard_map/ppermute | solution.py:212
  102.6 1.0 copy-start.3
  103.5 1.0 copy-start.5
  104.5 10.0 %copy-start.9 = (f32[128,1152]{1,0:T(8,128)S(1)}, f32[128,1152]{1,0:T(8,128)}, u32[]{:S(2)}) copy-start(f32[128,1152]{1,0:T(8,128)} %copy-done.8) | copy-start | bytes 1769476
  (1 other events, 0.7 us)

commit v5 on v4

--- a/solution.py
+++ b/solution.py
@@ -11,6 +11,8 @@
 LANES = 128
 MAIN = 16
 EXTRA = 4
+NEAR_COST = 28_825_000_000
+TAIL_COST = 23_060_000_000
 F32 = jnp.float32
 BF16 = jnp.bfloat16
 
@@ -19,7 +21,7 @@
 TN = ((0,), (0,))
 
 
-def call(kernel, outs, *operands, scalars=0, away=0, scratch=()):
+def call(kernel, outs, *operands, scalars=0, away=0, scratch=(), flops=0):
     smem = pl.BlockSpec(memory_space=pltpu.SMEM)
     vmem = pl.BlockSpec(memory_space=pltpu.VMEM)
     return pl.pallas_call(
@@ -30,6 +32,7 @@
         + [pl.BlockSpec(memory_space=pl.ANY)] * away,
         scratch_shapes=scratch,
         compiler_params=pltpu.CompilerParams(vmem_limit_bytes=48 * 2**20),
+        cost_estimate=pl.CostEstimate(flops=flops, bytes_accessed=flops // 300, transcendentals=0) if flops else None,
     )(*operands)
 
 
@@ -228,23 +231,24 @@
     x, y, unit_y, inv_y = call(
         embed_kernel, (block, block, wide, jax.ShapeDtypeStruct((rows, 1), F32)), image, feat, text_head
     )
-    part = call(near_image_kernel, wide, *scalars, lab, x, y, *ring(y), scalars=2)
+    part = call(near_image_kernel, wide, *scalars, lab, x, y, *ring(y), scalars=2, flops=NEAR_COST)
     far_x = lax.ppermute(x, "loop", across)
     far_y = call(text_kernel, block, far_feat, text_head)
     far_ys = ring(far_y)
-    part, far_x = lax.optimization_barrier((part, far_x))
     sent = call(
         far_image_kernel,
         jax.ShapeDtypeStruct((owners, (MAIN + EXTRA) * width // LANES + EXTRA, LANES), BF16),
         *scalars, image, x, part, far_y, *far_ys, picks, tags, scalars=2,
     )
     sent, x_near = lax.optimization_barrier((sent, x))
+    x_near, far_x = lax.optimization_barrier((x_near, far_x))
     arrived = lax.all_to_all(sent, "dp", split_axis=0, concat_axis=0, tiled=True)
     part_txt = call(near_text_kernel, wide, *scalars, lab, x, y, *ring(x_near), far_x, scalars=2)
     d_text_feat = call(
         text_grad_kernel, wide, *scalars, y, part_txt, *ring(far_x), inv_y, unit_y, text_head,
         scalars=2,
         away=3,
+        flops=TAIL_COST,
         scratch=[
             pltpu.VMEM((rows, 1), F32),
             pltpu.VMEM((rows, width), F32),

time: 122 us -> 116 us (0.951)
  the two profiles are of different devices: /device:TPU:35 before, /device:TPU:1 now
where the time goes in v5:
time: 116 us; the launch traced here: 114 us
  starting transfers between devices  77.5 us (67%)
  Pallas kernels  14.2 us (12%)
  waiting for transfers between devices  13.8 us (12%)
  local copies, waits for them, and re-layouts  6.52 us (6%)
  between operations  2.2 us (2%)
    ppermute x12, starting transfers between devices, ring(): return [lax.ppermute(value, 'loop', turn) for turn in turns]  37.9 us
    all_to_all x1, starting transfers between devices, shards(): lax.all_to_all(sent, 'dp', split_axis=0, concat_axis=0, tiled=True)  21.4 us
    ppermute x1, starting transfers between devices, shards(): far_feat = lax.ppermute(feat, 'loop', across)  16.3 us
    pallas_call x8, Pallas kernels, call(): pl.pallas_call(kernel, out_shape=outs, in_specs=[smem] * scalars + [vmem]...  14.2 us
    ppermute x12, waiting for transfers between devices, ring(): return [lax.ppermute(value, 'loop', turn) for turn in turns]  13.8 us
    unnamed x20, local copies, waits for them, and re-layouts  6.52 us
  transfers between devices with their start and end apart: 15, of which 6 were waited for; matrix products, arithmetic and copies ran while one was open for 0% of the time, Pallas kernels for 12%

profile of v5, /device:TPU:1, one launch (start us, length us, event | category | flops | bytes accessed | tf_op | source)
XLA Modules:
  0.0 114.2 jit_solution(18372298113409377780)
XLA Ops:
  0.6 16.3 %collective-permute-start.3 = (bf16[128,1152]{1,0:T(8,128)(2,1)}, bf16[128,1152]{1,0:T(8,128)(2,1)S(1)}, u32[]{:S(2)}, u32[]{:S(2)}) collective-permute-start(bf16[128,1152]{1,0:T(8,128)(2,1)} %bitcast.17), channel_id=1, source_target_pairs={{0,64},{16,80},{32,96},{48,112},{64,0},{80,16},{96,32},{112,48},{1... | collective-permute-start | bytes 884744 | tf_op jit(solution)/shard_map/ppermute | solution.py:230
  16.9 1.7 %copy-done = bf16[1152,1152]{1,0:T(8,128)(2,1)S(1)} copy-done((bf16[1152,1152]{1,0:T(8,128)(2,1)S(1)}, bf16[1152,1152]{1,0:T(8,128)(2,1)}, u32[]{:S(2)}) %copy-start) | copy-done | bytes 2654232
  18.7 1.0 copy-done.2
  19.6 1.0 copy-done.4
  20.6 1.4 %shard_map.77 = (bf16[128,1152]{1,0:T(8,128)(2,1)}, bf16[128,1152]{1,0:T(8,128)(2,1)S(1)}, f32[128,1152]{1,0:T(8,128)S(1)}, f32[128,1]{1,0:T(8,128)S(1)}) custom-call(bf16[128,1152]{1,0:T(8,128)(2,1)S(1)} %bitcast.15, bf16[128,1152]{1,0:T(8,128)(2,1)S(1)} %bitcast.18, bf16[1152,1152]{1,0:T(8,128)(2,1)S(1)} %copy-done), custom_call_target="tpu_custom_call" | custom-call | tf_op jit(solution)/shard_map/pallas_call | solution.py:27
  22.0 0.8 copy-done.8
  22.8 3.1 %collective-permute-start = (bf16[128,1152]{1,0:T(8,128)(2,1)S(1)}, bf16[128,1152]{1,0:T(8,128)(2,1)}, u32[]{:S(2)}, u32[]{:S(2)}) collective-permute-start(bf16[128,1152]{1,0:T(8,128)(2,1)S(1)} %get-tuple-element.12.y_ref), channel_id=1, source_target_pairs={{0,16},{16,32},{32,48},{48,0},{64,80},{80,96},{96,112},{112,64},{1... | collective-permute-start | bytes 884744 | tf_op jit(solution)/shard_map/ppermute | solution.py:215
  25.9 3.4 %collective-permute-start.1 = (bf16[128,1152]{1,0:T(8,128)(2,1)S(1)}, bf16[128,1152]{1,0:T(8,128)(2,1)}, u32[]{:S(2)}, u32[]{:S(2)}) collective-permute-start(bf16[128,1152]{1,0:T(8,128)(2,1)S(1)} %get-tuple-element.12.y_ref), channel_id=1, source_target_pairs={{0,48},{16,0},{32,16},{48,32},{64,112},{80,64},{96,80},{112,96},{1... | collective-permute-start | bytes 884744 | tf_op jit(solution)/shard_map/ppermute | solution.py:215
  29.3 3.4 %collective-permute-start.2 = (bf16[128,1152]{1,0:T(8,128)(2,1)S(1)}, bf16[128,1152]{1,0:T(8,128)(2,1)}, u32[]{:S(2)}, u32[]{:S(2)}) collective-permute-start(bf16[128,1152]{1,0:T(8,128)(2,1)S(1)} %get-tuple-element.12.y_ref), channel_id=1, source_target_pairs={{0,32},{16,48},{32,0},{48,16},{64,96},{80,112},{96,64},{112,80},{1... | collective-permute-start | bytes 884744 | tf_op jit(solution)/shard_map/ppermute | solution.py:215
  32.7 1.9 %collective-permute-start.7 = (bf16[128,1152]{1,0:T(8,128)(2,1)}, bf16[128,1152]{1,0:T(8,128)(2,1)}, u32[]{:S(2)}, u32[]{:S(2)}) collective-permute-start(bf16[128,1152]{1,0:T(8,128)(2,1)} %get-tuple-element.17.x_ref), channel_id=1, source_target_pairs={{0,64},{16,80},{32,96},{48,112},{64,0},{80,16},{96,32},{112,48},{1... | collective-permute-start | bytes 884744 | tf_op jit(solution)/shard_map/ppermute | solution.py:235
  36.4 0.7 shard_map.79.a_ref
  37.1 2.2 %collective-permute-start.4 = (bf16[128,1152]{1,0:T(8,128)(2,1)S(1)}, bf16[128,1152]{1,0:T(8,128)(2,1)S(1)}, u32[]{:S(2)}, u32[]{:S(2)}) collective-permute-start(bf16[128,1152]{1,0:T(8,128)(2,1)S(1)} %shard_map.79.a_ref), channel_id=1, source_target_pairs={{0,16},{16,32},{32,48},{48,0},{64,80},{80,96},{96,112},{112,64},{1... | collective-permute-start | bytes 884744 | tf_op jit(solution)/shard_map/ppermute | solution.py:215
  39.3 4.3 %collective-permute-start.5 = (bf16[128,1152]{1,0:T(8,128)(2,1)S(1)}, bf16[128,1152]{1,0:T(8,128)(2,1)S(1)}, u32[]{:S(2)}, u32[]{:S(2)}) collective-permute-start(bf16[128,1152]{1,0:T(8,128)(2,1)S(1)} %shard_map.79.a_ref), channel_id=1, source_target_pairs={{0,48},{16,0},{32,16},{48,32},{64,112},{80,64},{96,80},{112,96},{1... | collective-permute-start | bytes 884744 | tf_op jit(solution)/shard_map/ppermute | solution.py:215
  43.6 2.1 %collective-permute-start.6 = (bf16[128,1152]{1,0:T(8,128)(2,1)S(1)}, bf16[128,1152]{1,0:T(8,128)(2,1)S(1)}, u32[]{:S(2)}, u32[]{:S(2)}) collective-permute-start(bf16[128,1152]{1,0:T(8,128)(2,1)S(1)} %shard_map.79.a_ref), channel_id=1, source_target_pairs={{0,32},{16,48},{32,0},{48,16},{64,96},{80,112},{96,64},{112,80},{1... | collective-permute-start | bytes 884744 | tf_op jit(solution)/shard_map/ppermute | solution.py:215
  45.8 2.2 %shard_map.78.part_ref = f32[128,1152]{1,0:T(8,128)S(1)} custom-call(f32[1]{0:T(128)} %bitcast.7.scale_ref, f32[1]{0:T(128)} %bitcast.11.shift_ref, s32[1,128]{1,0:T(1,128)S(1)} %copy-done.7, bf16[128,1152]{1,0:T(8,128)(2,1)} %get-tuple-element.17.x_ref, bf16[128,1152]{1,0:T(8,128)(2,1)S(1)} %get-tuple-element.12.y_ref, ...), custom_call_target="tpu_custom_call" | custom-call | flops 28824999936 | bytes 96083336 | tf_op jit(solution)/shard_map/pallas_call | solution.py:27
  48.0 1.5 %collective-permute-done.5.c_ref = bf16[128,1152]{1,0:T(8,128)(2,1)S(1)} collective-permute-done((bf16[128,1152]{1,0:T(8,128)(2,1)S(1)}, bf16[128,1152]{1,0:T(8,128)(2,1)S(1)}, u32[]{:S(2)}, u32[]{:S(2)}) %collective-permute-start.5) | collective-permute-done | bytes 294944 | tf_op jit(solution)/shard_map/ppermute | solution.py:215
  49.4 3.6 %collective-permute-done.6.d_ref = bf16[128,1152]{1,0:T(8,128)(2,1)S(1)} collective-permute-done((bf16[128,1152]{1,0:T(8,128)(2,1)S(1)}, bf16[128,1152]{1,0:T(8,128)(2,1)S(1)}, u32[]{:S(2)}, u32[]{:S(2)}) %collective-permute-start.6) | collective-permute-done | bytes 294944 | tf_op jit(solution)/shard_map/ppermute | solution.py:215
  53.0 3.2 %shard_map.81 = bf16[16,184,128]{2,1,0:T(8,128)(2,1)} custom-call(f32[1]{0:T(128)} %bitcast.8.scale_ref, f32[1]{0:T(128)} %bitcast.12.shift_ref, bf16[128,1152]{1,0:T(8,128)(2,1)S(1)} %bitcast.16, bf16[128,1152]{1,0:T(8,128)(2,1)} %get-tuple-element.17.x_ref, f32[128,1152]{1,0:T(8,128)S(1)} %shard_map.78.part_ref, bf16[128,1152]{1,0:T(8,128)(2,1)S(1)} %shard_map.79.a_ref, ...), custom_call_target="tpu_custom_call" | custom-call | tf_op jit(solution)/shard_map/pallas_call | solution.py:27
  56.2 21.4 %all-to-all-start = ((bf16[16,184,128]{2,1,0:T(8,128)(2,1)}), bf16[16,184,128]{2,1,0:T(8,128)(2,1)S(1)}, u32[]{:S(2)}, u32[]{:S(2)}) async-start(bf16[16,184,128]{2,1,0:T(8,128)(2,1)} %shard_map.81), calls=%async_computation | async-start | bytes 1507328 | tf_op jit(solution)/shard_map/all_to_all | solution.py:245
  77.7 2.4 %collective-permute-start.10 = (bf16[128,1152]{1,0:T(8,128)(2,1)}, bf16[128,1152]{1,0:T(8,128)(2,1)S(1)}, u32[]{:S(2)}, u32[]{:S(2)}) collective-permute-start(bf16[128,1152]{1,0:T(8,128)(2,1)} %get-tuple-element.17.x_ref), channel_id=1, source_target_pairs={{0,32},{16,48},{32,0},{48,16},{64,96},{80,112},{96,64},{112,80},{1... | collective-permute-start | bytes 884744 | tf_op jit(solution)/shard_map/ppermute | solution.py:215
  80.1 5.4 %collective-permute-start.8 = (bf16[128,1152]{1,0:T(8,128)(2,1)}, bf16[128,1152]{1,0:T(8,128)(2,1)S(1)}, u32[]{:S(2)}, u32[]{:S(2)}) collective-permute-start(bf16[128,1152]{1,0:T(8,128)(2,1)} %get-tuple-element.17.x_ref), channel_id=1, source_target_pairs={{0,16},{16,32},{32,48},{48,0},{64,80},{80,96},{96,112},{112,64},{1... | collective-permute-start | bytes 884744 | tf_op jit(solution)/shard_map/ppermute | solution.py:215
  85.5 3.1 %collective-permute-start.9 = (bf16[128,1152]{1,0:T(8,128)(2,1)}, bf16[128,1152]{1,0:T(8,128)(2,1)S(1)}, u32[]{:S(2)}, u32[]{:S(2)}) collective-permute-start(bf16[128,1152]{1,0:T(8,128)(2,1)} %get-tuple-element.17.x_ref), channel_id=1, source_target_pairs={{0,48},{16,0},{32,16},{48,32},{64,112},{80,64},{96,80},{112,96},{1... | collective-permute-start | bytes 884744 | tf_op jit(solution)/shard_map/ppermute | solution.py:215
  88.6 2.2 %collective-permute-start.11 = (bf16[128,1152]{1,0:T(8,128)(2,1)}, bf16[128,1152]{1,0:T(8,128)(2,1)S(1)}, u32[]{:S(2)}, u32[]{:S(2)}) collective-permute-start(bf16[128,1152]{1,0:T(8,128)(2,1)} %collective-permute-done.7.d_ref), channel_id=1, source_target_pairs={{0,16},{16,32},{32,48},{48,0},{64,80},{80,96},{96,112},{112,64},{1... | collective-permute-start | bytes 884744 | tf_op jit(solution)/shard_map/ppermute | solution.py:215
  90.8 4.3 %collective-permute-start.12 = (bf16[128,1152]{1,0:T(8,128)(2,1)}, bf16[128,1152]{1,0:T(8,128)(2,1)S(1)}, u32[]{:S(2)}, u32[]{:S(2)}) collective-permute-start(bf16[128,1152]{1,0:T(8,128)(2,1)} %collective-permute-done.7.d_ref), channel_id=1, source_target_pairs={{0,48},{16,0},{32,16},{48,32},{64,112},{80,64},{96,80},{112,96},{1... | collective-permute-start | bytes 884744 | tf_op jit(solution)/shard_map/ppermute | solution.py:215
  95.1 1.9 %collective-permute-start.13 = (bf16[128,1152]{1,0:T(8,128)(2,1)}, bf16[128,1152]{1,0:T(8,128)(2,1)S(1)}, u32[]{:S(2)}, u32[]{:S(2)}) collective-permute-start(bf16[128,1152]{1,0:T(8,128)(2,1)} %collective-permute-done.7.d_ref), channel_id=1, source_target_pairs={{0,32},{16,48},{32,0},{48,16},{64,96},{80,112},{96,64},{112,80},{1... | collective-permute-start | bytes 884744 | tf_op jit(solution)/shard_map/ppermute | solution.py:215
  97.2 1.0 copy-done.6
  98.1 2.1 %shard_map.82.part_ref = f32[128,1152]{1,0:T(8,128)S(1)} custom-call(f32[1]{0:T(128)} %bitcast.9.scale_ref, f32[1]{0:T(128)} %bitcast.13.shift_ref, s32[1,128]{1,0:T(1,128)S(1)} %copy-done.7, bf16[128,1152]{1,0:T(8,128)(2,1)} %get-tuple-element.17.x_ref, bf16[128,1152]{1,0:T(8,128)(2,1)S(1)} %copy-done.6, ...), custom_call_target="tpu_custom_call" | custom-call | tf_op jit(solution)/shard_map/pallas_call | solution.py:27
  100.2 3.1 %collective-permute-done.11.a_ref = bf16[128,1152]{1,0:T(8,128)(2,1)S(1)} collective-permute-done((bf16[128,1152]{1,0:T(8,128)(2,1)}, bf16[128,1152]{1,0:T(8,128)(2,1)S(1)}, u32[]{:S(2)}, u32[]{:S(2)}) %collective-permute-start.11) | collective-permute-done | bytes 294944 | tf_op jit(solution)/shard_map/ppermute | solution.py:215
  103.5 5.3 %collective-permute-done.13.c_ref = bf16[128,1152]{1,0:T(8,128)(2,1)S(1)} collective-permute-done((bf16[128,1152]{1,0:T(8,128)(2,1)}, bf16[128,1152]{1,0:T(8,128)(2,1)S(1)}, u32[]{:S(2)}, u32[]{:S(2)}) %collective-permute-start.13) | collective-permute-done | bytes 294944 | tf_op jit(solution)/shard_map/ppermute | solution.py:215
  108.8 1.1 copy-done.9
  109.9 3.2 %shard_map.83 = f32[128,1152]{1,0:T(8,128)} custom-call(f32[1]{0:T(128)} %bitcast.10.scale_ref, f32[1]{0:T(128)} %bitcast.14.shift_ref, bf16[128,1152]{1,0:T(8,128)(2,1)S(1)} %copy-done.6, f32[128,1152]{1,0:T(8,128)S(1)} %shard_map.82.part_ref, bf16[128,1152]{1,0:T(8,128)(2,1)S(1)} %collective-permute-done.11.a_ref, ...), custom_call_target="tpu_custom_call" | custom-call | flops 23060000768 | bytes 76866664 | tf_op jit(solution)/shard_map/pallas_call | solution.py:27
  113.1 1.1 shard_map.84
  (26 shorter events, 0.7 us)
Async XLA Ops:
  0.6 35.3 %copy-start.7 = (s32[1,128]{1,0:T(1,128)S(1)}, s32[1,128]{1,0:T(1,128)}, u32[]{:S(2)}) copy-start(s32[1,128]{1,0:T(1,128)} %lab_ref.5) | copy-start | bytes 1540
  0.6 35.7 %collective-permute-start.3 = (bf16[128,1152]{1,0:T(8,128)(2,1)}, bf16[128,1152]{1,0:T(8,128)(2,1)S(1)}, u32[]{:S(2)}, u32[]{:S(2)}) collective-permute-start(bf16[128,1152]{1,0:T(8,128)(2,1)} %bitcast.17), channel_id=1, source_target_pairs={{0,64},{16,80},{32,96},{48,112},{64,0},{80,16},{96,32},{112,48},{1... | collective-permute-start | bytes 884744 | tf_op jit(solution)/shard_map/ppermute | solution.py:230
  16.9 1.8 %copy-start = (bf16[1152,1152]{1,0:T(8,128)(2,1)S(1)}, bf16[1152,1152]{1,0:T(8,128)(2,1)}, u32[]{:S(2)}) copy-start(bf16[1152,1152]{1,0:T(8,128)(2,1)} %head_hbm.1) | copy-start | bytes 7962628
  18.7 1.0 copy-start.2
  19.6 1.0 copy-start.4
  20.6 15.8 %copy-start.1 = (bf16[1152,1152]{1,0:T(8,128)(2,1)S(1)}, bf16[1152,1152]{1,0:T(8,128)(2,1)}, u32[]{:S(2)}) copy-start(bf16[1152,1152]{1,0:T(8,128)(2,1)} %head_hbm.1) | copy-start | bytes 7962628
  22.0 0.8 copy-start.8
  22.8 25.2 %copy-start.5 = (bf16[128,1152]{1,0:T(8,128)(2,1)}, bf16[128,1152]{1,0:T(8,128)(2,1)S(1)}, u32[]{:S(2)}) copy-start(bf16[128,1152]{1,0:T(8,128)(2,1)S(1)} %get-tuple-element.12.y_ref) | copy-start | bytes 884740
  22.8 16.5 %collective-permute-start = (bf16[128,1152]{1,0:T(8,128)(2,1)S(1)}, bf16[128,1152]{1,0:T(8,128)(2,1)}, u32[]{:S(2)}, u32[]{:S(2)}) collective-permute-start(bf16[128,1152]{1,0:T(8,128)(2,1)S(1)} %get-tuple-element.12.y_ref), channel_id=1, source_target_pairs={{0,16},{16,32},{32,48},{48,0},{64,80},{80,96},{96,112},{112,64},{1... | collective-permute-start | bytes 884744 | tf_op jit(solution)/shard_map/ppermute | solution.py:215
  25.9 17.7 %collective-permute-start.1 = (bf16[128,1152]{1,0:T(8,128)(2,1)S(1)}, bf16[128,1152]{1,0:T(8,128)(2,1)}, u32[]{:S(2)}, u32[]{:S(2)}) collective-permute-start(bf16[128,1152]{1,0:T(8,128)(2,1)S(1)} %get-tuple-element.12.y_ref), channel_id=1, source_target_pairs={{0,48},{16,0},{32,16},{48,32},{64,112},{80,64},{96,80},{112,96},{1... | collective-permute-start | bytes 884744 | tf_op jit(solution)/shard_map/ppermute | solution.py:215
  29.3 16.5 %collective-permute-start.2 = (bf16[128,1152]{1,0:T(8,128)(2,1)S(1)}, bf16[128,1152]{1,0:T(8,128)(2,1)}, u32[]{:S(2)}, u32[]{:S(2)}) collective-permute-start(bf16[128,1152]{1,0:T(8,128)(2,1)S(1)} %get-tuple-element.12.y_ref), channel_id=1, source_target_pairs={{0,32},{16,48},{32,0},{48,16},{64,96},{80,112},{96,64},{112,80},{1... | collective-permute-start | bytes 884744 | tf_op jit(solution)/shard_map/ppermute | solution.py:215
  32.7 44.9 %collective-permute-start.7 = (bf16[128,1152]{1,0:T(8,128)(2,1)}, bf16[128,1152]{1,0:T(8,128)(2,1)}, u32[]{:S(2)}, u32[]{:S(2)}) collective-permute-start(bf16[128,1152]{1,0:T(8,128)(2,1)} %get-tuple-element.17.x_ref), channel_id=1, source_target_pairs={{0,64},{16,80},{32,96},{48,112},{64,0},{80,16},{96,32},{112,48},{1... | collective-permute-start | bytes 884744 | tf_op jit(solution)/shard_map/ppermute | solution.py:235
  37.1 10.9 %collective-permute-start.4 = (bf16[128,1152]{1,0:T(8,128)(2,1)S(1)}, bf16[128,1152]{1,0:T(8,128)(2,1)S(1)}, u32[]{:S(2)}, u32[]{:S(2)}) collective-permute-start(bf16[128,1152]{1,0:T(8,128)(2,1)S(1)} %shard_map.79.a_ref), channel_id=1, source_target_pairs={{0,16},{16,32},{32,48},{48,0},{64,80},{80,96},{96,112},{112,64},{1... | collective-permute-start | bytes 884744 | tf_op jit(solution)/shard_map/ppermute | solution.py:215
  39.3 10.1 %collective-permute-start.5 = (bf16[128,1152]{1,0:T(8,128)(2,1)S(1)}, bf16[128,1152]{1,0:T(8,128)(2,1)S(1)}, u32[]{:S(2)}, u32[]{:S(2)}) collective-permute-start(bf16[128,1152]{1,0:T(8,128)(2,1)S(1)} %shard_map.79.a_ref), channel_id=1, source_target_pairs={{0,48},{16,0},{32,16},{48,32},{64,112},{80,64},{96,80},{112,96},{1... | collective-permute-start | bytes 884744 | tf_op jit(solution)/shard_map/ppermute | solution.py:215
  43.6 9.4 %collective-permute-start.6 = (bf16[128,1152]{1,0:T(8,128)(2,1)S(1)}, bf16[128,1152]{1,0:T(8,128)(2,1)S(1)}, u32[]{:S(2)}, u32[]{:S(2)}) collective-permute-start(bf16[128,1152]{1,0:T(8,128)(2,1)S(1)} %shard_map.79.a_ref), channel_id=1, source_target_pairs={{0,32},{16,48},{32,0},{48,16},{64,96},{80,112},{96,64},{112,80},{1... | collective-permute-start | bytes 884744 | tf_op jit(solution)/shard_map/ppermute | solution.py:215
  45.8 7.2 %copy-start.3 = (bf16[1,128,1152]{2,1,0:T(8,128)(2,1)S(1)}, bf16[1,128,1152]{2,1,0:T(8,128)(2,1)}, u32[]{:S(2)}) copy-start(bf16[1,128,1152]{2,1,0:T(8,128)(2,1)} %param.6) | copy-start | bytes 884740
  56.2 56.9 %all-to-all-start = ((bf16[16,184,128]{2,1,0:T(8,128)(2,1)}), bf16[16,184,128]{2,1,0:T(8,128)(2,1)S(1)}, u32[]{:S(2)}, u32[]{:S(2)}) async-start(bf16[16,184,128]{2,1,0:T(8,128)(2,1)} %shard_map.81), calls=%async_computation | async-start | bytes 1507328 | tf_op jit(solution)/shard_map/all_to_all | solution.py:245
  77.7 17.4 %collective-permute-start.10 = (bf16[128,1152]{1,0:T(8,128)(2,1)}, bf16[128,1152]{1,0:T(8,128)(2,1)S(1)}, u32[]{:S(2)}, u32[]{:S(2)}) collective-permute-start(bf16[128,1152]{1,0:T(8,128)(2,1)} %get-tuple-element.17.x_ref), channel_id=1, source_target_pairs={{0,32},{16,48},{32,0},{48,16},{64,96},{80,112},{96,64},{112,80},{1... | collective-permute-start | bytes 884744 | tf_op jit(solution)/shard_map/ppermute | solution.py:215
  80.1 16.9 %collective-permute-start.8 = (bf16[128,1152]{1,0:T(8,128)(2,1)}, bf16[128,1152]{1,0:T(8,128)(2,1)S(1)}, u32[]{:S(2)}, u32[]{:S(2)}) collective-permute-start(bf16[128,1152]{1,0:T(8,128)(2,1)} %get-tuple-element.17.x_ref), channel_id=1, source_target_pairs={{0,16},{16,32},{32,48},{48,0},{64,80},{80,96},{96,112},{112,64},{1... | collective-permute-start | bytes 884744 | tf_op jit(solution)/shard_map/ppermute | solution.py:215
  85.5 11.7 %collective-permute-start.9 = (bf16[128,1152]{1,0:T(8,128)(2,1)}, bf16[128,1152]{1,0:T(8,128)(2,1)S(1)}, u32[]{:S(2)}, u32[]{:S(2)}) collective-permute-start(bf16[128,1152]{1,0:T(8,128)(2,1)} %get-tuple-element.17.x_ref), channel_id=1, source_target_pairs={{0,48},{16,0},{32,16},{48,32},{64,112},{80,64},{96,80},{112,96},{1... | collective-permute-start | bytes 884744 | tf_op jit(solution)/shard_map/ppermute | solution.py:215
  88.6 14.7 %collective-permute-start.11 = (bf16[128,1152]{1,0:T(8,128)(2,1)}, bf16[128,1152]{1,0:T(8,128)(2,1)S(1)}, u32[]{:S(2)}, u32[]{:S(2)}) collective-permute-start(bf16[128,1152]{1,0:T(8,128)(2,1)} %collective-permute-done.7.d_ref), channel_id=1, source_target_pairs={{0,16},{16,32},{32,48},{48,0},{64,80},{80,96},{96,112},{112,64},{1... | collective-permute-start | bytes 884744 | tf_op jit(solution)/shard_map/ppermute | solution.py:215
  90.8 12.7 %collective-permute-start.12 = (bf16[128,1152]{1,0:T(8,128)(2,1)}, bf16[128,1152]{1,0:T(8,128)(2,1)S(1)}, u32[]{:S(2)}, u32[]{:S(2)}) collective-permute-start(bf16[128,1152]{1,0:T(8,128)(2,1)} %collective-permute-done.7.d_ref), channel_id=1, source_target_pairs={{0,48},{16,0},{32,16},{48,32},{64,112},{80,64},{96,80},{112,96},{1... | collective-permute-start | bytes 884744 | tf_op jit(solution)/shard_map/ppermute | solution.py:215
  95.1 13.7 %collective-permute-start.13 = (bf16[128,1152]{1,0:T(8,128)(2,1)}, bf16[128,1152]{1,0:T(8,128)(2,1)S(1)}, u32[]{:S(2)}, u32[]{:S(2)}) collective-permute-start(bf16[128,1152]{1,0:T(8,128)(2,1)} %collective-permute-done.7.d_ref), channel_id=1, source_target_pairs={{0,32},{16,48},{32,0},{48,16},{64,96},{80,112},{96,64},{112,80},{1... | collective-permute-start | bytes 884744 | tf_op jit(solution)/shard_map/ppermute | solution.py:215
  97.2 1.0 copy-start.6
  108.8 1.1 copy-start.9

commit v6 on v5

--- a/solution.py
+++ b/solution.py
@@ -21,14 +21,15 @@
 TN = ((0,), (0,))
 
 
-def call(kernel, outs, *operands, scalars=0, away=0, scratch=(), flops=0):
+def call(kernel, outs, *operands, scalars=0, away=0, ahead=0, scratch=(), flops=0):
     smem = pl.BlockSpec(memory_space=pltpu.SMEM)
     vmem = pl.BlockSpec(memory_space=pltpu.VMEM)
     return pl.pallas_call(
         kernel,
         out_shape=outs,
         in_specs=[smem] * scalars
-        + [vmem] * (len(operands) - scalars - away)
+        + [pl.BlockSpec(memory_space=pl.ANY)] * ahead
+        + [vmem] * (len(operands) - scalars - away - ahead)
         + [pl.BlockSpec(memory_space=pl.ANY)] * away,
         scratch_shapes=scratch,
         compiler_params=pltpu.CompilerParams(vmem_limit_bytes=48 * 2**20),
@@ -117,22 +118,23 @@
 
 
 def text_grad_kernel(
-    scale_ref, shift_ref, y_ref, part_ref, a_ref, b_ref, c_ref, inv_hbm, unit_hbm, head_hbm, out_ref,
-    inv_ref, unit_ref, head_ref, sems,
+    scale_ref, shift_ref, part_hbm, y_ref, a_ref, b_ref, c_ref, inv_hbm, unit_hbm, head_hbm, out_ref,
+    part_ref, inv_ref, unit_ref, head_ref, sems,
 ):
     scale, shift = scale_ref[0], shift_ref[0]
-    pairs = ((inv_hbm, inv_ref), (unit_hbm, unit_ref), (head_hbm, head_ref))
+    pairs = ((part_hbm, part_ref), (inv_hbm, inv_ref), (unit_hbm, unit_ref), (head_hbm, head_ref))
     copies = [pltpu.make_async_copy(src, dst, sems.at[at]) for at, (src, dst) in enumerate(pairs)]
     for copy in copies:
         copy.start()
     others = jnp.concatenate([a_ref[...], b_ref[...], c_ref[...]], axis=0)
     weight = apart_weights(y_ref[...], others, scale, shift)
-    grad = scale * (part_ref[...] + dot(weight, others, NN))
-    copies[0].wait()
-    copies[1].wait()
+    far = dot(weight, others, NN)
+    for copy in copies[:3]:
+        copy.wait()
+    grad = scale * (part_ref[...] + far)
     unit = unit_ref[...]
     pre = (grad - unit * jnp.sum(unit * grad, axis=-1, keepdims=True)) * inv_ref[...]
-    copies[2].wait()
+    copies[3].wait()
     out_ref[...] = dot(pre.astype(BF16), head_ref[...], NT)
 
 
@@ -245,15 +247,17 @@
     arrived = lax.all_to_all(sent, "dp", split_axis=0, concat_axis=0, tiled=True)
     part_txt = call(near_text_kernel, wide, *scalars, lab, x, y, *ring(x_near), far_x, scalars=2)
     d_text_feat = call(
-        text_grad_kernel, wide, *scalars, y, part_txt, *ring(far_x), inv_y, unit_y, text_head,
+        text_grad_kernel, wide, *scalars, part_txt, y, *ring(far_x), inv_y, unit_y, text_head,
         scalars=2,
         away=3,
+        ahead=1,
         flops=TAIL_COST,
         scratch=[
+            pltpu.VMEM((rows, width), F32),
             pltpu.VMEM((rows, 1), F32),
             pltpu.VMEM((rows, width), F32),
             pltpu.VMEM(text_head.shape, BF16),
-            pltpu.SemaphoreType.DMA((3,)),
+            pltpu.SemaphoreType.DMA((4,)),
         ],
     )
     d_image = call(

time: 116 us -> 116 us (level)
  no operation moved by 1% of the time
where the time goes in v6:
time: 116 us; the launch traced here: 114 us
  starting transfers between devices  77.5 us (67%)
  Pallas kernels  14.4 us (12%)
  waiting for transfers between devices  13.8 us (12%)
  local copies, waits for them, and re-layouts  6.52 us (6%)
  between operations  2.2 us (2%)
    ppermute x12, starting transfers between devices, ring(): return [lax.ppermute(value, 'loop', turn) for turn in turns]  37.9 us
    all_to_all x1, starting transfers between devices, shards(): lax.all_to_all(sent, 'dp', split_axis=0, concat_axis=0, tiled=True)  21.4 us
    ppermute x1, starting transfers between devices, shards(): far_feat = lax.ppermute(feat, 'loop', across)  16.3 us
    pallas_call x8, Pallas kernels, call(): pl.pallas_call(kernel, out_shape=outs, in_specs=[smem] * scalars + [pl.Bl...  14.4 us
    ppermute x12, waiting for transfers between devices, ring(): return [lax.ppermute(value, 'loop', turn) for turn in turns]  13.8 us
    unnamed x20, local copies, waits for them, and re-layouts  6.52 us
  transfers between devices with their start and end apart: 15, of which 6 were waited for; matrix products, arithmetic and copies ran while one was open for 0% of the time, Pallas kernels for 12%

profile of v6, /device:TPU:1, one launch (start us, length us, event | category | flops | bytes accessed | tf_op | source)
XLA Modules:
  0.0 114.4 jit_solution(5505232068994284709)
XLA Ops:
  0.6 16.3 %collective-permute-start.3 = (bf16[128,1152]{1,0:T(8,128)(2,1)}, bf16[128,1152]{1,0:T(8,128)(2,1)S(1)}, u32[]{:S(2)}, u32[]{:S(2)}) collective-permute-start(bf16[128,1152]{1,0:T(8,128)(2,1)} %bitcast.17), channel_id=1, source_target_pairs={{0,64},{16,80},{32,96},{48,112},{64,0},{80,16},{96,32},{112,48},{1... | collective-permute-start | bytes 884744 | tf_op jit(solution)/shard_map/ppermute | solution.py:232
  16.9 1.7 %copy-done = bf16[1152,1152]{1,0:T(8,128)(2,1)S(1)} copy-done((bf16[1152,1152]{1,0:T(8,128)(2,1)S(1)}, bf16[1152,1152]{1,0:T(8,128)(2,1)}, u32[]{:S(2)}) %copy-start) | copy-done | bytes 2654232
  18.7 1.0 copy-done.2
  19.6 1.0 copy-done.4
  20.6 1.4 %shard_map.77 = (bf16[128,1152]{1,0:T(8,128)(2,1)}, bf16[128,1152]{1,0:T(8,128)(2,1)S(1)}, f32[128,1152]{1,0:T(8,128)S(1)}, f32[128,1]{1,0:T(8,128)S(1)}) custom-call(bf16[128,1152]{1,0:T(8,128)(2,1)S(1)} %bitcast.15, bf16[128,1152]{1,0:T(8,128)(2,1)S(1)} %bitcast.18, bf16[1152,1152]{1,0:T(8,128)(2,1)S(1)} %copy-done), custom_call_target="tpu_custom_call" | custom-call | tf_op jit(solution)/shard_map/pallas_call | solution.py:27
  22.0 0.8 copy-done.8
  22.8 3.1 %collective-permute-start = (bf16[128,1152]{1,0:T(8,128)(2,1)S(1)}, bf16[128,1152]{1,0:T(8,128)(2,1)}, u32[]{:S(2)}, u32[]{:S(2)}) collective-permute-start(bf16[128,1152]{1,0:T(8,128)(2,1)S(1)} %get-tuple-element.13.y_ref), channel_id=1, source_target_pairs={{0,16},{16,32},{32,48},{48,0},{64,80},{80,96},{96,112},{112,64},{1... | collective-permute-start | bytes 884744 | tf_op jit(solution)/shard_map/ppermute | solution.py:217
  25.9 3.4 %collective-permute-start.1 = (bf16[128,1152]{1,0:T(8,128)(2,1)S(1)}, bf16[128,1152]{1,0:T(8,128)(2,1)}, u32[]{:S(2)}, u32[]{:S(2)}) collective-permute-start(bf16[128,1152]{1,0:T(8,128)(2,1)S(1)} %get-tuple-element.13.y_ref), channel_id=1, source_target_pairs={{0,48},{16,0},{32,16},{48,32},{64,112},{80,64},{96,80},{112,96},{1... | collective-permute-start | bytes 884744 | tf_op jit(solution)/shard_map/ppermute | solution.py:217
  29.3 3.4 %collective-permute-start.2 = (bf16[128,1152]{1,0:T(8,128)(2,1)S(1)}, bf16[128,1152]{1,0:T(8,128)(2,1)}, u32[]{:S(2)}, u32[]{:S(2)}) collective-permute-start(bf16[128,1152]{1,0:T(8,128)(2,1)S(1)} %get-tuple-element.13.y_ref), channel_id=1, source_target_pairs={{0,32},{16,48},{32,0},{48,16},{64,96},{80,112},{96,64},{112,80},{1... | collective-permute-start | bytes 884744 | tf_op jit(solution)/shard_map/ppermute | solution.py:217
  32.7 1.9 %collective-permute-start.7 = (bf16[128,1152]{1,0:T(8,128)(2,1)}, bf16[128,1152]{1,0:T(8,128)(2,1)}, u32[]{:S(2)}, u32[]{:S(2)}) collective-permute-start(bf16[128,1152]{1,0:T(8,128)(2,1)} %get-tuple-element.17.x_ref), channel_id=1, source_target_pairs={{0,64},{16,80},{32,96},{48,112},{64,0},{80,16},{96,32},{112,48},{1... | collective-permute-start | bytes 884744 | tf_op jit(solution)/shard_map/ppermute | solution.py:237
  36.4 0.7 shard_map.79.a_ref
  37.1 2.2 %collective-permute-start.4 = (bf16[128,1152]{1,0:T(8,128)(2,1)S(1)}, bf16[128,1152]{1,0:T(8,128)(2,1)S(1)}, u32[]{:S(2)}, u32[]{:S(2)}) collective-permute-start(bf16[128,1152]{1,0:T(8,128)(2,1)S(1)} %shard_map.79.a_ref), channel_id=1, source_target_pairs={{0,16},{16,32},{32,48},{48,0},{64,80},{80,96},{96,112},{112,64},{1... | collective-permute-start | bytes 884744 | tf_op jit(solution)/shard_map/ppermute | solution.py:217
  39.3 4.3 %collective-permute-start.5 = (bf16[128,1152]{1,0:T(8,128)(2,1)S(1)}, bf16[128,1152]{1,0:T(8,128)(2,1)S(1)}, u32[]{:S(2)}, u32[]{:S(2)}) collective-permute-start(bf16[128,1152]{1,0:T(8,128)(2,1)S(1)} %shard_map.79.a_ref), channel_id=1, source_target_pairs={{0,48},{16,0},{32,16},{48,32},{64,112},{80,64},{96,80},{112,96},{1... | collective-permute-start | bytes 884744 | tf_op jit(solution)/shard_map/ppermute | solution.py:217
  43.6 2.1 %collective-permute-start.6 = (bf16[128,1152]{1,0:T(8,128)(2,1)S(1)}, bf16[128,1152]{1,0:T(8,128)(2,1)S(1)}, u32[]{:S(2)}, u32[]{:S(2)}) collective-permute-start(bf16[128,1152]{1,0:T(8,128)(2,1)S(1)} %shard_map.79.a_ref), channel_id=1, source_target_pairs={{0,32},{16,48},{32,0},{48,16},{64,96},{80,112},{96,64},{112,80},{1... | collective-permute-start | bytes 884744 | tf_op jit(solution)/shard_map/ppermute | solution.py:217
  45.8 2.2 %shard_map.78.part_ref = f32[128,1152]{1,0:T(8,128)S(1)} custom-call(f32[1]{0:T(128)} %bitcast.7.scale_ref, f32[1]{0:T(128)} %bitcast.11.shift_ref, s32[1,128]{1,0:T(1,128)S(1)} %copy-done.7, bf16[128,1152]{1,0:T(8,128)(2,1)} %get-tuple-element.17.x_ref, bf16[128,1152]{1,0:T(8,128)(2,1)S(1)} %get-tuple-element.13.y_ref, ...), custom_call_target="tpu_custom_call" | custom-call | flops 28824999936 | bytes 96083336 | tf_op jit(solution)/shard_map/pallas_call | solution.py:27
  48.0 1.5 %collective-permute-done.5.c_ref = bf16[128,1152]{1,0:T(8,128)(2,1)S(1)} collective-permute-done((bf16[128,1152]{1,0:T(8,128)(2,1)S(1)}, bf16[128,1152]{1,0:T(8,128)(2,1)S(1)}, u32[]{:S(2)}, u32[]{:S(2)}) %collective-permute-start.5) | collective-permute-done | bytes 294944 | tf_op jit(solution)/shard_map/ppermute | solution.py:217
  49.4 3.6 %collective-permute-done.6.d_ref = bf16[128,1152]{1,0:T(8,128)(2,1)S(1)} collective-permute-done((bf16[128,1152]{1,0:T(8,128)(2,1)S(1)}, bf16[128,1152]{1,0:T(8,128)(2,1)S(1)}, u32[]{:S(2)}, u32[]{:S(2)}) %collective-permute-start.6) | collective-permute-done | bytes 294944 | tf_op jit(solution)/shard_map/ppermute | solution.py:217
  53.0 3.2 %shard_map.81 = bf16[16,184,128]{2,1,0:T(8,128)(2,1)} custom-call(f32[1]{0:T(128)} %bitcast.8.scale_ref, f32[1]{0:T(128)} %bitcast.12.shift_ref, bf16[128,1152]{1,0:T(8,128)(2,1)S(1)} %bitcast.16, bf16[128,1152]{1,0:T(8,128)(2,1)} %get-tuple-element.17.x_ref, f32[128,1152]{1,0:T(8,128)S(1)} %shard_map.78.part_ref, bf16[128,1152]{1,0:T(8,128)(2,1)S(1)} %shard_map.79.a_ref, ...), custom_call_target="tpu_custom_call" | custom-call | tf_op jit(solution)/shard_map/pallas_call | solution.py:27
  56.2 21.4 %all-to-all-start = ((bf16[16,184,128]{2,1,0:T(8,128)(2,1)}), bf16[16,184,128]{2,1,0:T(8,128)(2,1)S(1)}, u32[]{:S(2)}, u32[]{:S(2)}) async-start(bf16[16,184,128]{2,1,0:T(8,128)(2,1)} %shard_map.81), calls=%async_computation | async-start | bytes 1507328 | tf_op jit(solution)/shard_map/all_to_all | solution.py:247
  77.7 2.4 %collective-permute-start.10 = (bf16[128,1152]{1,0:T(8,128)(2,1)}, bf16[128,1152]{1,0:T(8,128)(2,1)S(1)}, u32[]{:S(2)}, u32[]{:S(2)}) collective-permute-start(bf16[128,1152]{1,0:T(8,128)(2,1)} %get-tuple-element.17.x_ref), channel_id=1, source_target_pairs={{0,32},{16,48},{32,0},{48,16},{64,96},{80,112},{96,64},{112,80},{1... | collective-permute-start | bytes 884744 | tf_op jit(solution)/shard_map/ppermute | solution.py:217
  80.1 5.4 %collective-permute-start.8 = (bf16[128,1152]{1,0:T(8,128)(2,1)}, bf16[128,1152]{1,0:T(8,128)(2,1)S(1)}, u32[]{:S(2)}, u32[]{:S(2)}) collective-permute-start(bf16[128,1152]{1,0:T(8,128)(2,1)} %get-tuple-element.17.x_ref), channel_id=1, source_target_pairs={{0,16},{16,32},{32,48},{48,0},{64,80},{80,96},{96,112},{112,64},{1... | collective-permute-start | bytes 884744 | tf_op jit(solution)/shard_map/ppermute | solution.py:217
  85.5 3.1 %collective-permute-start.9 = (bf16[128,1152]{1,0:T(8,128)(2,1)}, bf16[128,1152]{1,0:T(8,128)(2,1)S(1)}, u32[]{:S(2)}, u32[]{:S(2)}) collective-permute-start(bf16[128,1152]{1,0:T(8,128)(2,1)} %get-tuple-element.17.x_ref), channel_id=1, source_target_pairs={{0,48},{16,0},{32,16},{48,32},{64,112},{80,64},{96,80},{112,96},{1... | collective-permute-start | bytes 884744 | tf_op jit(solution)/shard_map/ppermute | solution.py:217
  88.6 2.2 %collective-permute-start.11 = (bf16[128,1152]{1,0:T(8,128)(2,1)}, bf16[128,1152]{1,0:T(8,128)(2,1)S(1)}, u32[]{:S(2)}, u32[]{:S(2)}) collective-permute-start(bf16[128,1152]{1,0:T(8,128)(2,1)} %collective-permute-done.7.d_ref), channel_id=1, source_target_pairs={{0,16},{16,32},{32,48},{48,0},{64,80},{80,96},{96,112},{112,64},{1... | collective-permute-start | bytes 884744 | tf_op jit(solution)/shard_map/ppermute | solution.py:217
  90.8 4.3 %collective-permute-start.12 = (bf16[128,1152]{1,0:T(8,128)(2,1)}, bf16[128,1152]{1,0:T(8,128)(2,1)S(1)}, u32[]{:S(2)}, u32[]{:S(2)}) collective-permute-start(bf16[128,1152]{1,0:T(8,128)(2,1)} %collective-permute-done.7.d_ref), channel_id=1, source_target_pairs={{0,48},{16,0},{32,16},{48,32},{64,112},{80,64},{96,80},{112,96},{1... | collective-permute-start | bytes 884744 | tf_op jit(solution)/shard_map/ppermute | solution.py:217
  95.1 1.9 %collective-permute-start.13 = (bf16[128,1152]{1,0:T(8,128)(2,1)}, bf16[128,1152]{1,0:T(8,128)(2,1)S(1)}, u32[]{:S(2)}, u32[]{:S(2)}) collective-permute-start(bf16[128,1152]{1,0:T(8,128)(2,1)} %collective-permute-done.7.d_ref), channel_id=1, source_target_pairs={{0,32},{16,48},{32,0},{48,16},{64,96},{80,112},{96,64},{112,80},{1... | collective-permute-start | bytes 884744 | tf_op jit(solution)/shard_map/ppermute | solution.py:217
  97.2 1.0 copy-done.6
  98.1 2.1 %shard_map.82.part_hbm = f32[128,1152]{1,0:T(8,128)S(1)} custom-call(f32[1]{0:T(128)} %bitcast.9.scale_ref, f32[1]{0:T(128)} %bitcast.13.shift_ref, s32[1,128]{1,0:T(1,128)S(1)} %copy-done.7, bf16[128,1152]{1,0:T(8,128)(2,1)} %get-tuple-element.17.x_ref, bf16[128,1152]{1,0:T(8,128)(2,1)S(1)} %copy-done.6, ...), custom_call_target="tpu_custom_call" | custom-call | tf_op jit(solution)/shard_map/pallas_call | solution.py:27
  100.2 3.1 %collective-permute-done.11.a_ref = bf16[128,1152]{1,0:T(8,128)(2,1)S(1)} collective-permute-done((bf16[128,1152]{1,0:T(8,128)(2,1)}, bf16[128,1152]{1,0:T(8,128)(2,1)S(1)}, u32[]{:S(2)}, u32[]{:S(2)}) %collective-permute-start.11) | collective-permute-done | bytes 294944 | tf_op jit(solution)/shard_map/ppermute | solution.py:217
  103.5 5.3 %collective-permute-done.13.c_ref = bf16[128,1152]{1,0:T(8,128)(2,1)S(1)} collective-permute-done((bf16[128,1152]{1,0:T(8,128)(2,1)}, bf16[128,1152]{1,0:T(8,128)(2,1)S(1)}, u32[]{:S(2)}, u32[]{:S(2)}) %collective-permute-start.13) | collective-permute-done | bytes 294944 | tf_op jit(solution)/shard_map/ppermute | solution.py:217
  108.8 1.1 copy-done.9
  109.9 3.4 %shard_map.83 = f32[128,1152]{1,0:T(8,128)} custom-call(f32[1]{0:T(128)} %bitcast.10.scale_ref, f32[1]{0:T(128)} %bitcast.14.shift_ref, f32[128,1152]{1,0:T(8,128)S(1)} %shard_map.82.part_hbm, bf16[128,1152]{1,0:T(8,128)(2,1)S(1)} %copy-done.6, bf16[128,1152]{1,0:T(8,128)(2,1)S(1)} %collective-permute-done.11.a_ref, ...), custom_call_target="tpu_custom_call" | custom-call | flops 23060000768 | bytes 76866664 | tf_op jit(solution)/shard_map/pallas_call | solution.py:27
  113.3 1.1 shard_map.84
  (26 shorter events, 0.7 us)
Async XLA Ops:
  0.6 35.3 %copy-start.7 = (s32[1,128]{1,0:T(1,128)S(1)}, s32[1,128]{1,0:T(1,128)}, u32[]{:S(2)}) copy-start(s32[1,128]{1,0:T(1,128)} %lab_ref.5) | copy-start | bytes 1540
  0.6 35.7 %collective-permute-start.3 = (bf16[128,1152]{1,0:T(8,128)(2,1)}, bf16[128,1152]{1,0:T(8,128)(2,1)S(1)}, u32[]{:S(2)}, u32[]{:S(2)}) collective-permute-start(bf16[128,1152]{1,0:T(8,128)(2,1)} %bitcast.17), channel_id=1, source_target_pairs={{0,64},{16,80},{32,96},{48,112},{64,0},{80,16},{96,32},{112,48},{1... | collective-permute-start | bytes 884744 | tf_op jit(solution)/shard_map/ppermute | solution.py:232
  16.9 1.8 %copy-start = (bf16[1152,1152]{1,0:T(8,128)(2,1)S(1)}, bf16[1152,1152]{1,0:T(8,128)(2,1)}, u32[]{:S(2)}) copy-start(bf16[1152,1152]{1,0:T(8,128)(2,1)} %head_hbm.1) | copy-start | bytes 7962628
  18.7 1.0 copy-start.2
  19.6 1.0 copy-start.4
  20.6 15.8 %copy-start.1 = (bf16[1152,1152]{1,0:T(8,128)(2,1)S(1)}, bf16[1152,1152]{1,0:T(8,128)(2,1)}, u32[]{:S(2)}) copy-start(bf16[1152,1152]{1,0:T(8,128)(2,1)} %head_hbm.1) | copy-start | bytes 7962628
  22.0 0.8 copy-start.8
  22.8 25.2 %copy-start.5 = (bf16[128,1152]{1,0:T(8,128)(2,1)}, bf16[128,1152]{1,0:T(8,128)(2,1)S(1)}, u32[]{:S(2)}) copy-start(bf16[128,1152]{1,0:T(8,128)(2,1)S(1)} %get-tuple-element.13.y_ref) | copy-start | bytes 884740
  22.8 16.5 %collective-permute-start = (bf16[128,1152]{1,0:T(8,128)(2,1)S(1)}, bf16[128,1152]{1,0:T(8,128)(2,1)}, u32[]{:S(2)}, u32[]{:S(2)}) collective-permute-start(bf16[128,1152]{1,0:T(8,128)(2,1)S(1)} %get-tuple-element.13.y_ref), channel_id=1, source_target_pairs={{0,16},{16,32},{32,48},{48,0},{64,80},{80,96},{96,112},{112,64},{1... | collective-permute-start | bytes 884744 | tf_op jit(solution)/shard_map/ppermute | solution.py:217
  25.9 17.7 %collective-permute-start.1 = (bf16[128,1152]{1,0:T(8,128)(2,1)S(1)}, bf16[128,1152]{1,0:T(8,128)(2,1)}, u32[]{:S(2)}, u32[]{:S(2)}) collective-permute-start(bf16[128,1152]{1,0:T(8,128)(2,1)S(1)} %get-tuple-element.13.y_ref), channel_id=1, source_target_pairs={{0,48},{16,0},{32,16},{48,32},{64,112},{80,64},{96,80},{112,96},{1... | collective-permute-start | bytes 884744 | tf_op jit(solution)/shard_map/ppermute | solution.py:217
  29.3 16.5 %collective-permute-start.2 = (bf16[128,1152]{1,0:T(8,128)(2,1)S(1)}, bf16[128,1152]{1,0:T(8,128)(2,1)}, u32[]{:S(2)}, u32[]{:S(2)}) collective-permute-start(bf16[128,1152]{1,0:T(8,128)(2,1)S(1)} %get-tuple-element.13.y_ref), channel_id=1, source_target_pairs={{0,32},{16,48},{32,0},{48,16},{64,96},{80,112},{96,64},{112,80},{1... | collective-permute-start | bytes 884744 | tf_op jit(solution)/shard_map/ppermute | solution.py:217
  32.7 44.9 %collective-permute-start.7 = (bf16[128,1152]{1,0:T(8,128)(2,1)}, bf16[128,1152]{1,0:T(8,128)(2,1)}, u32[]{:S(2)}, u32[]{:S(2)}) collective-permute-start(bf16[128,1152]{1,0:T(8,128)(2,1)} %get-tuple-element.17.x_ref), channel_id=1, source_target_pairs={{0,64},{16,80},{32,96},{48,112},{64,0},{80,16},{96,32},{112,48},{1... | collective-permute-start | bytes 884744 | tf_op jit(solution)/shard_map/ppermute | solution.py:237
  37.1 10.9 %collective-permute-start.4 = (bf16[128,1152]{1,0:T(8,128)(2,1)S(1)}, bf16[128,1152]{1,0:T(8,128)(2,1)S(1)}, u32[]{:S(2)}, u32[]{:S(2)}) collective-permute-start(bf16[128,1152]{1,0:T(8,128)(2,1)S(1)} %shard_map.79.a_ref), channel_id=1, source_target_pairs={{0,16},{16,32},{32,48},{48,0},{64,80},{80,96},{96,112},{112,64},{1... | collective-permute-start | bytes 884744 | tf_op jit(solution)/shard_map/ppermute | solution.py:217
  39.3 10.1 %collective-permute-start.5 = (bf16[128,1152]{1,0:T(8,128)(2,1)S(1)}, bf16[128,1152]{1,0:T(8,128)(2,1)S(1)}, u32[]{:S(2)}, u32[]{:S(2)}) collective-permute-start(bf16[128,1152]{1,0:T(8,128)(2,1)S(1)} %shard_map.79.a_ref), channel_id=1, source_target_pairs={{0,48},{16,0},{32,16},{48,32},{64,112},{80,64},{96,80},{112,96},{1... | collective-permute-start | bytes 884744 | tf_op jit(solution)/shard_map/ppermute | solution.py:217
  43.6 9.4 %collective-permute-start.6 = (bf16[128,1152]{1,0:T(8,128)(2,1)S(1)}, bf16[128,1152]{1,0:T(8,128)(2,1)S(1)}, u32[]{:S(2)}, u32[]{:S(2)}) collective-permute-start(bf16[128,1152]{1,0:T(8,128)(2,1)S(1)} %shard_map.79.a_ref), channel_id=1, source_target_pairs={{0,32},{16,48},{32,0},{48,16},{64,96},{80,112},{96,64},{112,80},{1... | collective-permute-start | bytes 884744 | tf_op jit(solution)/shard_map/ppermute | solution.py:217
  45.8 7.2 %copy-start.3 = (bf16[1,128,1152]{2,1,0:T(8,128)(2,1)S(1)}, bf16[1,128,1152]{2,1,0:T(8,128)(2,1)}, u32[]{:S(2)}) copy-start(bf16[1,128,1152]{2,1,0:T(8,128)(2,1)} %param.6) | copy-start | bytes 884740
  56.2 57.1 %all-to-all-start = ((bf16[16,184,128]{2,1,0:T(8,128)(2,1)}), bf16[16,184,128]{2,1,0:T(8,128)(2,1)S(1)}, u32[]{:S(2)}, u32[]{:S(2)}) async-start(bf16[16,184,128]{2,1,0:T(8,128)(2,1)} %shard_map.81), calls=%async_computation | async-start | bytes 1507328 | tf_op jit(solution)/shard_map/all_to_all | solution.py:247
  77.7 17.4 %collective-permute-start.10 = (bf16[128,1152]{1,0:T(8,128)(2,1)}, bf16[128,1152]{1,0:T(8,128)(2,1)S(1)}, u32[]{:S(2)}, u32[]{:S(2)}) collective-permute-start(bf16[128,1152]{1,0:T(8,128)(2,1)} %get-tuple-element.17.x_ref), channel_id=1, source_target_pairs={{0,32},{16,48},{32,0},{48,16},{64,96},{80,112},{96,64},{112,80},{1... | collective-permute-start | bytes 884744 | tf_op jit(solution)/shard_map/ppermute | solution.py:217
  80.1 16.9 %collective-permute-start.8 = (bf16[128,1152]{1,0:T(8,128)(2,1)}, bf16[128,1152]{1,0:T(8,128)(2,1)S(1)}, u32[]{:S(2)}, u32[]{:S(2)}) collective-permute-start(bf16[128,1152]{1,0:T(8,128)(2,1)} %get-tuple-element.17.x_ref), channel_id=1, source_target_pairs={{0,16},{16,32},{32,48},{48,0},{64,80},{80,96},{96,112},{112,64},{1... | collective-permute-start | bytes 884744 | tf_op jit(solution)/shard_map/ppermute | solution.py:217
  85.5 11.7 %collective-permute-start.9 = (bf16[128,1152]{1,0:T(8,128)(2,1)}, bf16[128,1152]{1,0:T(8,128)(2,1)S(1)}, u32[]{:S(2)}, u32[]{:S(2)}) collective-permute-start(bf16[128,1152]{1,0:T(8,128)(2,1)} %get-tuple-element.17.x_ref), channel_id=1, source_target_pairs={{0,48},{16,0},{32,16},{48,32},{64,112},{80,64},{96,80},{112,96},{1... | collective-permute-start | bytes 884744 | tf_op jit(solution)/shard_map/ppermute | solution.py:217
  88.6 14.7 %collective-permute-start.11 = (bf16[128,1152]{1,0:T(8,128)(2,1)}, bf16[128,1152]{1,0:T(8,128)(2,1)S(1)}, u32[]{:S(2)}, u32[]{:S(2)}) collective-permute-start(bf16[128,1152]{1,0:T(8,128)(2,1)} %collective-permute-done.7.d_ref), channel_id=1, source_target_pairs={{0,16},{16,32},{32,48},{48,0},{64,80},{80,96},{96,112},{112,64},{1... | collective-permute-start | bytes 884744 | tf_op jit(solution)/shard_map/ppermute | solution.py:217
  90.8 12.7 %collective-permute-start.12 = (bf16[128,1152]{1,0:T(8,128)(2,1)}, bf16[128,1152]{1,0:T(8,128)(2,1)S(1)}, u32[]{:S(2)}, u32[]{:S(2)}) collective-permute-start(bf16[128,1152]{1,0:T(8,128)(2,1)} %collective-permute-done.7.d_ref), channel_id=1, source_target_pairs={{0,48},{16,0},{32,16},{48,32},{64,112},{80,64},{96,80},{112,96},{1... | collective-permute-start | bytes 884744 | tf_op jit(solution)/shard_map/ppermute | solution.py:217
  95.1 13.7 %collective-permute-start.13 = (bf16[128,1152]{1,0:T(8,128)(2,1)}, bf16[128,1152]{1,0:T(8,128)(2,1)S(1)}, u32[]{:S(2)}, u32[]{:S(2)}) collective-permute-start(bf16[128,1152]{1,0:T(8,128)(2,1)} %collective-permute-done.7.d_ref), channel_id=1, source_target_pairs={{0,32},{16,48},{32,0},{48,16},{64,96},{80,112},{96,64},{112,80},{1... | collective-permute-start | bytes 884744 | tf_op jit(solution)/shard_map/ppermute | solution.py:217
  97.2 1.0 copy-start.6
  108.8 1.1 copy-start.9
